TPU v7x, 512 devices: a whole 4x4x16 slice. The times are simulated.
512 devices in a mesh: section: 32 (over z, core), dp: 16 (over x, y).
Axes of the slice: x: 4, y: 4, z: 16, core: 2. Of those that a mesh axis runs over, the one named last changes fastest.
Arguments:
- hidden: bfloat16 [256, 8192], P('section', 'dp'), may hold values from -64 to 64, as said below
- head_weight: bfloat16 [65536, 8192], P('section', 'dp'), may hold values from -1 to 1
- labels: int32 [256], replicated, may hold values from 0 to 65535
- loss_grad: float32 [256], replicated, may hold values from 3 to 30
Outputs:
- token_loss: float32 [256], P('dp')
- grad_hidden: bfloat16 [256, 8192], P('section', 'dp')
- grad_weight: bfloat16 [65536, 8192], P('section', 'dp')
Inputs may be any that keep to these rules, and one draw needn't show every extreme that they name: `hidden`: hidden states of order one in most rows; some rows may be larger.
All inputs are finite; a program needn't handle non-finite values.
Results may differ from a plain program's by a relative error of at most 0.0048.
Values may be sent and summed in bfloat16 or wider, within the bound.
No kernel may reach another device: no remote copies, remote signals or barrier semaphores. Data moves between devices by JAX's collectives and lax.ppermute only.
A program may use at most 64 MiB of HBM per device.

v0:
```python
import jax
import jax.numpy as jnp
from jax import lax
from jax.sharding import PartitionSpec as P


def local(hidden, head_weight, labels, loss_grad):
    voc_dev = head_weight.shape[0]
    whole = lax.all_gather(hidden, "section", axis=0, tiled=True)
    all_tokens = whole.shape[0]
    share = all_tokens // lax.axis_size("dp")
    my_start = lax.axis_index("dp") * share
    logits = lax.psum_scatter(
        lax.dot_general(
            whole, head_weight, (((1,), (1,)), ((), ())), preferred_element_type=jnp.float32
        ),
        "dp",
        scatter_dimension=0,
        tiled=True,
    )
    row_labels = lax.dynamic_slice_in_dim(labels, my_start, share, 0)
    row_grads = lax.dynamic_slice_in_dim(loss_grad, my_start, share, 0)
    offset = lax.axis_index("section") * voc_dev
    columns = offset + jnp.arange(voc_dev, dtype=jnp.int32)
    onehot = (row_labels[:, None] == columns[None, :]).astype(jnp.float32)
    local_max = jnp.max(logits, axis=1)
    local_target = jnp.sum(logits * onehot, axis=1)
    largest = lax.pmax(local_max, "section")
    local_sum = jnp.sum(jnp.exp(logits - largest[:, None]), axis=1)
    total, target = lax.psum((local_sum, local_target), "section")
    log_total = largest + jnp.log(total)
    row_loss = log_total - target
    dlogits = (row_grads[:, None] * (jnp.exp(logits - log_total[:, None]) - onehot)).astype(
        jnp.bfloat16
    )
    grads_all = lax.all_gather(dlogits, "dp", axis=0, tiled=True)
    grad_weight = lax.dot_general(
        grads_all, whole, (((0,), (0,)), ((), ())), preferred_element_type=jnp.float32
    ).astype(jnp.bfloat16)
    hidden_term = jnp.dot(grads_all, head_weight, preferred_element_type=jnp.float32)
    grad_hidden = lax.psum_scatter(hidden_term, "section", scatter_dimension=0, tiled=True).astype(
        jnp.bfloat16
    )
    return (row_loss, grad_hidden, grad_weight)


def solution(mesh):
    return jax.shard_map(
        local,
        mesh=mesh,
        in_specs=(P("section", "dp"), P("section", "dp"), P(), P()),
        out_specs=(P("dp"), P("section", "dp"), P("section", "dp")),
        check_vma=False,
    )
```

profile of v0, /device:TPU:6, one launch (start us, length us, event | category | flops | bytes accessed | tf_op | source)
XLA Modules:
  0.0 403.5 jit_solution(8363964498841201728)
XLA Ops:
  7.2 0.0 copy-start
  7.2 0.0 reduce-scatter.3.cloned.1.call-start
  7.2 37.3 %all_gather.6 = bf16[256,512]{1,0:T(8,128)(2,1)S(1)} all-gather(bf16[8,512]{1,0:T(8,128)(2,1)} %param.4), channel_id=1, replica_groups=mesh['section'=32,'dp'=16] {'section'}, dimensions={0}, use_global_device_ids=true | all-gather | bytes 270336 | tf_op jit(solution)/shard_map/all_gather | solution.py:9
  44.6 0.0 copy-done
  44.6 2.1 fusion.5
  46.6 0.0 copy-start.2
  46.6 0.0 copy-start.3
  46.6 0.0 reduce-scatter.3.cloned.1.call-update
  46.7 0.0 all-gather.2.cloned.1.call-start
  46.7 0.6 copy-done.2
  47.3 0.1 dynamic_slice.6
  47.4 0.0 copy-done.3
  47.4 0.1 dynamic_slice.7
  47.5 84.6 %reduce-scatter.3.cloned.1.call-done = f32[16,2048]{1,0:T(8,128)} async-done(((f32[256,2048]{1,0:T(8,128)}), f32[16,2048]{1,0:T(8,128)}) %reduce-scatter.3.cloned.1.call-update) | async-done | bytes 131088 | tf_op jit(solution)/shard_map/reduce_scatter | solution.py:13
  132.0 1.0 reduce_max.9
  133.1 47.0 %pmax.7 = f32[16]{0:T(128)S(1)} all-reduce(f32[16]{0:T(128)S(1)} %reduce_max.9), channel_id=1, replica_groups=mesh['section'=32,'dp'=16] {'section'}, use_global_device_ids=true, to_apply=%region_2.0 | all-reduce | flops 16 | bytes 128 | tf_op jit(solution)/shard_map/pmax | solution.py:28
  180.1 1.1 fusion
  181.2 45.8 %all-reduce = (f32[16]{0:T(128)S(1)}, f32[16]{0:T(128)S(1)}) all-reduce(f32[16]{0:T(128)S(1)} %get-tuple-element.4, f32[16]{0:T(128)S(1)} %get-tuple-element.3), channel_id=1, replica_groups=mesh['section'=32,'dp'=16] {'section'}, use_global_device_ids=true, to_apply=%region_4.0 | all-reduce | flops 32 | bytes 256 | tf_op jit(solution)/shard_map/psum | solution.py:30
  227.0 0.5 fusion.4
  227.5 1.6 fusion.3
  229.2 0.0 all-gather.2.cloned.1.call-update
  229.2 0.0 reduce-scatter.5.cloned.1.call-start
  229.2 56.2 %all-gather.2.cloned.1.call-done = bf16[256,2048]{1,0:T(8,128)(2,1)} async-done(((bf16[16,2048]{1,0:T(8,128)(2,1)}), bf16[256,2048]{1,0:T(8,128)(2,1)}) %all-gather.2.cloned.1.call-update) | async-done | bytes 1048592 | tf_op jit(solution)/shard_map/all_gather | solution.py:36
  285.5 0.0 copy-start.1
  285.5 2.8 fusion.6
  288.3 0.0 reduce-scatter.5.cloned.1.call-update
  288.3 0.0 copy-done.1
  288.3 2.1 convolution_convert_fusion
  290.4 105.3 %reduce-scatter.5.cloned.1.call-done = f32[8,512]{1,0:T(8,128)} async-done(((f32[256,512]{1,0:T(8,128)}), f32[8,512]{1,0:T(8,128)}) %reduce-scatter.5.cloned.1.call-update) | async-done | bytes 16400 | tf_op jit(solution)/shard_map/reduce_scatter | solution.py:41
  395.7 1.3 convert_element_type.14
  (1 shorter events, 0.0 us)
Async XLA Ops:
  7.2 37.4 %copy-start = (bf16[2048,512]{1,0:T(8,128)(2,1)S(1)}, bf16[2048,512]{1,0:T(8,128)(2,1)}, u32[]{:S(2)}) copy-start(bf16[2048,512]{1,0:T(8,128)(2,1)} %param.5) | copy-start | bytes 6291460
  7.2 124.9 %reduce-scatter.3.cloned.1.call-start = ((), (), s32[]{:S(2)}) async-start(), calls=%async_computation.2 | async-start | bytes 2228224 | tf_op jit(solution)/shard_map/reduce_scatter | solution.py:13
  46.6 0.7 copy-start.2
  46.6 0.8 copy-start.3
  46.7 238.8 %all-gather.2.cloned.1.call-start = ((), (), s32[]{:S(2)}) async-start(), calls=%async_computation.3 | async-start | bytes 1114112 | tf_op jit(solution)/shard_map/all_gather | solution.py:36
  229.2 166.5 %reduce-scatter.5.cloned.1.call-start = ((), (), s32[]{:S(2)}) async-start(), calls=%async_computation.4 | async-start | bytes 540672 | tf_op jit(solution)/shard_map/reduce_scatter | solution.py:41
  285.5 2.9 copy-start.1
Sparse Core Ops, SparseCore 0:
  46.8 85.2 reduce-scatter.2
  229.3 56.1 all-gather.1
  288.5 107.1 reduce-scatter.4
where the time goes:
time: 404 us
  waiting for transfers between devices  246 us (61%)
  blocking collectives  130 us (32%)
  between operations  13.8 us (3%)
  matrix products  6.96 us (2%)
  other arithmetic  5.63 us (1%)
    reduce_scatter x1, waiting for transfers between devices, local(): lax.psum_scatter(hidden_term, 'section', scatter_dimension=0, tiled=True)  105 us
    reduce_scatter x1, waiting for transfers between devices, local(): lax.psum_scatter(lax.dot_general(whole, head_weight, (((1,), (1,)), ((),...  84.6 us
    all_gather x1, waiting for transfers between devices, local(): grads_all = lax.all_gather(dlogits, 'dp', axis=0, tiled=True)  56.2 us
    pmax x1, blocking collectives, local(): largest = lax.pmax(local_max, 'section')  47 us
    psum x1, blocking collectives, local(): total, target = lax.psum((local_sum, local_target), 'section')  45.8 us
    all_gather x1, blocking collectives, local(): whole = lax.all_gather(hidden, 'section', axis=0, tiled=True)  37.3 us
  transfers between devices with their start and end apart: 3, of which 3 were waited for; matrix products, arithmetic and copies ran while one was open for 1% of the time, Pallas kernels for 0%

commit v1 on v0

v1 whole, which is shorter than its diff:
```python
import jax
import jax.numpy as jnp
from jax import lax
from jax.sharding import PartitionSpec as P

F32 = jnp.float32
BF16 = jnp.bfloat16
LANES = 128


def to_bf16(x):
    return lax.reduce_precision(x, 8, 7)


def split3(x):
    a = to_bf16(x)
    b = to_bf16(x - a)
    c = x - a - b
    return a.astype(BF16), b.astype(BF16), c.astype(BF16)


def join3(a, b, c):
    return (a.astype(F32) + b.astype(F32)) + c.astype(F32)


def code(part, row, owner):
    high = to_bf16(part)
    low = jnp.where(owner, row, part - high)
    return high.astype(BF16), low.astype(BF16)


def decode(high, low, owner):
    high, low = high.astype(F32), low.astype(F32)
    return high + jnp.where(owner, 0.0, low), jnp.where(owner, low, 0.0)


def local(hidden, head_weight, labels, loss_grad):
    voc_dev, feat = head_weight.shape
    mine_n = hidden.shape[0]
    n_dp = lax.axis_size("dp")
    n_sec = lax.axis_size("section")
    n_z = n_sec // 2
    half = n_z * mine_n
    tokens = 2 * half
    share = tokens // n_dp
    section = lax.axis_index("section")
    z, core = section // 2, section % 2
    j = lax.axis_index("dp")
    along_z = [[2 * k + c for k in range(n_z)] for c in range(2)]
    swap = [(i, i ^ 1) for i in range(n_sec)]

    def exchange_z(x):
        return lax.all_to_all(x, "section", 0, 0, tiled=True, axis_index_groups=along_z)

    def exchange_dp(x):
        return lax.all_to_all(x, "dp", 0, 0, tiled=True)

    def own_core_first(x):
        x = x.reshape(n_z, 2, mine_n)
        first = jnp.where(core == 0, x[:, 0], x[:, 1])
        second = jnp.where(core == 0, x[:, 1], x[:, 0])
        return jnp.concatenate([first.reshape(half), second.reshape(half)])

    label = own_core_first(labels)
    grad = own_core_first(loss_grad)
    columns = section * voc_dev + jnp.arange(voc_dev, dtype=jnp.int32)

    mine = exchange_z(jnp.broadcast_to(hidden[None], (n_z, mine_n, feat))).reshape(half, feat)
    whole = jnp.concatenate([mine, lax.ppermute(mine, "section", swap)])

    partial = lax.dot_general(
        whole, head_weight, (((1,), (1,)), ((), ())), preferred_element_type=F32
    )
    logits = jnp.sum(exchange_dp(partial.reshape(n_dp, share, voc_dev)), axis=0)
    share_label = lax.dynamic_slice_in_dim(label, j * share, share, 0)
    hot = share_label[:, None] == columns[None, :]
    top = jnp.max(logits, axis=1)
    expo = jnp.exp(logits - top[:, None])
    total = jnp.sum(expo, axis=1)
    target = jnp.sum(jnp.where(hot, logits, 0.0), axis=1)
    soft = jnp.where(hot, 0.0, expo * (1.0 / total)[:, None]).astype(BF16)
    stats = jnp.stack(split3(top + jnp.log(total)) + split3(target), axis=1)
    stats = jnp.pad(stats, ((0, 0), (0, LANES - 6)))
    message = jnp.concatenate([soft, stats], axis=1)
    got = exchange_dp(jnp.broadcast_to(message[None], (n_dp, share, voc_dev + LANES)))
    got = got.reshape(tokens, voc_dev + LANES)
    soft = got[:, :voc_dev]
    log_sum = join3(got[:, voc_dev], got[:, voc_dev + 1], got[:, voc_dev + 2])
    target = join3(got[:, voc_dev + 3], got[:, voc_dev + 4], got[:, voc_dev + 5])

    hot = label[:, None] == columns[None, :]
    part = jnp.dot(soft, head_weight, preferred_element_type=F32)
    row = jnp.dot(hot.astype(BF16), head_weight, preferred_element_type=F32)
    owner = label // voc_dev == section
    high, low = code(part[half:], row[half:], owner[half:, None])
    high, low = lax.ppermute(jnp.concatenate([high, low], axis=1), "section", swap).reshape(
        half, 2, feat
    ).transpose(1, 0, 2)
    other = lax.ppermute(jnp.stack([log_sum, target]), "section", swap)
    other_log, other_target = jnp.roll(other, half, axis=1)
    other_part, other_row = decode(high, low, (label // voc_dev == section + 1 - 2 * core)[:half, None])
    low_log = jnp.where(core == 0, log_sum, other_log)
    high_log = jnp.where(core == 0, other_log, log_sum)
    top = jnp.maximum(low_log, high_log)
    pair_log = top + jnp.log(jnp.exp(low_log - top) + jnp.exp(high_log - top))
    pair_target = target + other_target
    part = (
        part[:half] * jnp.exp(log_sum - pair_log)[:half, None]
        + other_part * jnp.exp(other_log - pair_log)[:half, None]
    )
    row = row[:half] + other_row
    high, low = code(part, row, (label // (2 * voc_dev) == z)[:half, None])
    rows = 2 * mine_n
    stats = jnp.stack(split3(pair_log) + split3(pair_target)).reshape(-1, LANES)
    stats = jnp.pad(stats, ((0, rows - stats.shape[0]), (0, 0)))
    message = jnp.concatenate(
        [high.reshape(n_z, mine_n, feat), low.reshape(n_z, mine_n, feat)], axis=1
    )
    message = jnp.concatenate(
        [message, jnp.broadcast_to(stats[None], (n_z, rows, LANES))], axis=2
    )
    got = exchange_z(message)
    stats = got[:, :, feat:].reshape(n_z, -1)[:, : 6 * tokens].reshape(n_z, 6, tokens)
    logs = join3(stats[:, 0], stats[:, 1], stats[:, 2])
    target = jnp.sum(join3(stats[:, 3], stats[:, 4], stats[:, 5]), axis=0)
    top = jnp.max(logs, axis=0)
    log_total = top + jnp.log(jnp.sum(jnp.exp(logs - top), axis=0))
    loss = log_total - target
    loss = lax.dynamic_slice_in_dim(loss.reshape(2, half), j * (share // 2), share // 2, 1)
    loss = jnp.where(core == 0, loss, loss[::-1]).reshape(share)
    label_grad = grad * (jnp.exp(target - log_total) - 1.0)

    def my_tokens(x):
        return lax.dynamic_slice_in_dim(x, z * mine_n, mine_n, x.ndim - 1)

    owners = my_tokens(label)[None, :] // (2 * voc_dev) == jnp.arange(n_z)[:, None]
    parts, rows_ = decode(got[:, :mine_n, :feat], got[:, mine_n:, :feat], owners[:, :, None])
    weights = jnp.exp(my_tokens(logs) - my_tokens(log_total)[None])
    grad_hidden = (
        my_tokens(grad)[:, None] * jnp.sum(parts * weights[:, :, None], axis=0)
        + my_tokens(label_grad)[:, None] * jnp.sum(rows_, axis=0)
    ).astype(BF16)

    scale = grad * jnp.exp(log_sum - log_total)
    dlogits = jnp.where(hot, label_grad[:, None], soft.astype(F32) * scale[:, None]).astype(BF16)
    grad_weight = lax.dot_general(
        dlogits, whole, (((0,), (0,)), ((), ())), preferred_element_type=F32
    ).astype(BF16)
    return (loss, grad_hidden, grad_weight)


def solution(mesh):
    return jax.shard_map(
        local,
        mesh=mesh,
        in_specs=(P("section", "dp"), P("section", "dp"), P(), P()),
        out_specs=(P("dp"), P("section", "dp"), P("section", "dp")),
        check_vma=False,
    )
```

time: 404 us -> 154 us (0.38)
  waiting for transfers between devices: 246 us -> 49.4 us
  blocking collectives: 130 us -> 29.7 us
  starting transfers between devices: 0.12 us -> 24.5 us
  local copies, waits for them, and re-layouts: 0.76 us -> 23 us
  between operations: 13.8 us -> 0.97 us
  other arithmetic: 5.63 us -> 17.1 us
    reduce_scatter x2 -> x0, waiting for transfers between devices: 190 us -> none  [the longest x1 105 us: local(): lax.psum_scatter(hidden_term, 'section', scatter_dimension=0, tiled=True)]
    all_gather x1 -> x0, waiting for transfers between devices: 56.2 us -> none  [local(): grads_all = lax.all_gather(dlogits, 'dp', axis=0, tiled=True)]
    pmax x1 -> x0, blocking collectives: 47 us -> none  [local(): largest = lax.pmax(local_max, 'section')]
    all_to_all x0 -> x3, waiting for transfers between devices: none -> 46.9 us  [the longest x2 39.5 us: exchange_dp(): return lax.all_to_all(x, 'dp', 0, 0, tiled=True)]
    psum x1 -> x0, blocking collectives: 45.8 us -> none  [local(): total, target = lax.psum((local_sum, local_target), 'section')]
    all_gather x1 -> x0, blocking collectives: 37.3 us -> none  [local(): whole = lax.all_gather(hidden, 'section', axis=0, tiled=True)]
    all_to_all x0 -> x1, blocking collectives: none -> 29.7 us  [exchange_z(): lax.all_to_all(x, 'section', 0, 0, tiled=True, axis_index_groups=along_z)]
    all_to_all x0 -> x3, starting transfers between devices: none -> 18.3 us  [the longest x2 14.4 us: exchange_dp(): return lax.all_to_all(x, 'dp', 0, 0, tiled=True)]
  transfers between devices with their start and end apart: 3 -> 6, of which waited for: 3 -> 5; matrix products, arithmetic and copies ran while one was open for 1% -> 13% of each run, Pallas kernels for 0% -> 0%
where the time goes in v1:
time: 154 us; the launch traced here: 152 us
  waiting for transfers between devices  49.4 us (32%)
  blocking collectives  29.7 us (19%)
  starting transfers between devices  24.5 us (16%)
  local copies, waits for them, and re-layouts  23 us (15%)
  other arithmetic  17.1 us (11%)
  matrix products  7.56 us (5%)
    all_to_all x2, waiting for transfers between devices, exchange_dp(): return lax.all_to_all(x, 'dp', 0, 0, tiled=True)  39.5 us
    all_to_all x1, blocking collectives, exchange_z(): lax.all_to_all(x, 'section', 0, 0, tiled=True, axis_index_groups=along_z)  29.7 us
    all_to_all x2, starting transfers between devices, exchange_dp(): return lax.all_to_all(x, 'dp', 0, 0, tiled=True)  14.4 us
    all_to_all x1, waiting for transfers between devices, exchange_z(): lax.all_to_all(x, 'section', 0, 0, tiled=True, axis_index_groups=along_z)  7.42 us
    all_to_all x1, starting transfers between devices, exchange_z(): lax.all_to_all(x, 'section', 0, 0, tiled=True, axis_index_groups=along_z)  3.85 us
    dot_general x1, matrix products, local(): lax.dot_general(dlogits, whole, (((0,), (0,)), ((), ())), preferred_eleme...  3.26 us
    select_n x4, local copies, waits for them, and re-layouts, own_core_first(): first = jnp.where(core == 0, x[:, 0], x[:, 1])  3.18 us
  transfers between devices with their start and end apart: 6, of which 5 were waited for; matrix products, arithmetic and copies ran while one was open for 13% of the time, Pallas kernels for 0%

profile of v1, /device:TPU:6, one launch (start us, length us, event | category | flops | bytes accessed | tf_op | source)
XLA Modules:
  0.0 152.2 jit_solution(1875663042007071027)
XLA Ops:
  0.6 0.9 broadcast_in_dim.71
  1.5 29.7 %all_to_all.20 = bf16[16,8,512]{2,1,0:T(8,128)(2,1)S(1)} all-to-all(bf16[16,8,512]{2,1,0:T(8,128)(2,1)S(1)} %broadcast_in_dim.71), channel_id=1, replica_groups={{0,32,64,96,128,160,192,224,256,288,320,352,384,416,448,480},{16,48,80,..., dimensions={0} | all-to-all | bytes 262144 | tf_op jit(solution)/shard_map/all_to_all | solution.py:53
  31.2 1.9 %collective-permute-start = (bf16[128,512]{1,0:T(8,128)(2,1)S(1)}, bf16[128,512]{1,0:T(8,128)(2,1)S(1)}, u32[]{:S(2)}, u32[]{:S(2)}) collective-permute-start(bf16[128,512]{1,0:T(8,128)(2,1)S(1)} %bitcast.85), channel_id=1, source_target_pairs={{0,16},{16,0},{32,48},{48,32},{64,80},{80,64},{96,112},{112,96},{1... | collective-permute-start | bytes 393224 | tf_op jit(solution)/shard_map/ppermute | solution.py:69
  33.1 1.3 collective-permute-done
  34.4 2.1 %fusion.25 = f32[256,2048]{1,0:T(8,128)} fusion(bf16[2048,512]{1,0:T(8,128)(2,1)S(1)} %copy-done, bf16[128,512]{1,0:T(8,128)(2,1)S(1)} %collective-permute-done, bf16[128,512]{1,0:T(8,128)(2,1)S(1)} %bitcast.86), kind=kOutput, calls=%fused_computation.39 | convolution fusion | flops 537395200 | bytes 4456448 | tf_op jit(solution)/shard_map/dot_general | solution.py:71
  36.5 7.6 %all-to-all-start.1 = ((f32[16,16,2048]{2,1,0:T(8,128)}), f32[16,16,2048]{2,1,0:T(8,128)}, u32[]{:S(2)}, u32[]{:S(2)}) async-start(f32[16,16,2048]{2,1,0:T(8,128)} %bitcast.77), calls=%async_computation.1 | async-start | bytes 4194304 | tf_op jit(solution)/shard_map/all_to_all | solution.py:56
  44.6 27.7 %all-to-all-done.1 = f32[16,16,2048]{2,1,0:T(8,128)} async-done(((f32[16,16,2048]{2,1,0:T(8,128)}), f32[16,16,2048]{2,1,0:T(8,128)}, u32[]{:S(2)}, u32[]{:S(2)}) %all-to-all-start.1) | async-done | bytes 2097184 | tf_op jit(solution)/shard_map/all_to_all | solution.py:56
  72.3 1.7 %reduce_sum.65 = f32[16,2048]{1,0:T(8,128)S(1)} reduce(f32[16,16,2048]{2,1,0:T(8,128)} %all-to-all-done.1, f32[]{:T(128)} %constant.79.clone.1), dimensions={0}, to_apply=%region_0.1 | reduce | flops 491520 | bytes 2228228 | tf_op jit(solution)/shard_map/reduce_sum | solution.py:74
  74.6 1.1 broadcast_in_dim.72
  75.7 6.9 %all-to-all-start.2 = ((bf16[16,16,2176]{2,1,0:T(8,128)(2,1)}), bf16[16,16,2176]{2,1,0:T(8,128)(2,1)S(1)}, u32[]{:S(2)}, u32[]{:S(2)}) async-start(bf16[16,16,2176]{2,1,0:T(8,128)(2,1)} %broadcast_in_dim.72), calls=%async_computation.2 | async-start | bytes 2228224 | tf_op jit(solution)/shard_map/all_to_all | solution.py:56
  84.1 1.5 %fusion = f32[256,512]{1,0:T(8,128)} fusion(bf16[2048,512]{1,0:T(8,128)(2,1)S(1)} %copy-done, s32[2048]{0:T(1024)S(1)} %iota_add_fusion, s32[256]{0:T(256)S(1)} %constant_dynamic-update-slice_fusion), kind=kOutput, calls=%fused_computation.2 | convolution fusion | flops 537395200 | bytes 2630656 | tf_op jit(solution)/shard_map/dot_general | solution.py:93
  85.6 11.8 %all-to-all-done.2 = bf16[16,16,2176]{2,1,0:T(8,128)(2,1)S(1)} async-done(((bf16[16,16,2176]{2,1,0:T(8,128)(2,1)}), bf16[16,16,2176]{2,1,0:T(8,128)(2,1)S(1)}, u32[]{:S(2)}, u32[]{:S(2)}) %all-to-all-start.2) | async-done | bytes 1114144 | tf_op jit(solution)/shard_map/all_to_all | solution.py:56
  97.4 0.7 fusion.11
  99.2 1.9 %collective-permute-start.1 = (f32[2,256]{1,0:T(2,128)S(1)}, f32[2,256]{1,0:T(2,128)S(1)}, u32[]{:S(2)}, u32[]{:S(2)}) collective-permute-start(f32[2,256]{1,0:T(2,128)S(1)} %pad_maximum_fusion.5), channel_id=1, source_target_pairs={{0,16},{16,0},{32,48},{48,32},{64,80},{80,64},{96,112},{112,96},{1... | collective-permute-start | bytes 6152 | tf_op jit(solution)/shard_map/ppermute | solution.py:99
  101.2 1.1 fusion.24
  102.3 0.7 pad_maximum_fusion.2
  103.0 2.4 %collective-permute-start.2 = (bf16[128,1024]{1,0:T(8,128)(2,1)}, bf16[128,1024]{1,0:T(8,128)(2,1)S(1)}, u32[]{:S(2)}, u32[]{:S(2)}) collective-permute-start(bf16[128,1024]{1,0:T(8,128)(2,1)} %pad_maximum_fusion.2), channel_id=1, source_target_pairs={{0,16},{16,0},{32,48},{48,32},{64,80},{80,64},{96,112},{112,96},{1... | collective-permute-start | bytes 786440 | tf_op jit(solution)/shard_map/ppermute | solution.py:96
  105.6 1.2 collective-permute-done.2
  106.8 1.2 fusion.30
  108.1 0.8 pad_maximum_fusion
  108.8 3.9 %all-to-all-start.3 = ((bf16[16,16,640]{2,1,0:T(8,128)(2,1)}), bf16[16,16,640]{2,1,0:T(8,128)(2,1)S(1)}, u32[]{:S(2)}, u32[]{:S(2)}) async-start(bf16[16,16,640]{2,1,0:T(8,128)(2,1)} %pad_maximum_fusion), calls=%async_computation.3 | async-start | bytes 655360 | tf_op jit(solution)/shard_map/all_to_all | solution.py:53
  112.7 1.4 reshape.415
  114.6 2.6 %fusion.49 = (f32[16,8]{1,0:T(8,128)}, f32[16,1,8]{2,1,0:T(1,128)S(1)}, f32[16,8]{1,0:T(8,128)}, f32[16,1,8]{2,1,0:T(1,128)}) fusion(f32[]{:T(128)} %broadcast.149, f32[16,2,8]{2,1,0:T(2,128)} %reshape.415, pred[]{:T(512)S(6)} %eq.72), kind=kLoop, calls=%fused_computation.136 | loop fusion | flops 256 | bytes 3077 | tf_op jit(solution)/shard_map/jit(_where)/select_n | solution.py:61
  117.3 1.3 select_n.188
  118.5 1.4 select_n.190
  119.9 1.3 select_n.195
  121.2 0.7 select_n.196
  121.9 1.2 constant_dynamic-update-slice_fusion.3
  123.1 1.2 constant_dynamic-update-slice_fusion.1
  124.3 1.3 dynamic_slice.25
  125.6 0.7 and_select_fusion
  126.3 0.6 iota_compare_fusion.1
  126.9 7.4 %all-to-all-done.3 = bf16[16,16,640]{2,1,0:T(8,128)(2,1)S(1)} async-done(((bf16[16,16,640]{2,1,0:T(8,128)(2,1)}), bf16[16,16,640]{2,1,0:T(8,128)(2,1)S(1)}, u32[]{:S(2)}, u32[]{:S(2)}) %all-to-all-start.3) | async-done | bytes 327712 | tf_op jit(solution)/shard_map/all_to_all | solution.py:53
  134.3 0.6 slice.149
  134.9 1.9 %copy.36 = bf16[16,16,128]{0,2,1:T(8,128)(2,1)} copy(bf16[16,16,128]{2,1,0:T(8,128)(2,1)} %slice.149) | data formatting | bytes 131072 | tf_op jit(solution)/shard_map/reshape | solution.py:123
  136.8 1.0 slice.150
  138.3 0.6 subtract_bitcast_fusion
  138.8 0.6 dynamic_slice.30
  139.5 0.7 fusion.37
  140.2 0.8 copy.35
  140.9 1.3 constant_dynamic-slice_fusion
  142.2 1.3 rev.3
  143.5 1.3 broadcast_select_fusion.6
  144.8 1.3 reshape.414
  146.1 0.7 maximum_multiply_fusion
  146.8 0.8 fusion.15
  147.6 1.3 add_convert_fusion
  148.9 3.3 %convolution_convert_fusion = bf16[2048,512]{1,0:T(8,128)(2,1)} fusion(f32[256]{0:T(256)S(1)} %bitcast.99, f32[256]{0:T(256)} %copy-done.7, s32[2048]{0:T(1024)S(1)} %iota_add_fusion, s32[256]{0:T(256)} %copy-done.9, bf16[256,2176]{1,0:T(8,128)(2,1)S(1)} %bitcast.81, bf16[128,512]{1,0:T(8,128)(2,1)} %copy-done.3, bf16[128,512]{1,0:T(8,128)(2,1)} %bitcast.87), kind=kOutput, calls=%fused_computation | convolution fusion | flops 540540928 | bytes 3419136 | tf_op jit(solution)/shard_map/dot_general | solution.py:146
  (67 shorter events, 4.8 us)
Async XLA Ops:
  0.6 33.8 %copy-start = (bf16[2048,512]{1,0:T(8,128)(2,1)S(1)}, bf16[2048,512]{1,0:T(8,128)(2,1)}, u32[]{:S(2)}) copy-start(bf16[2048,512]{1,0:T(8,128)(2,1)} %param.5) | copy-start | bytes 6291460
  31.2 5.3 %copy-start.2 = (bf16[16,8,512]{2,1,0:T(8,128)(2,1)}, bf16[16,8,512]{2,1,0:T(8,128)(2,1)S(1)}, u32[]{:S(2)}) copy-start(bf16[16,8,512]{2,1,0:T(8,128)(2,1)S(1)} %all_to_all.20) | copy-start | bytes 393220
  31.2 3.2 %collective-permute-start = (bf16[128,512]{1,0:T(8,128)(2,1)S(1)}, bf16[128,512]{1,0:T(8,128)(2,1)S(1)}, u32[]{:S(2)}, u32[]{:S(2)}) collective-permute-start(bf16[128,512]{1,0:T(8,128)(2,1)S(1)} %bitcast.85), channel_id=1, source_target_pairs={{0,16},{16,0},{32,48},{48,32},{64,80},{80,64},{96,112},{112,96},{1... | collective-permute-start | bytes 393224 | tf_op jit(solution)/shard_map/ppermute | solution.py:69
  34.4 2.1 %copy-start.3 = (bf16[128,512]{1,0:T(8,128)(2,1)}, bf16[128,512]{1,0:T(8,128)(2,1)S(1)}, u32[]{:S(2)}) copy-start(bf16[128,512]{1,0:T(8,128)(2,1)S(1)} %collective-permute-done) | copy-start | bytes 393220
  36.5 7.6 %copy-start.6 = (s32[256]{0:T(256)S(1)}, s32[256]{0:T(256)}, u32[]{:S(2)}) copy-start(s32[256]{0:T(256)} %param.6) | copy-start | bytes 3076
  36.5 35.8 %all-to-all-start.1 = ((f32[16,16,2048]{2,1,0:T(8,128)}), f32[16,16,2048]{2,1,0:T(8,128)}, u32[]{:S(2)}, u32[]{:S(2)}) async-start(f32[16,16,2048]{2,1,0:T(8,128)} %bitcast.77), calls=%async_computation.1 | async-start | bytes 4194304 | tf_op jit(solution)/shard_map/all_to_all | solution.py:56
  44.5 39.6 %copy-start.9 = (s32[256]{0:T(256)}, s32[256]{0:T(256)S(1)}, u32[]{:S(2)}) copy-start(s32[256]{0:T(256)S(1)} %constant_dynamic-update-slice_fusion) | copy-start | bytes 3076
  75.7 21.7 %all-to-all-start.2 = ((bf16[16,16,2176]{2,1,0:T(8,128)(2,1)}), bf16[16,16,2176]{2,1,0:T(8,128)(2,1)S(1)}, u32[]{:S(2)}, u32[]{:S(2)}) async-start(bf16[16,16,2176]{2,1,0:T(8,128)(2,1)} %broadcast_in_dim.72), calls=%async_computation.2 | async-start | bytes 2228224 | tf_op jit(solution)/shard_map/all_to_all | solution.py:56
  98.1 0.8 copy-start.1
  99.2 9.6 %copy-start.4 = (f32[256,1]{0,1:T(1,128)}, f32[256,1]{0,1:T(1,128)S(1)}, u32[]{:S(2)}) copy-start(f32[256,1]{0,1:T(1,128)S(1)} %convert_add_fusion.1) | copy-start | bytes 3076
  99.2 6.2 %collective-permute-start.1 = (f32[2,256]{1,0:T(2,128)S(1)}, f32[2,256]{1,0:T(2,128)S(1)}, u32[]{:S(2)}, u32[]{:S(2)}) collective-permute-start(f32[2,256]{1,0:T(2,128)S(1)} %pad_maximum_fusion.5), channel_id=1, source_target_pairs={{0,16},{16,0},{32,48},{48,32},{64,80},{80,64},{96,112},{112,96},{1... | collective-permute-start | bytes 6152 | tf_op jit(solution)/shard_map/ppermute | solution.py:99
  103.0 3.8 %collective-permute-start.2 = (bf16[128,1024]{1,0:T(8,128)(2,1)}, bf16[128,1024]{1,0:T(8,128)(2,1)S(1)}, u32[]{:S(2)}, u32[]{:S(2)}) collective-permute-start(bf16[128,1024]{1,0:T(8,128)(2,1)} %pad_maximum_fusion.2), channel_id=1, source_target_pairs={{0,16},{16,0},{32,48},{48,32},{64,80},{80,64},{96,112},{112,96},{1... | collective-permute-start | bytes 786440 | tf_op jit(solution)/shard_map/ppermute | solution.py:96
  108.8 25.4 %all-to-all-start.3 = ((bf16[16,16,640]{2,1,0:T(8,128)(2,1)}), bf16[16,16,640]{2,1,0:T(8,128)(2,1)S(1)}, u32[]{:S(2)}, u32[]{:S(2)}) async-start(bf16[16,16,640]{2,1,0:T(8,128)(2,1)} %pad_maximum_fusion), calls=%async_computation.3 | async-start | bytes 655360 | tf_op jit(solution)/shard_map/all_to_all | solution.py:53
  124.3 13.8 %copy-start.8 = (f32[256]{0:T(256)S(1)}, f32[256]{0:T(256)}, u32[]{:S(2)}) copy-start(f32[256]{0:T(256)} %constant_dynamic-update-slice_fusion.1) | copy-start | bytes 3076
  138.2 1.3 copy-start.5
  138.2 1.3 copy-start.7

commit v2 on v0

v2 whole, which is shorter than its diff:
```python
import functools

import jax
import jax.numpy as jnp
from jax import lax
from jax.experimental import pallas as pl
from jax.experimental.pallas import tpu as pltpu
from jax.sharding import PartitionSpec as P

F32 = jnp.float32
BF16 = jnp.bfloat16
I16 = jnp.int16
I32 = jnp.int32
LANES = 128
CHUNK = 256
STEPS = 32760.0
GRAIN = 64.0
MIB = 1 << 20

SCALARS = pl.BlockSpec(memory_space=pltpu.SMEM)
WHOLE = pl.BlockSpec(memory_space=pltpu.VMEM)


def call(kernel, scalars, args, outs, scratch=(), limit=24, flops=0):
    return pl.pallas_call(
        kernel,
        out_shape=[jax.ShapeDtypeStruct(s, d) for s, d in outs],
        in_specs=[SCALARS] + [WHOLE] * len(args),
        out_specs=[WHOLE] * len(outs),
        scratch_shapes=[pltpu.VMEM(s, d) for s, d in scratch],
        compiler_params=pltpu.CompilerParams(vmem_limit_bytes=limit * MIB),
        cost_estimate=pl.CostEstimate(flops=flops, bytes_accessed=4 * MIB, transcendentals=0),
    )(scalars, *args)


def high_part(x):
    return x.astype(BF16).astype(F32)


def split3(x):
    a = high_part(x)
    b = high_part(x - a)
    return a, b, x - a - b


def lane_block(rows, values):
    lane = lax.broadcasted_iota(I32, (rows, LANES), 1)
    block = jnp.zeros((rows, LANES), F32)
    for k, value in enumerate(values):
        block = jnp.where(lane == k, value, block)
    return block


def join3(block, k):
    return block[:, k : k + 1] + block[:, k + 1 : k + 2] + block[:, k + 2 : k + 3]


def logits_kernel(_, mine, other, weight, out, part):
    half = mine.shape[0]
    voc = weight.shape[0]
    tops = []
    for h, tokens in enumerate((mine, other)):
        top = jnp.zeros((half, LANES), F32)
        for k in range(0, voc, CHUNK):
            block = lax.dot_general(
                tokens[...],
                weight[k : k + CHUNK, :],
                (((1,), (1,)), ((), ())),
                preferred_element_type=F32,
            )
            part[h * half : (h + 1) * half, k : k + CHUNK] = block
            size = jnp.abs(block)
            for c in range(0, CHUNK, LANES):
                top = jnp.maximum(top, size[:, c : c + LANES])
        tops.append(jnp.max(top, axis=1, keepdims=True))
    for h, top in enumerate(tops):
        grade = jnp.ceil(jnp.log2(jnp.maximum(top, 1e-30)) * GRAIN)
        per = STEPS * jnp.exp2(grade * (-1.0 / GRAIN))
        rows = slice(h * half, (h + 1) * half)
        for k in range(0, voc, CHUNK):
            out[rows, k : k + CHUNK] = (
                jnp.round(part[rows, k : k + CHUNK] * per).astype(I32).astype(I16)
            )
        out[rows, voc:] = jnp.broadcast_to(grade, (half, LANES)).astype(I32).astype(I16)


def softmax_kernel(scalars, got, label, out, logits):
    n, share, width = got.shape
    voc = width - LANES
    scales = [
        jnp.exp2(got[i, :, voc:].astype(I32).astype(F32)[:, :1] * (1.0 / GRAIN)) * (1.0 / STEPS)
        for i in range(n)
    ]
    top = jnp.full((share, LANES), -jnp.inf, F32)
    for k in range(0, voc, CHUNK):
        block = jnp.zeros((share, CHUNK), F32)
        for i in range(n):
            block += got[i, :, k : k + CHUNK].astype(I32).astype(F32) * scales[i]
        logits[:, k : k + CHUNK] = block
        for c in range(0, CHUNK, LANES):
            top = jnp.maximum(top, block[:, c : c + LANES])
    top = jnp.max(top, axis=1, keepdims=True)
    total = jnp.zeros((share, CHUNK), F32)
    target = jnp.zeros((share, CHUNK), F32)
    place = label[...] - scalars[0] * voc
    lane = lax.broadcasted_iota(I32, (share, CHUNK), 1)
    for k in range(0, voc, CHUNK):
        block = logits[:, k : k + CHUNK]
        expo = jnp.exp(block - top)
        total += expo
        hot = lane + k == place
        target += jnp.where(hot, block, 0.0)
        logits[:, k : k + CHUNK] = jnp.where(hot, 0.0, expo)
    total = jnp.sum(total, axis=1, keepdims=True)
    target = jnp.sum(target, axis=1, keepdims=True)
    inverse = 1.0 / total
    for k in range(0, voc, CHUNK):
        soft = (logits[:, k : k + CHUNK] * inverse).astype(BF16)
        for i in range(n):
            out[i, :, k : k + CHUNK] = soft
    stats = lane_block(share, split3(top + jnp.log(total)) + split3(target)).astype(BF16)
    for i in range(n):
        out[i, :, voc:] = stats


def partial_kernel(scalars, got, weight, row, label, send, part, stat):
    voc, feat = weight.shape
    half = got.shape[0] // 2
    product = jnp.dot(got[:, :voc], weight[...], preferred_element_type=F32)
    part[...] = product[:half]
    rest = product[half:]
    place = label[half:, :] - scalars[0] * voc
    owner = (place >= 0) & (place < voc)
    high = high_part(rest)
    send[:, :feat] = high.astype(BF16)
    send[:, feat : 2 * feat] = jnp.where(owner, row[half:, :], rest - high).astype(BF16)
    stats = got[:, voc:].astype(F32)
    lane = lax.broadcasted_iota(I32, (half, LANES), 1)
    moved = pltpu.roll(stats[half:], 6, 1)
    send[:, 2 * feat :] = jnp.where(lane < 6, stats[:half], moved).astype(BF16)
    stat[...] = lane_block(2 * half, [join3(stats, 0), join3(stats, 3)])


def pair_kernel(scalars, part, row, stat, got, label, out, rows):
    half, feat = part.shape
    section, core = scalars[0], scalars[2]
    voc = scalars[4]
    n_z = out.shape[0]
    mine_n = half // n_z
    theirs = got[:, 2 * feat :].astype(F32)
    own_log, own_target = stat[:, 0:1], stat[:, 1:2]
    other_log = jnp.concatenate([join3(theirs, 6), join3(theirs, 0)], axis=0)
    other_target = jnp.concatenate([join3(theirs, 9), join3(theirs, 3)], axis=0)
    first = jnp.where(core == 0, own_log, other_log)
    second = jnp.where(core == 0, other_log, own_log)
    top = jnp.maximum(first, second)
    pair_log = top + jnp.log(jnp.exp(first - top) + jnp.exp(second - top))
    pair_target = own_target + other_target
    stats = lane_block(
        2 * half, split3(pair_log) + split3(pair_target) + (own_log, own_target)
    ).T[:8]
    rows[...] = stats
    block = jnp.concatenate([stats[:, :half], stats[:, half:]], axis=0).astype(BF16)
    place = label[:half, :] - (section - core) * voc
    owner = (place >= 0) & (place < 2 * voc)
    own_owner = owner & (place >= core * voc) & (place < (core + 1) * voc)
    other_owner = owner & jnp.logical_not(own_owner)
    low = got[:, feat : 2 * feat].astype(F32)
    other_part = got[:, :feat].astype(F32) + jnp.where(other_owner, 0.0, low)
    total = part[...] * jnp.exp(own_log - pair_log)[:half] + other_part * jnp.exp(
        other_log - pair_log
    )[:half]
    high = high_part(total)
    low = jnp.where(own_owner, row[:half, :], jnp.where(other_owner, low, total - high))
    for i in range(n_z):
        at = slice(i * mine_n, (i + 1) * mine_n)
        out[i, :, :feat] = jnp.concatenate([high[at], low[at]], axis=0).astype(BF16)
        out[i, :, feat:] = block


def tail_kernel(
    scalars, got, soft, rows, mine, other, label, grad, own_label, own_grad, loss, hidden, weight
):
    n_z, twice, width = got.shape
    feat = width - LANES
    mine_n = twice // 2
    half, tokens = mine.shape[0], 2 * mine.shape[0]
    section, z, core, j, voc = (scalars[k] for k in range(5))

    def stat_rows(k):
        both = []
        for h in range(2):
            pieces = [got[:, h * mine_n + k + i, feat:].astype(F32) for i in range(3)]
            both.append(pieces[0] + pieces[1] + pieces[2])
        return jnp.concatenate(both, axis=1)

    logs = stat_rows(0)
    target = jnp.sum(stat_rows(3), axis=0, keepdims=True)
    top = jnp.max(logs, axis=0, keepdims=True)
    log_total = top + jnp.log(jnp.sum(jnp.exp(logs - top), axis=0, keepdims=True))
    label_part = jnp.exp(target - log_total) - 1.0
    losses = log_total - target
    pick = (half - j * (loss.shape[1] // 2)) % half
    first = pltpu.roll(jnp.broadcast_to(losses[:, :half], (8, half)), pick, 1)
    second = pltpu.roll(jnp.broadcast_to(losses[:, half:], (8, half)), pick, 1)
    loss_low = jnp.where(core == 0, first, second)
    loss_high = pltpu.roll(jnp.where(core == 0, second, first), loss.shape[1] // 2, 1)
    lane = lax.broadcasted_iota(I32, (8, half), 1)
    loss[...] = jnp.where(lane < loss.shape[1] // 2, loss_low, loss_high)[:1, : loss.shape[1]]

    shares = jnp.exp(logs - log_total)[:, :half]
    block = jnp.concatenate(
        [shares, jnp.broadcast_to(label_part[:, :half], (half - n_z, half))], axis=0
    )
    block = pltpu.roll(block, (half - z * mine_n) % half, 1).T[:mine_n]
    total = jnp.zeros((mine_n, feat), F32)
    row = jnp.zeros((mine_n, feat), F32)
    for i in range(n_z):
        both = got[i, :, :feat].astype(F32)
        place = own_label[...] - i * 2 * voc
        owner = (place >= 0) & (place < 2 * voc)
        low = both[mine_n:]
        total += (both[:mine_n] + jnp.where(owner, 0.0, low)) * block[:, i : i + 1]
        row += jnp.where(owner, low, 0.0)
    hidden[...] = (own_grad[...] * (total + row * block[:, n_z : n_z + 1])).astype(BF16)

    scale = grad[...] * jnp.exp(rows[6:7, :] - log_total)
    label_grad = grad[...] * label_part
    place = label[...] - section * voc
    tall = weight.shape[0]
    line = lax.broadcasted_iota(I32, (CHUNK, tokens), 0)
    for k in range(0, tall, CHUNK):
        value = soft[k : k + CHUNK, :].astype(F32) * scale
        value = jnp.where(line + k == place, label_grad, value).astype(BF16)
        weight[k : k + CHUNK, :] = (
            jnp.dot(value[:, :half], mine[...], preferred_element_type=F32)
            + jnp.dot(value[:, half:], other[...], preferred_element_type=F32)
        ).astype(BF16)


def local(hidden, head_weight, labels, loss_grad):
    voc, feat = head_weight.shape
    mine_n = hidden.shape[0]
    n_dp = lax.axis_size("dp")
    n_sec = lax.axis_size("section")
    n_z = n_sec // 2
    half = n_z * mine_n
    tokens = 2 * half
    share = tokens // n_dp
    section = lax.axis_index("section")
    z, core = section // 2, section % 2
    j = lax.axis_index("dp")
    scalars = jnp.stack([section, z, core, j, jnp.int32(voc)]).astype(I32)
    along_z = [[2 * k + c for k in range(n_z)] for c in range(2)]
    swap = [(i, i ^ 1) for i in range(n_sec)]
    flops = 2 * tokens * voc * feat

    def exchange_z(x):
        return lax.all_to_all(x, "section", 0, 0, tiled=True, axis_index_groups=along_z)

    def exchange_dp(x):
        return lax.all_to_all(x, "dp", 0, 0, tiled=True)

    def own_core_first(x):
        x = x.reshape(n_z, 2, mine_n)
        first = jnp.where(core == 0, x[:, 0], x[:, 1])
        second = jnp.where(core == 0, x[:, 1], x[:, 0])
        return jnp.concatenate([first.reshape(half), second.reshape(half)])

    label = own_core_first(labels)
    grad = own_core_first(loss_grad)
    label_column = label[:, None]
    share_label = lax.dynamic_slice_in_dim(label, j * share, share, 0)[:, None]
    own_label = lax.dynamic_slice_in_dim(label, z * mine_n, mine_n, 0)[:, None]
    own_grad = lax.dynamic_slice_in_dim(grad, z * mine_n, mine_n, 0)[:, None]
    columns = section * voc + jnp.arange(voc, dtype=I32)

    mine = exchange_z(jnp.broadcast_to(hidden[None], (n_z, mine_n, feat))).reshape(half, feat)
    other = lax.ppermute(mine, "section", swap)

    width = voc + LANES
    (coded,) = call(
        logits_kernel,
        scalars,
        [mine, other, head_weight],
        [((tokens, width), I16)],
        scratch=[((tokens, voc), F32)],
        flops=flops,
    )
    coded = exchange_dp(coded.reshape(n_dp, share, width))
    (message,) = call(
        softmax_kernel,
        scalars,
        [coded, share_label],
        [((n_dp, share, width), BF16)],
        scratch=[((share, voc), F32)],
    )
    got = exchange_dp(message).reshape(tokens, width)

    hot = label[:, None] == columns[None, :]
    row = jnp.dot(hot.astype(BF16), head_weight, preferred_element_type=F32)
    send, part, stat = call(
        partial_kernel,
        scalars,
        [got, head_weight, row, label_column],
        [((half, 2 * feat + LANES), BF16), ((half, feat), F32), ((tokens, LANES), F32)],
        flops=flops,
    )
    theirs = lax.ppermute(send, "section", swap)
    message, rows = call(
        pair_kernel,
        scalars,
        [part, row, stat, theirs, label_column],
        [((n_z, 2 * mine_n, feat + LANES), BF16), ((8, tokens), F32)],
    )
    last = exchange_z(message)
    soft = got[:, :voc].T
    loss, grad_hidden, grad_weight = call(
        tail_kernel,
        scalars,
        [last, soft, rows, mine, other, label[None], grad[None], own_label, own_grad],
        [((1, share), F32), ((mine_n, feat), BF16), ((voc, feat), BF16)],
        flops=flops,
    )
    return (loss.reshape(share), grad_hidden, grad_weight)


def solution(mesh):
    return jax.shard_map(
        local,
        mesh=mesh,
        in_specs=(P("section", "dp"), P("section", "dp"), P(), P()),
        out_specs=(P("dp"), P("section", "dp"), P("section", "dp")),
        check_vma=False,
    )
```

time: 404 us -> 124 us (0.31)
  waiting for transfers between devices: 246 us -> 51.6 us
  blocking collectives: 130 us -> 29.7 us
  starting transfers between devices: 0.12 us -> 21.1 us
  between operations: 13.8 us -> 0.84 us
  Pallas kernels: 0 us -> 11.1 us
  local copies, waits for them, and re-layouts: 0.76 us -> 6.28 us
  other arithmetic: 5.63 us -> 0.11 us
  matrix products: 6.96 us -> 1.55 us
    reduce_scatter x2 -> x0, waiting for transfers between devices: 190 us -> none  [the longest x1 105 us: local(): lax.psum_scatter(hidden_term, 'section', scatter_dimension=0, tiled=True)]
    all_gather x1 -> x0, waiting for transfers between devices: 56.2 us -> none  [local(): grads_all = lax.all_gather(dlogits, 'dp', axis=0, tiled=True)]
    all_to_all x0 -> x3, waiting for transfers between devices: none -> 48.9 us  [the longest x2 28.9 us: exchange_dp(): return lax.all_to_all(x, 'dp', 0, 0, tiled=True)]
    pmax x1 -> x0, blocking collectives: 47 us -> none  [local(): largest = lax.pmax(local_max, 'section')]
    psum x1 -> x0, blocking collectives: 45.8 us -> none  [local(): total, target = lax.psum((local_sum, local_target), 'section')]
    all_gather x1 -> x0, blocking collectives: 37.3 us -> none  [local(): whole = lax.all_gather(hidden, 'section', axis=0, tiled=True)]
    all_to_all x0 -> x1, blocking collectives: none -> 29.7 us  [exchange_z(): lax.all_to_all(x, 'section', 0, 0, tiled=True, axis_index_groups=along_z)]
    all_to_all x0 -> x3, starting transfers between devices: none -> 17.3 us  [the longest x2 13.5 us: exchange_dp(): return lax.all_to_all(x, 'dp', 0, 0, tiled=True)]
  transfers between devices with their start and end apart: 3 -> 5, of which waited for: 3 -> 5; matrix products, arithmetic and copies ran while one was open for 1% -> 3% of each run, Pallas kernels for 0% -> 0%
where the time goes in v2:
time: 124 us; the launch traced here: 122 us
  waiting for transfers between devices  51.6 us (42%)
  blocking collectives  29.7 us (24%)
  starting transfers between devices  21.1 us (17%)
  Pallas kernels  11.1 us (9%)
  local copies, waits for them, and re-layouts  6.28 us (5%)
  matrix products  1.55 us (1%)
    all_to_all x1, blocking collectives, exchange_z(): lax.all_to_all(x, 'section', 0, 0, tiled=True, axis_index_groups=along_z)  29.7 us
    all_to_all x2, waiting for transfers between devices, exchange_dp(): return lax.all_to_all(x, 'dp', 0, 0, tiled=True)  28.9 us
    all_to_all x1, waiting for transfers between devices, exchange_z(): lax.all_to_all(x, 'section', 0, 0, tiled=True, axis_index_groups=along_z)  20 us
    all_to_all x2, starting transfers between devices, exchange_dp(): return lax.all_to_all(x, 'dp', 0, 0, tiled=True)  13.5 us
    pallas_call x5, Pallas kernels, call(): pl.pallas_call(kernel, out_shape=[jax.ShapeDtypeStruct(s, d) for s, d in...  11.1 us
    unnamed x19, local copies, waits for them, and re-layouts  4.19 us
    all_to_all x1, starting transfers between devices, exchange_z(): lax.all_to_all(x, 'section', 0, 0, tiled=True, axis_index_groups=along_z)  3.83 us
  transfers between devices with their start and end apart: 5, of which 5 were waited for; matrix products, arithmetic and copies ran while one was open for 3% of the time, Pallas kernels for 0%

profile of v2, /device:TPU:6, one launch (start us, length us, event | category | flops | bytes accessed | tf_op | source)
XLA Modules:
  0.0 122.3 jit_solution(15876787755156767341)
XLA Ops:
  0.6 0.7 broadcast_in_dim.26
  1.3 29.7 %all_to_all.20 = bf16[16,8,512]{2,1,0:T(8,128)(2,1)S(1)} all-to-all(bf16[16,8,512]{2,1,0:T(8,128)(2,1)S(1)} %broadcast_in_dim.26), channel_id=1, replica_groups={{0,32,64,96,128,160,192,224,256,288,320,352,384,416,448,480},{16,48,80,..., dimensions={0} | all-to-all | bytes 262144 | tf_op jit(solution)/shard_map/all_to_all | solution.py:259
  31.0 1.9 %collective-permute-start = (bf16[128,512]{1,0:T(8,128)(2,1)S(1)}, bf16[128,512]{1,0:T(8,128)(2,1)S(1)}, u32[]{:S(2)}, u32[]{:S(2)}) collective-permute-start(bf16[128,512]{1,0:T(8,128)(2,1)S(1)} %bitcast.22), channel_id=1, source_target_pairs={{0,16},{16,0},{32,48},{48,32},{64,80},{80,64},{96,112},{112,96},{1... | collective-permute-start | bytes 393224 | tf_op jit(solution)/shard_map/ppermute | solution.py:279
  33.0 0.1 stack.19._.scalars
  33.1 1.2 collective-permute-done.other
  34.3 0.0 copy-start
  34.3 1.6 %copy-done = bf16[2048,512]{1,0:T(8,128)(2,1)S(1)} copy-done((bf16[2048,512]{1,0:T(8,128)(2,1)S(1)}, bf16[2048,512]{1,0:T(8,128)(2,1)}, u32[]{:S(2)}) %copy-start) | copy-done | bytes 2097176
  35.9 0.0 copy-start.4
  35.9 0.0 copy-start.6
  35.9 3.2 %shard_map.67 = s16[256,2176]{1,0:T(8,128)(2,1)} custom-call(s32[5]{0:T(128)S(1)} %stack.19._.scalars, bf16[128,512]{1,0:T(8,128)(2,1)S(1)} %bitcast.23, bf16[128,512]{1,0:T(8,128)(2,1)S(1)} %collective-permute-done.other, bf16[2048,512]{1,0:T(8,128)(2,1)S(1)} %copy-done), custom_call_target="tpu_custom_call" | custom-call | flops 536870912 | bytes 4194304 | tf_op jit(solution)/shard_map/pallas_call | solution.py:25
  39.1 0.0 copy-done.4
  39.1 7.4 %all-to-all-start.1 = ((s16[16,16,2176]{2,1,0:T(8,128)(2,1)}), s16[16,16,2176]{2,1,0:T(8,128)(2,1)S(1)}, u32[]{:S(2)}, u32[]{:S(2)}) async-start(s16[16,16,2176]{2,1,0:T(8,128)(2,1)} %bitcast.5), calls=%async_computation.1 | async-start | bytes 2228224 | tf_op jit(solution)/shard_map/all_to_all | solution.py:262
  46.5 0.0 copy-done.6
  46.5 0.1 reshape.52
  46.6 0.1 fusion.5
  46.7 0.1 select_n.60
  46.8 0.1 select_n.62
  46.9 0.1 dynamic-slice_bitcast_fusion.2
  47.0 0.1 copy.12.label
  47.0 15.9 %all-to-all-done.1.got = s16[16,16,2176]{2,1,0:T(8,128)(2,1)S(1)} async-done(((s16[16,16,2176]{2,1,0:T(8,128)(2,1)}), s16[16,16,2176]{2,1,0:T(8,128)(2,1)S(1)}, u32[]{:S(2)}, u32[]{:S(2)}) %all-to-all-start.1) | async-done | bytes 1114144 | tf_op jit(solution)/shard_map/all_to_all | solution.py:262
  62.9 1.1 shard_map.68
  64.0 0.0 copy-start.2
  64.0 1.0 copy-done.2
  65.0 6.1 %all-to-all-start.2 = ((bf16[16,16,2176]{2,1,0:T(8,128)(2,1)}), bf16[16,16,2176]{2,1,0:T(8,128)(2,1)S(1)}, u32[]{:S(2)}, u32[]{:S(2)}) async-start(bf16[16,16,2176]{2,1,0:T(8,128)(2,1)} %copy-done.2), calls=%async_computation.2 | async-start | bytes 2228224 | tf_op jit(solution)/shard_map/all_to_all | solution.py:262
  71.1 0.1 copy.13.label
  71.2 0.0 copy-done.1
  71.2 1.6 %fusion.row = f32[256,512]{1,0:T(8,128)} fusion(bf16[2048,512]{1,0:T(8,128)(2,1)S(1)} %copy-done.1, s32[2048]{0:T(1024)S(1)} %iota_add_fusion, s32[256]{0:T(256)S(1)} %constant_dynamic-update-slice_fusion), kind=kOutput, calls=%fused_computation | convolution fusion | flops 537395200 | bytes 2630656 | tf_op jit(solution)/shard_map/dot_general | solution.py:301
  72.8 13.0 %all-to-all-done.2 = bf16[16,16,2176]{2,1,0:T(8,128)(2,1)S(1)} async-done(((bf16[16,16,2176]{2,1,0:T(8,128)(2,1)}), bf16[16,16,2176]{2,1,0:T(8,128)(2,1)S(1)}, u32[]{:S(2)}, u32[]{:S(2)}) %all-to-all-start.2) | async-done | bytes 1114144 | tf_op jit(solution)/shard_map/all_to_all | solution.py:262
  85.8 1.0 copy-done.3
  86.8 1.3 %shard_map.69 = (bf16[128,1152]{1,0:T(8,128)(2,1)S(1)}, f32[128,512]{1,0:T(8,128)S(1)}, f32[256,128]{1,0:T(8,128)S(1)}) custom-call(s32[5]{0:T(128)S(1)} %stack.19._.scalars, bf16[256,2176]{1,0:T(8,128)(2,1)S(1)} %bitcast.19, bf16[2048,512]{1,0:T(8,128)(2,1)S(1)} %copy-done.1, f32[256,512]{1,0:T(8,128)S(1)} %copy-done.3, s32[256,1]{1,0:T(8,128)S(1)} %copy.13.label), custom_call_target="tpu_custom_call" | custom-call | flops 536870912 | bytes 4194304 | tf_op jit(solution)/shard_map/pallas_call | solution.py:25
  88.1 1.9 %collective-permute-start.1 = (bf16[128,1152]{1,0:T(8,128)(2,1)S(1)}, bf16[128,1152]{1,0:T(8,128)(2,1)S(1)}, u32[]{:S(2)}, u32[]{:S(2)}) collective-permute-start(bf16[128,1152]{1,0:T(8,128)(2,1)S(1)} %get-tuple-element.13), channel_id=1, source_target_pairs={{0,16},{16,0},{32,48},{48,32},{64,80},{80,64},{96,112},{112,96},{1... | collective-permute-start | bytes 884744 | tf_op jit(solution)/shard_map/ppermute | solution.py:309
  90.0 1.5 %collective-permute-done.1.got = bf16[128,1152]{1,0:T(8,128)(2,1)S(1)} collective-permute-done((bf16[128,1152]{1,0:T(8,128)(2,1)S(1)}, bf16[128,1152]{1,0:T(8,128)(2,1)S(1)}, u32[]{:S(2)}, u32[]{:S(2)}) %collective-permute-start.1) | collective-permute-done | bytes 294944 | tf_op jit(solution)/shard_map/ppermute | solution.py:309
  91.6 2.4 %shard_map.70 = (bf16[16,16,640]{2,1,0:T(8,128)(2,1)}, f32[8,256]{1,0:T(8,128)S(1)}) custom-call(s32[5]{0:T(128)S(1)} %stack.19._.scalars, f32[128,512]{1,0:T(8,128)S(1)} %get-tuple-element.11.part, f32[256,512]{1,0:T(8,128)S(1)} %copy-done.3, f32[256,128]{1,0:T(8,128)S(1)} %get-tuple-element.12.stat, bf16[128,1152]{1,0:T(8,128)(2,1)S(1)} %collective-permute-done.1.got, ...), custom_call_target="tpu_custom_call" | custom-call | bytes 4194304 | tf_op jit(solution)/shard_map/pallas_call | solution.py:25
  93.9 3.8 %all-to-all-start.3 = ((bf16[16,16,640]{2,1,0:T(8,128)(2,1)}), bf16[16,16,640]{2,1,0:T(8,128)(2,1)S(1)}, u32[]{:S(2)}, u32[]{:S(2)}) async-start(bf16[16,16,640]{2,1,0:T(8,128)(2,1)} %get-tuple-element.14), calls=%async_computation.3 | async-start | bytes 655360 | tf_op jit(solution)/shard_map/all_to_all | solution.py:259
  97.8 0.0 copy-done.7
  97.8 0.1 reshape.54
  97.9 0.1 fusion.7
  98.0 0.1 select_n.65
  98.0 0.1 select_n.67
  98.1 0.1 dynamic-slice_bitcast_fusion.1
  98.2 0.1 copy.16.own_label
  98.3 0.1 dynamic-slice_bitcast_fusion
  98.4 0.1 copy.17.own_grad
  98.5 0.1 slice.26
  98.6 0.5 copy.18
  99.2 20.0 %all-to-all-done.3.got = bf16[16,16,640]{2,1,0:T(8,128)(2,1)S(1)} async-done(((bf16[16,16,640]{2,1,0:T(8,128)(2,1)}), bf16[16,16,640]{2,1,0:T(8,128)(2,1)S(1)}, u32[]{:S(2)}, u32[]{:S(2)}) %all-to-all-start.3) | async-done | bytes 327712 | tf_op jit(solution)/shard_map/all_to_all | solution.py:259
  119.1 0.0 copy-done.5
  119.1 3.2 %shard_map.71 = (f32[1,16]{1,0:T(1,128)}, bf16[8,512]{1,0:T(8,128)(2,1)}, bf16[2048,512]{1,0:T(8,128)(2,1)}) custom-call(s32[5]{0:T(128)S(1)} %stack.19._.scalars, bf16[16,16,640]{2,1,0:T(8,128)(2,1)S(1)} %all-to-all-done.3.got, bf16[2048,256]{1,0:T(8,128)(2,1)S(1)} %bitcast.21, f32[8,256]{1,0:T(8,128)S(1)} %get-tuple-element.15.rows, ...), custom_call_target="tpu_custom_call" | custom-call | flops 536870912 | bytes 4194304 | tf_op jit(solution)/shard_map/pallas_call | solution.py:25
  (11 shorter events, 0.1 us)
Async XLA Ops:
  31.0 3.2 %collective-permute-start = (bf16[128,512]{1,0:T(8,128)(2,1)S(1)}, bf16[128,512]{1,0:T(8,128)(2,1)S(1)}, u32[]{:S(2)}, u32[]{:S(2)}) collective-permute-start(bf16[128,512]{1,0:T(8,128)(2,1)S(1)} %bitcast.22), channel_id=1, source_target_pairs={{0,16},{16,0},{32,48},{48,32},{64,80},{80,64},{96,112},{112,96},{1... | collective-permute-start | bytes 393224 | tf_op jit(solution)/shard_map/ppermute | solution.py:279
  34.3 1.6 %copy-start = (bf16[2048,512]{1,0:T(8,128)(2,1)S(1)}, bf16[2048,512]{1,0:T(8,128)(2,1)}, u32[]{:S(2)}) copy-start(bf16[2048,512]{1,0:T(8,128)(2,1)} %weight.3) | copy-start | bytes 6291460
  35.9 3.2 %copy-start.4 = (bf16[128,512]{1,0:T(8,128)(2,1)}, bf16[128,512]{1,0:T(8,128)(2,1)S(1)}, u32[]{:S(2)}) copy-start(bf16[128,512]{1,0:T(8,128)(2,1)S(1)} %collective-permute-done.other) | copy-start | bytes 393220
  35.9 10.6 %copy-start.6 = (s32[256]{0:T(256)S(1)}, s32[256]{0:T(256)}, u32[]{:S(2)}) copy-start(s32[256]{0:T(256)} %param.6) | copy-start | bytes 3076
  39.1 23.9 %all-to-all-start.1 = ((s16[16,16,2176]{2,1,0:T(8,128)(2,1)}), s16[16,16,2176]{2,1,0:T(8,128)(2,1)S(1)}, u32[]{:S(2)}, u32[]{:S(2)}) async-start(s16[16,16,2176]{2,1,0:T(8,128)(2,1)} %bitcast.5), calls=%async_computation.1 | async-start | bytes 2228224 | tf_op jit(solution)/shard_map/all_to_all | solution.py:262
  47.0 24.2 %copy-start.1 = (bf16[2048,512]{1,0:T(8,128)(2,1)S(1)}, bf16[2048,512]{1,0:T(8,128)(2,1)}, u32[]{:S(2)}) copy-start(bf16[2048,512]{1,0:T(8,128)(2,1)} %weight.3) | copy-start | bytes 6291460
  64.0 1.0 copy-start.2
  65.0 20.8 %all-to-all-start.2 = ((bf16[16,16,2176]{2,1,0:T(8,128)(2,1)}), bf16[16,16,2176]{2,1,0:T(8,128)(2,1)S(1)}, u32[]{:S(2)}, u32[]{:S(2)}) async-start(bf16[16,16,2176]{2,1,0:T(8,128)(2,1)} %copy-done.2), calls=%async_computation.2 | async-start | bytes 2228224 | tf_op jit(solution)/shard_map/all_to_all | solution.py:262
  85.8 1.0 copy-start.3
  86.8 11.0 %copy-start.7 = (f32[256]{0:T(256)S(1)}, f32[256]{0:T(256)}, u32[]{:S(2)}) copy-start(f32[256]{0:T(256)} %param.7) | copy-start | bytes 3076
  88.1 3.5 %collective-permute-start.1 = (bf16[128,1152]{1,0:T(8,128)(2,1)S(1)}, bf16[128,1152]{1,0:T(8,128)(2,1)S(1)}, u32[]{:S(2)}, u32[]{:S(2)}) collective-permute-start(bf16[128,1152]{1,0:T(8,128)(2,1)S(1)} %get-tuple-element.13), channel_id=1, source_target_pairs={{0,16},{16,0},{32,48},{48,32},{64,80},{80,64},{96,112},{112,96},{1... | collective-permute-start | bytes 884744 | tf_op jit(solution)/shard_map/ppermute | solution.py:309
  93.9 25.2 %all-to-all-start.3 = ((bf16[16,16,640]{2,1,0:T(8,128)(2,1)}), bf16[16,16,640]{2,1,0:T(8,128)(2,1)S(1)}, u32[]{:S(2)}, u32[]{:S(2)}) async-start(bf16[16,16,640]{2,1,0:T(8,128)(2,1)} %get-tuple-element.14), calls=%async_computation.3 | async-start | bytes 655360 | tf_op jit(solution)/shard_map/all_to_all | solution.py:259
  98.5 20.6 %copy-start.5 = (bf16[128,512]{1,0:T(8,128)(2,1)S(1)}, bf16[128,512]{1,0:T(8,128)(2,1)}, u32[]{:S(2)}) copy-start(bf16[128,512]{1,0:T(8,128)(2,1)} %copy-done.4) | copy-start | bytes 393220

commit v3 on v2

--- a/solution.py
+++ b/solution.py
@@ -21,14 +21,19 @@
 WHOLE = pl.BlockSpec(memory_space=pltpu.VMEM)
 
 
-def call(kernel, scalars, args, outs, scratch=(), limit=24, flops=0):
+def call(kernel, scalars, args, outs, scratch=(), copies=0, flops=0):
+    out_specs = [WHOLE] * len(outs)
+    scratch_shapes = [pltpu.VMEM(s, d) for s, d in scratch]
+    if copies:
+        out_specs[-1] = pl.BlockSpec(memory_space=pl.ANY)
+        scratch_shapes.append(pltpu.SemaphoreType.DMA((copies,)))
     return pl.pallas_call(
         kernel,
         out_shape=[jax.ShapeDtypeStruct(s, d) for s, d in outs],
         in_specs=[SCALARS] + [WHOLE] * len(args),
-        out_specs=[WHOLE] * len(outs),
-        scratch_shapes=[pltpu.VMEM(s, d) for s, d in scratch],
-        compiler_params=pltpu.CompilerParams(vmem_limit_bytes=limit * MIB),
+        out_specs=out_specs,
+        scratch_shapes=scratch_shapes,
+        compiler_params=pltpu.CompilerParams(vmem_limit_bytes=16 * MIB),
         cost_estimate=pl.CostEstimate(flops=flops, bytes_accessed=4 * MIB, transcendentals=0),
     )(scalars, *args)
 
@@ -52,36 +57,27 @@
 
 
 def join3(block, k):
-    return block[:, k : k + 1] + block[:, k + 1 : k + 2] + block[:, k + 2 : k + 3]
-
-
-def logits_kernel(_, mine, other, weight, out, part):
+    return block[k : k + 1] + block[k + 1 : k + 2] + block[k + 2 : k + 3]
+
+
+def logits_kernel(_, mine, other, weight, out, whole, part):
     half = mine.shape[0]
-    voc = weight.shape[0]
-    tops = []
-    for h, tokens in enumerate((mine, other)):
-        top = jnp.zeros((half, LANES), F32)
-        for k in range(0, voc, CHUNK):
-            block = lax.dot_general(
-                tokens[...],
-                weight[k : k + CHUNK, :],
-                (((1,), (1,)), ((), ())),
-                preferred_element_type=F32,
-            )
-            part[h * half : (h + 1) * half, k : k + CHUNK] = block
-            size = jnp.abs(block)
-            for c in range(0, CHUNK, LANES):
-                top = jnp.maximum(top, size[:, c : c + LANES])
-        tops.append(jnp.max(top, axis=1, keepdims=True))
-    for h, top in enumerate(tops):
-        grade = jnp.ceil(jnp.log2(jnp.maximum(top, 1e-30)) * GRAIN)
-        per = STEPS * jnp.exp2(grade * (-1.0 / GRAIN))
-        rows = slice(h * half, (h + 1) * half)
-        for k in range(0, voc, CHUNK):
-            out[rows, k : k + CHUNK] = (
-                jnp.round(part[rows, k : k + CHUNK] * per).astype(I32).astype(I16)
-            )
-        out[rows, voc:] = jnp.broadcast_to(grade, (half, LANES)).astype(I32).astype(I16)
+    voc = weight.shape[1]
+    whole[:half, :] = mine[...]
+    whole[half:, :] = other[...]
+    top = jnp.zeros((2 * half, LANES), F32)
+    for k in range(0, voc, CHUNK):
+        block = jnp.dot(whole[...], weight[:, k : k + CHUNK], preferred_element_type=F32)
+        part[:, k : k + CHUNK] = block
+        size = jnp.abs(block)
+        for c in range(0, CHUNK, LANES):
+            top = jnp.maximum(top, size[:, c : c + LANES])
+    top = jnp.max(top, axis=1, keepdims=True)
+    grade = jnp.ceil(jnp.log2(jnp.maximum(top, 1e-30)) * GRAIN)
+    per = STEPS * jnp.exp2(grade * (-1.0 / GRAIN))
+    for k in range(0, voc, CHUNK):
+        out[:, k : k + CHUNK] = jnp.round(part[:, k : k + CHUNK] * per).astype(I32).astype(I16)
+    out[:, voc:] = jnp.broadcast_to(grade, (2 * half, LANES)).astype(I32).astype(I16)
 
 
 def softmax_kernel(scalars, got, label, out, logits):
@@ -126,52 +122,53 @@
 def partial_kernel(scalars, got, weight, row, label, send, part, stat):
     voc, feat = weight.shape
     half = got.shape[0] // 2
-    product = jnp.dot(got[:, :voc], weight[...], preferred_element_type=F32)
-    part[...] = product[:half]
-    rest = product[half:]
+    stats = got[:, voc:].astype(F32).T[:8]
+    send[half:, :LANES] = jnp.concatenate([stats[:, :half], stats[:, half:]], axis=0).astype(BF16)
+    stat[...] = jnp.concatenate([join3(stats, 0), join3(stats, 3), stats[:6]], axis=0)
+    rest = jnp.dot(got[half:, :voc], weight[...], preferred_element_type=F32)
     place = label[half:, :] - scalars[0] * voc
     owner = (place >= 0) & (place < voc)
-    high = high_part(rest)
-    send[:, :feat] = high.astype(BF16)
-    send[:, feat : 2 * feat] = jnp.where(owner, row[half:, :], rest - high).astype(BF16)
-    stats = got[:, voc:].astype(F32)
-    lane = lax.broadcasted_iota(I32, (half, LANES), 1)
-    moved = pltpu.roll(stats[half:], 6, 1)
-    send[:, 2 * feat :] = jnp.where(lane < 6, stats[:half], moved).astype(BF16)
-    stat[...] = lane_block(2 * half, [join3(stats, 0), join3(stats, 3)])
-
-
-def pair_kernel(scalars, part, row, stat, got, label, out, rows):
+    high = rest.astype(BF16)
+    send[:half, :feat] = high
+    send[:half, feat:] = jnp.where(
+        owner, row[half:, :].astype(F32), rest - high.astype(F32)
+    ).astype(BF16)
+    part[...] = jnp.dot(got[:half, :voc], weight[...], preferred_element_type=F32)
+
+
+def pair_kernel(scalars, part, row, stat, got, label, out):
     half, feat = part.shape
     section, core = scalars[0], scalars[2]
     voc = scalars[4]
     n_z = out.shape[0]
     mine_n = half // n_z
-    theirs = got[:, 2 * feat :].astype(F32)
-    own_log, own_target = stat[:, 0:1], stat[:, 1:2]
-    other_log = jnp.concatenate([join3(theirs, 6), join3(theirs, 0)], axis=0)
-    other_target = jnp.concatenate([join3(theirs, 9), join3(theirs, 3)], axis=0)
+    theirs = got[half:, :LANES].astype(F32)
+    own_log, own_target = stat[0:1, :], stat[1:2, :]
+    other_log = jnp.concatenate([join3(theirs, 8), join3(theirs, 0)], axis=1)
+    other_target = jnp.concatenate([join3(theirs, 11), join3(theirs, 3)], axis=1)
     first = jnp.where(core == 0, own_log, other_log)
     second = jnp.where(core == 0, other_log, own_log)
     top = jnp.maximum(first, second)
     pair_log = top + jnp.log(jnp.exp(first - top) + jnp.exp(second - top))
-    pair_target = own_target + other_target
-    stats = lane_block(
-        2 * half, split3(pair_log) + split3(pair_target) + (own_log, own_target)
-    ).T[:8]
-    rows[...] = stats
+    shares = jnp.concatenate(
+        [jnp.exp(own_log - pair_log)[:, :half], jnp.exp(other_log - pair_log)[:, :half]], axis=0
+    )
+    shares = jnp.concatenate([shares] * (half // 2), axis=0).T
+    stats = jnp.concatenate(
+        split3(pair_log) + split3(own_target + other_target) + (own_log, own_log), axis=0
+    )
     block = jnp.concatenate([stats[:, :half], stats[:, half:]], axis=0).astype(BF16)
     place = label[:half, :] - (section - core) * voc
     owner = (place >= 0) & (place < 2 * voc)
     own_owner = owner & (place >= core * voc) & (place < (core + 1) * voc)
     other_owner = owner & jnp.logical_not(own_owner)
-    low = got[:, feat : 2 * feat].astype(F32)
-    other_part = got[:, :feat].astype(F32) + jnp.where(other_owner, 0.0, low)
-    total = part[...] * jnp.exp(own_log - pair_log)[:half] + other_part * jnp.exp(
-        other_log - pair_log
-    )[:half]
+    low = got[:half, feat:].astype(F32)
+    other_part = got[:half, :feat].astype(F32) + jnp.where(other_owner, 0.0, low)
+    total = part[...] * shares[:, 0:1] + other_part * shares[:, 1:2]
     high = high_part(total)
-    low = jnp.where(own_owner, row[:half, :], jnp.where(other_owner, low, total - high))
+    low = jnp.where(
+        own_owner, row[:half, :].astype(F32), jnp.where(other_owner, low, total - high)
+    )
     for i in range(n_z):
         at = slice(i * mine_n, (i + 1) * mine_n)
         out[i, :, :feat] = jnp.concatenate([high[at], low[at]], axis=0).astype(BF16)
@@ -179,12 +176,13 @@
 
 
 def tail_kernel(
-    scalars, got, soft, rows, mine, other, label, grad, own_label, own_grad, loss, hidden, weight
+    scalars, got, soft, stat, whole, label, grad, own_label, own_grad, loss, hidden, weight, staged, sems
 ):
     n_z, twice, width = got.shape
     feat = width - LANES
     mine_n = twice // 2
-    half, tokens = mine.shape[0], 2 * mine.shape[0]
+    tokens = whole.shape[0]
+    half = tokens // 2
     section, z, core, j, voc = (scalars[k] for k in range(5))
 
     def stat_rows(k):
@@ -200,6 +198,22 @@
     log_total = top + jnp.log(jnp.sum(jnp.exp(logs - top), axis=0, keepdims=True))
     label_part = jnp.exp(target - log_total) - 1.0
     losses = log_total - target
+
+    scale = grad[...] * jnp.exp(stat[0:1, :] - log_total)
+    label_grad = grad[...] * label_part
+    place = label[...] - section * voc
+    line = lax.broadcasted_iota(I32, (CHUNK, tokens), 0)
+    copies = []
+    for n, k in enumerate(range(0, weight.shape[0], CHUNK)):
+        value = soft[k : k + CHUNK, :].astype(F32) * scale
+        value = jnp.where(line + k == place, label_grad, value).astype(BF16)
+        staged[k : k + CHUNK, :] = jnp.dot(
+            value, whole[...], preferred_element_type=F32
+        ).astype(BF16)
+        at = pl.ds(k, CHUNK)
+        copies.append(pltpu.make_async_copy(staged.at[at], weight.at[at], sems.at[n]))
+        copies[-1].start()
+
     pick = (half - j * (loss.shape[1] // 2)) % half
     first = pltpu.roll(jnp.broadcast_to(losses[:, :half], (8, half)), pick, 1)
     second = pltpu.roll(jnp.broadcast_to(losses[:, half:], (8, half)), pick, 1)
@@ -223,19 +237,8 @@
         total += (both[:mine_n] + jnp.where(owner, 0.0, low)) * block[:, i : i + 1]
         row += jnp.where(owner, low, 0.0)
     hidden[...] = (own_grad[...] * (total + row * block[:, n_z : n_z + 1])).astype(BF16)
-
-    scale = grad[...] * jnp.exp(rows[6:7, :] - log_total)
-    label_grad = grad[...] * label_part
-    place = label[...] - section * voc
-    tall = weight.shape[0]
-    line = lax.broadcasted_iota(I32, (CHUNK, tokens), 0)
-    for k in range(0, tall, CHUNK):
-        value = soft[k : k + CHUNK, :].astype(F32) * scale
-        value = jnp.where(line + k == place, label_grad, value).astype(BF16)
-        weight[k : k + CHUNK, :] = (
-            jnp.dot(value[:, :half], mine[...], preferred_element_type=F32)
-            + jnp.dot(value[:, half:], other[...], preferred_element_type=F32)
-        ).astype(BF16)
+    for copy in copies:
+        copy.wait()
 
 
 def local(hidden, head_weight, labels, loss_grad):
@@ -276,14 +279,19 @@
     columns = section * voc + jnp.arange(voc, dtype=I32)
 
     mine = exchange_z(jnp.broadcast_to(hidden[None], (n_z, mine_n, feat))).reshape(half, feat)
+    hot = label[:, None] == columns[None, :]
+    row = jnp.dot(hot.astype(BF16), head_weight, preferred_element_type=F32).astype(BF16)
+    ready = (mine, row, head_weight.T, label, grad, label_column, share_label, own_label, own_grad)
+    ready = lax.optimization_barrier(ready)
+    mine, row, tall, label, grad, label_column, share_label, own_label, own_grad = ready
     other = lax.ppermute(mine, "section", swap)
 
     width = voc + LANES
-    (coded,) = call(
+    coded, whole = call(
         logits_kernel,
         scalars,
-        [mine, other, head_weight],
-        [((tokens, width), I16)],
+        [mine, other, tall],
+        [((tokens, width), I16), ((tokens, feat), BF16)],
         scratch=[((tokens, voc), F32)],
         flops=flops,
     )
@@ -297,29 +305,29 @@
     )
     got = exchange_dp(message).reshape(tokens, width)
 
-    hot = label[:, None] == columns[None, :]
-    row = jnp.dot(hot.astype(BF16), head_weight, preferred_element_type=F32)
     send, part, stat = call(
         partial_kernel,
         scalars,
         [got, head_weight, row, label_column],
-        [((half, 2 * feat + LANES), BF16), ((half, feat), F32), ((tokens, LANES), F32)],
+        [((half + 16, 2 * feat), BF16), ((half, feat), F32), ((8, tokens), F32)],
         flops=flops,
     )
     theirs = lax.ppermute(send, "section", swap)
-    message, rows = call(
+    (message,) = call(
         pair_kernel,
         scalars,
         [part, row, stat, theirs, label_column],
-        [((n_z, 2 * mine_n, feat + LANES), BF16), ((8, tokens), F32)],
+        [((n_z, 2 * mine_n, feat + LANES), BF16)],
     )
     last = exchange_z(message)
     soft = got[:, :voc].T
     loss, grad_hidden, grad_weight = call(
         tail_kernel,
         scalars,
-        [last, soft, rows, mine, other, label[None], grad[None], own_label, own_grad],
+        [last, soft, stat, whole, label[None], grad[None], own_label, own_grad],
         [((1, share), F32), ((mine_n, feat), BF16), ((voc, feat), BF16)],
+        scratch=[((voc, feat), BF16)],
+        copies=voc // CHUNK,
         flops=flops,
     )
     return (loss.reshape(share), grad_hidden, grad_weight)

time: 124 us -> 123 us (level)
  blocking collectives: 29.7 us -> 0 us
  starting transfers between devices: 21.1 us -> 38.2 us
  waiting for transfers between devices: 51.6 us -> 60.6 us
  local copies, waits for them, and re-layouts: 6.28 us -> 9.54 us
  Pallas kernels: 11.1 us -> 9.22 us
  matrix products: 1.55 us -> 3.04 us
    all_to_all x1 -> x0, blocking collectives: 29.7 us -> none  [exchange_z(): lax.all_to_all(x, 'section', 0, 0, tiled=True, axis_index_groups=along_z)]
    all_to_all x1 -> x2, starting transfers between devices: 3.83 us -> 20.9 us  [exchange_z(): lax.all_to_all(x, 'section', 0, 0, tiled=True, axis_index_groups=along_z)]
    all_to_all x1 -> x2, waiting for transfers between devices: 20 us -> 26.9 us  [exchange_z(): lax.all_to_all(x, 'section', 0, 0, tiled=True, axis_index_groups=along_z)]
    all_to_all x2, waiting for transfers between devices: 28.9 us -> 30.9 us  [exchange_dp(): return lax.all_to_all(x, 'dp', 0, 0, tiled=True)]
    pallas_call x5, Pallas kernels: 11.1 us -> 9.22 us  [call(): pl.pallas_call(kernel, out_shape=[jax.ShapeDtypeStruct(s, d) for s, d in...]
    dot_general x1, matrix products: 1.55 us -> 3.04 us  [local(): jnp.dot(hot.astype(BF16), head_weight, preferred_element_type=F32)]
    reshape x2, local copies, waits for them, and re-layouts: 0.19 us -> 1.55 us  [own_core_first(): x = x.reshape(n_z, 2, mine_n)]
    unnamed x19 -> x16, local copies, waits for them, and re-layouts: 4.19 us -> 5.43 us
  transfers between devices with their start and end apart: 5 -> 6, of which waited for: 5 -> 6; matrix products, arithmetic and copies ran while one was open for 3% -> 8% of each run, Pallas kernels for 0% -> 0%
where the time goes in v3:
time: 123 us; the launch traced here: 122 us
  waiting for transfers between devices  60.6 us (49%)
  starting transfers between devices  38.2 us (31%)
  local copies, waits for them, and re-layouts  9.54 us (8%)
  Pallas kernels  9.22 us (7%)
  matrix products  3.04 us (2%)
    all_to_all x2, waiting for transfers between devices, exchange_dp(): return lax.all_to_all(x, 'dp', 0, 0, tiled=True)  30.9 us
    all_to_all x2, waiting for transfers between devices, exchange_z(): lax.all_to_all(x, 'section', 0, 0, tiled=True, axis_index_groups=along_z)  26.9 us
    all_to_all x2, starting transfers between devices, exchange_z(): lax.all_to_all(x, 'section', 0, 0, tiled=True, axis_index_groups=along_z)  20.9 us
    all_to_all x2, starting transfers between devices, exchange_dp(): return lax.all_to_all(x, 'dp', 0, 0, tiled=True)  13.5 us
    pallas_call x5, Pallas kernels, call(): pl.pallas_call(kernel, out_shape=[jax.ShapeDtypeStruct(s, d) for s, d in...  9.22 us
    unnamed x16, local copies, waits for them, and re-layouts  5.43 us
    dot_general x1, matrix products, local(): jnp.dot(hot.astype(BF16), head_weight, preferred_element_type=F32)  3.04 us
  transfers between devices with their start and end apart: 6, of which 6 were waited for; matrix products, arithmetic and copies ran while one was open for 8% of the time, Pallas kernels for 0%

profile of v3, /device:TPU:6, one launch (start us, length us, event | category | flops | bytes accessed | tf_op | source)
XLA Modules:
  0.0 121.5 jit_solution(5525571817488890332)
XLA Ops:
  0.6 1.4 %broadcast_in_dim.26 = bf16[16,8,512]{2,1,0:T(8,128)(2,1)} broadcast(bf16[8,512]{1,0:T(8,128)(2,1)} %param.4), dimensions={1,2} | broadcast | bytes 139264 | tf_op jit(solution)/shard_map/broadcast_in_dim | solution.py:281
  2.0 15.2 %all-to-all-start = ((bf16[16,8,512]{2,1,0:T(8,128)(2,1)}), bf16[16,8,512]{2,1,0:T(8,128)(2,1)S(1)}, u32[]{:S(2)}, u32[]{:S(2)}) async-start(bf16[16,8,512]{2,1,0:T(8,128)(2,1)} %broadcast_in_dim.26), calls=%async_computation | async-start | bytes 262144 | tf_op jit(solution)/shard_map/all_to_all | solution.py:262
  17.3 0.8 reshape.51
  18.0 0.1 fusion.8
  18.1 0.1 select_n.60
  18.2 0.1 select_n.62
  18.3 0.8 reshape.52
  19.1 0.1 fusion.10
  19.1 0.1 select_n.64
  19.2 0.1 select_n.66
  19.4 0.1 dynamic-slice_bitcast_fusion
  19.4 0.1 dynamic-slice_bitcast_fusion.1
  19.5 2.9 %copy.13 = bf16[2048,512]{0,1:T(8,128)(2,1)S(1)} copy(bf16[2048,512]{1,0:T(8,128)(2,1)} %weight.1) | data formatting | bytes 4194304 | tf_op args[1]
  22.4 0.1 dynamic-slice_bitcast_fusion.2
  22.5 3.0 %fusion.2.row = bf16[256,512]{1,0:T(8,128)(2,1)} fusion(bf16[2048,512]{1,0:T(8,128)(2,1)} %weight.1, s32[2048]{0:T(1024)S(1)} %iota_add_fusion, s32[256]{0:T(256)S(1)} %constant_dynamic-update-slice_fusion), kind=kOutput, calls=%fused_computation.2 | convolution fusion | flops 537526272 | bytes 2368512 | tf_op jit(solution)/shard_map/dot_general | solution.py:283
  25.6 6.3 %all-to-all-done = bf16[16,8,512]{2,1,0:T(8,128)(2,1)S(1)} async-done(((bf16[16,8,512]{2,1,0:T(8,128)(2,1)}), bf16[16,8,512]{2,1,0:T(8,128)(2,1)S(1)}, u32[]{:S(2)}, u32[]{:S(2)}) %all-to-all-start) | async-done | bytes 131104 | tf_op jit(solution)/shard_map/all_to_all | solution.py:262
  31.9 1.9 %collective-permute-start = (bf16[128,512]{1,0:T(8,128)(2,1)S(1)}, bf16[128,512]{1,0:T(8,128)(2,1)S(1)}, u32[]{:S(2)}, u32[]{:S(2)}) collective-permute-start(bf16[128,512]{1,0:T(8,128)(2,1)S(1)} %bitcast.24), channel_id=1, source_target_pairs={{0,16},{16,0},{32,48},{48,32},{64,80},{80,64},{96,112},{112,96},{1... | collective-permute-start | bytes 393224 | tf_op jit(solution)/shard_map/ppermute | solution.py:287
  33.8 0.1 stack.19._.scalars
  33.9 1.2 %collective-permute-done.other = bf16[128,512]{1,0:T(8,128)(2,1)S(1)} collective-permute-done((bf16[128,512]{1,0:T(8,128)(2,1)S(1)}, bf16[128,512]{1,0:T(8,128)(2,1)S(1)}, u32[]{:S(2)}, u32[]{:S(2)}) %collective-permute-start) | collective-permute-done | bytes 131104 | tf_op jit(solution)/shard_map/ppermute | solution.py:287
  35.1 2.5 %shard_map.67 = (s16[256,2176]{1,0:T(8,128)(2,1)}, bf16[256,512]{1,0:T(8,128)(2,1)S(1)}) custom-call(s32[5]{0:T(128)S(1)} %stack.19._.scalars, bf16[128,512]{1,0:T(8,128)(2,1)S(1)} %bitcast.25, bf16[128,512]{1,0:T(8,128)(2,1)S(1)} %collective-permute-done.other, bf16[512,2048]{1,0:T(8,128)(2,1)S(1)} %bitcast.22), custom_call_target="tpu_custom_call" | custom-call | flops 536870912 | bytes 4194304 | tf_op jit(solution)/shard_map/pallas_call | solution.py:30
  37.6 0.0 copy-start.4
  37.6 7.4 %all-to-all-start.1 = ((s16[16,16,2176]{2,1,0:T(8,128)(2,1)}), s16[16,16,2176]{2,1,0:T(8,128)(2,1)S(1)}, u32[]{:S(2)}, u32[]{:S(2)}) async-start(s16[16,16,2176]{2,1,0:T(8,128)(2,1)} %bitcast.10), calls=%async_computation.1 | async-start | bytes 2228224 | tf_op jit(solution)/shard_map/all_to_all | solution.py:265
  45.0 0.0 copy-done.4
  45.1 0.1 copy.14.label
  45.1 16.4 %all-to-all-done.1.got = s16[16,16,2176]{2,1,0:T(8,128)(2,1)S(1)} async-done(((s16[16,16,2176]{2,1,0:T(8,128)(2,1)}), s16[16,16,2176]{2,1,0:T(8,128)(2,1)S(1)}, u32[]{:S(2)}, u32[]{:S(2)}) %all-to-all-start.1) | async-done | bytes 1114144 | tf_op jit(solution)/shard_map/all_to_all | solution.py:265
  61.5 1.1 shard_map.68
  62.6 0.0 copy-start.1
  62.6 1.0 copy-done.1
  63.6 6.1 %all-to-all-start.2 = ((bf16[16,16,2176]{2,1,0:T(8,128)(2,1)}), bf16[16,16,2176]{2,1,0:T(8,128)(2,1)S(1)}, u32[]{:S(2)}, u32[]{:S(2)}) async-start(bf16[16,16,2176]{2,1,0:T(8,128)(2,1)} %copy-done.1), calls=%async_computation.2 | async-start | bytes 2228224 | tf_op jit(solution)/shard_map/all_to_all | solution.py:265
  69.6 0.1 copy.15.label
  69.8 14.6 %all-to-all-done.2 = bf16[16,16,2176]{2,1,0:T(8,128)(2,1)S(1)} async-done(((bf16[16,16,2176]{2,1,0:T(8,128)(2,1)}), bf16[16,16,2176]{2,1,0:T(8,128)(2,1)S(1)}, u32[]{:S(2)}, u32[]{:S(2)}) %all-to-all-start.2) | async-done | bytes 1114144 | tf_op jit(solution)/shard_map/all_to_all | solution.py:265
  84.3 0.0 copy-done
  84.3 0.0 copy-start.2
  84.3 0.9 copy-done.2
  85.3 0.0 copy-start.3
  85.3 1.3 %shard_map.69 = (bf16[144,1024]{1,0:T(8,128)(2,1)S(1)}, f32[128,512]{1,0:T(8,128)S(1)}, f32[8,256]{1,0:T(8,128)S(1)}) custom-call(s32[5]{0:T(128)S(1)} %stack.19._.scalars, bf16[256,2176]{1,0:T(8,128)(2,1)S(1)} %bitcast.20, bf16[2048,512]{1,0:T(8,128)(2,1)S(1)} %copy-done, bf16[256,512]{1,0:T(8,128)(2,1)S(1)} %copy-done.2, s32[256,1]{1,0:T(8,128)S(1)} %copy.15.label), custom_call_target="tpu_custom_call" | custom-call | flops 536870912 | bytes 4194304 | tf_op jit(solution)/shard_map/pallas_call | solution.py:30
  86.6 1.9 %collective-permute-start.1 = (bf16[144,1024]{1,0:T(8,128)(2,1)S(1)}, bf16[144,1024]{1,0:T(8,128)(2,1)S(1)}, u32[]{:S(2)}, u32[]{:S(2)}) collective-permute-start(bf16[144,1024]{1,0:T(8,128)(2,1)S(1)} %get-tuple-element.28), channel_id=1, source_target_pairs={{0,16},{16,0},{32,48},{48,32},{64,80},{80,64},{96,112},{112,96},{1... | collective-permute-start | bytes 884744 | tf_op jit(solution)/shard_map/ppermute | solution.py:315
  88.5 1.5 %collective-permute-done.1.got = bf16[144,1024]{1,0:T(8,128)(2,1)S(1)} collective-permute-done((bf16[144,1024]{1,0:T(8,128)(2,1)S(1)}, bf16[144,1024]{1,0:T(8,128)(2,1)S(1)}, u32[]{:S(2)}, u32[]{:S(2)}) %collective-permute-start.1) | collective-permute-done | bytes 294944 | tf_op jit(solution)/shard_map/ppermute | solution.py:315
  90.0 0.0 copy-done.3
  90.0 1.6 %shard_map.70 = bf16[16,16,640]{2,1,0:T(8,128)(2,1)} custom-call(s32[5]{0:T(128)S(1)} %stack.19._.scalars, f32[128,512]{1,0:T(8,128)S(1)} %get-tuple-element.26.part, bf16[256,512]{1,0:T(8,128)(2,1)S(1)} %copy-done.3, f32[8,256]{1,0:T(8,128)S(1)} %get-tuple-element.27.stat, bf16[144,1024]{1,0:T(8,128)(2,1)S(1)} %collective-permute-done.1.got, ...), custom_call_target="tpu_custom_call" | custom-call | bytes 4194304 | tf_op jit(solution)/shard_map/pallas_call | solution.py:30
  91.6 5.7 %all-to-all-start.3 = ((bf16[16,16,640]{2,1,0:T(8,128)(2,1)}), bf16[16,16,640]{2,1,0:T(8,128)(2,1)S(1)}, u32[]{:S(2)}, u32[]{:S(2)}) async-start(bf16[16,16,640]{2,1,0:T(8,128)(2,1)} %shard_map.70), calls=%async_computation.3 | async-start | bytes 655360 | tf_op jit(solution)/shard_map/all_to_all | solution.py:262
  97.3 0.1 copy.18.own_label
  97.4 0.1 copy.19.own_grad
  97.5 0.1 slice.28
  97.6 0.5 copy.20
  98.1 20.6 %all-to-all-done.3.got = bf16[16,16,640]{2,1,0:T(8,128)(2,1)S(1)} async-done(((bf16[16,16,640]{2,1,0:T(8,128)(2,1)}), bf16[16,16,640]{2,1,0:T(8,128)(2,1)S(1)}, u32[]{:S(2)}, u32[]{:S(2)}) %all-to-all-start.3) | async-done | bytes 327712 | tf_op jit(solution)/shard_map/all_to_all | solution.py:262
  118.7 0.0 copy-done.5
  118.7 2.9 %shard_map.71 = (f32[1,16]{1,0:T(1,128)}, bf16[8,512]{1,0:T(8,128)(2,1)}, bf16[2048,512]{1,0:T(8,128)(2,1)}) custom-call(s32[5]{0:T(128)S(1)} %stack.19._.scalars, bf16[16,16,640]{2,1,0:T(8,128)(2,1)S(1)} %all-to-all-done.3.got, bf16[2048,256]{1,0:T(8,128)(2,1)S(1)} %bitcast.23, f32[8,256]{1,0:T(8,128)S(1)} %get-tuple-element.27.stat, ...), custom_call_target="tpu_custom_call" | custom-call | flops 536870912 | bytes 4194304 | tf_op jit(solution)/shard_map/pallas_call | solution.py:30
  (9 shorter events, 0.1 us)
Async XLA Ops:
  2.0 29.9 %all-to-all-start = ((bf16[16,8,512]{2,1,0:T(8,128)(2,1)}), bf16[16,8,512]{2,1,0:T(8,128)(2,1)S(1)}, u32[]{:S(2)}, u32[]{:S(2)}) async-start(bf16[16,8,512]{2,1,0:T(8,128)(2,1)} %broadcast_in_dim.26), calls=%async_computation | async-start | bytes 262144 | tf_op jit(solution)/shard_map/all_to_all | solution.py:262
  31.9 3.2 %collective-permute-start = (bf16[128,512]{1,0:T(8,128)(2,1)S(1)}, bf16[128,512]{1,0:T(8,128)(2,1)S(1)}, u32[]{:S(2)}, u32[]{:S(2)}) collective-permute-start(bf16[128,512]{1,0:T(8,128)(2,1)S(1)} %bitcast.24), channel_id=1, source_target_pairs={{0,16},{16,0},{32,48},{48,32},{64,80},{80,64},{96,112},{112,96},{1... | collective-permute-start | bytes 393224 | tf_op jit(solution)/shard_map/ppermute | solution.py:287
  37.6 7.4 %copy-start.4 = (bf16[256,512]{1,0:T(8,128)(2,1)}, bf16[256,512]{1,0:T(8,128)(2,1)S(1)}, u32[]{:S(2)}) copy-start(bf16[256,512]{1,0:T(8,128)(2,1)S(1)} %get-tuple-element.29.whole) | copy-start | bytes 786436
  37.6 23.9 %all-to-all-start.1 = ((s16[16,16,2176]{2,1,0:T(8,128)(2,1)}), s16[16,16,2176]{2,1,0:T(8,128)(2,1)S(1)}, u32[]{:S(2)}, u32[]{:S(2)}) async-start(s16[16,16,2176]{2,1,0:T(8,128)(2,1)} %bitcast.10), calls=%async_computation.1 | async-start | bytes 2228224 | tf_op jit(solution)/shard_map/all_to_all | solution.py:265
  45.1 39.2 %copy-start = (bf16[2048,512]{1,0:T(8,128)(2,1)S(1)}, bf16[2048,512]{1,0:T(8,128)(2,1)}, u32[]{:S(2)}) copy-start(bf16[2048,512]{1,0:T(8,128)(2,1)} %weight.1) | copy-start | bytes 6291460
  62.6 1.0 copy-start.1
  63.6 20.8 %all-to-all-start.2 = ((bf16[16,16,2176]{2,1,0:T(8,128)(2,1)}), bf16[16,16,2176]{2,1,0:T(8,128)(2,1)S(1)}, u32[]{:S(2)}, u32[]{:S(2)}) async-start(bf16[16,16,2176]{2,1,0:T(8,128)(2,1)} %copy-done.1), calls=%async_computation.2 | async-start | bytes 2228224 | tf_op jit(solution)/shard_map/all_to_all | solution.py:265
  84.3 1.0 copy-start.2
  85.3 4.7 %copy-start.3 = (bf16[256,512]{1,0:T(8,128)(2,1)S(1)}, bf16[256,512]{1,0:T(8,128)(2,1)}, u32[]{:S(2)}) copy-start(bf16[256,512]{1,0:T(8,128)(2,1)} %fusion.2.row) | copy-start | bytes 786436
  86.6 3.5 %collective-permute-start.1 = (bf16[144,1024]{1,0:T(8,128)(2,1)S(1)}, bf16[144,1024]{1,0:T(8,128)(2,1)S(1)}, u32[]{:S(2)}, u32[]{:S(2)}) collective-permute-start(bf16[144,1024]{1,0:T(8,128)(2,1)S(1)} %get-tuple-element.28), channel_id=1, source_target_pairs={{0,16},{16,0},{32,48},{48,32},{64,80},{80,64},{96,112},{112,96},{1... | collective-permute-start | bytes 884744 | tf_op jit(solution)/shard_map/ppermute | solution.py:315
  91.6 27.1 %all-to-all-start.3 = ((bf16[16,16,640]{2,1,0:T(8,128)(2,1)}), bf16[16,16,640]{2,1,0:T(8,128)(2,1)S(1)}, u32[]{:S(2)}, u32[]{:S(2)}) async-start(bf16[16,16,640]{2,1,0:T(8,128)(2,1)} %shard_map.70), calls=%async_computation.3 | async-start | bytes 655360 | tf_op jit(solution)/shard_map/all_to_all | solution.py:262
  97.5 21.2 %copy-start.5 = (bf16[256,512]{1,0:T(8,128)(2,1)S(1)}, bf16[256,512]{1,0:T(8,128)(2,1)}, u32[]{:S(2)}) copy-start(bf16[256,512]{1,0:T(8,128)(2,1)} %copy-done.4) | copy-start | bytes 786436

commit v4 on v3

v4 whole, which is shorter than its diff:
```python
import functools

import jax
import jax.numpy as jnp
from jax import lax
from jax.experimental import pallas as pl
from jax.experimental.pallas import tpu as pltpu
from jax.sharding import PartitionSpec as P

F32 = jnp.float32
BF16 = jnp.bfloat16
I16 = jnp.int16
I32 = jnp.int32
LANES = 128
CHUNK = 256
SPACE = 32
STEPS = 32760.0
GRAIN = 64.0
MIB = 1 << 20

SCALARS = pl.BlockSpec(memory_space=pltpu.SMEM)
WHOLE = pl.BlockSpec(memory_space=pltpu.VMEM)


def call(kernel, scalars, args, outs, scratch=(), copies=0, flops=0):
    out_specs = [WHOLE] * len(outs)
    scratch_shapes = [pltpu.VMEM(s, d) for s, d in scratch]
    if copies:
        out_specs[-1] = pl.BlockSpec(memory_space=pl.ANY)
        scratch_shapes.append(pltpu.SemaphoreType.DMA((copies,)))
    return pl.pallas_call(
        kernel,
        out_shape=[jax.ShapeDtypeStruct(s, d) for s, d in outs],
        in_specs=[SCALARS] * len(scalars) + [WHOLE] * len(args),
        out_specs=out_specs,
        scratch_shapes=scratch_shapes,
        compiler_params=pltpu.CompilerParams(vmem_limit_bytes=16 * MIB),
        cost_estimate=pl.CostEstimate(flops=flops, bytes_accessed=4 * MIB, transcendentals=0),
    )(*scalars, *args)


def high_part(x):
    return x.astype(BF16).astype(F32)


def split3(x):
    a = high_part(x)
    b = high_part(x - a)
    return a, b, x - a - b


def lane_block(rows, values):
    lane = lax.broadcasted_iota(I32, (rows, LANES), 1)
    block = jnp.zeros((rows, LANES), F32)
    for k, value in enumerate(values):
        block = jnp.where(lane == k, value, block)
    return block


def join3(block, k):
    return block[k : k + 1] + block[k + 1 : k + 2] + block[k + 2 : k + 3]


def logits_kernel(mine, other, weight, out, whole, part):
    half = mine.shape[0]
    voc = weight.shape[1]
    whole[:half, :] = mine[...]
    whole[half:, :] = other[...]
    top = jnp.zeros((2 * half, LANES), F32)
    for k in range(0, voc, CHUNK):
        block = jnp.dot(whole[...], weight[:, k : k + CHUNK], preferred_element_type=F32)
        part[:, k : k + CHUNK] = block
        size = jnp.abs(block)
        for c in range(0, CHUNK, LANES):
            top = jnp.maximum(top, size[:, c : c + LANES])
    top = jnp.max(top, axis=1, keepdims=True)
    grade = jnp.ceil(jnp.log2(jnp.maximum(top, 1e-30)) * GRAIN)
    per = STEPS * jnp.exp2(grade * (-1.0 / GRAIN))
    for k in range(0, voc, CHUNK):
        out[:, k : k + CHUNK] = jnp.round(part[:, k : k + CHUNK] * per).astype(I32).astype(I16)
    out[:, voc:] = jnp.broadcast_to(grade, (2 * half, LANES)).astype(I32).astype(I16)


def softmax_kernel(scalars, labels, got, out, logits):
    n, share, width = got.shape
    section, core, j, mine_n = scalars[0], scalars[2], scalars[3], scalars[5]
    voc = width - LANES
    scales = [
        jnp.exp2(got[i, :, voc:].astype(I32).astype(F32)[:, :1] * (1.0 / GRAIN)) * (1.0 / STEPS)
        for i in range(n)
    ]
    top = jnp.full((share, LANES), -jnp.inf, F32)
    for k in range(0, voc, CHUNK):
        block = jnp.zeros((share, CHUNK), F32)
        for i in range(n):
            block += got[i, :, k : k + CHUNK].astype(I32).astype(F32) * scales[i]
        logits[:, k : k + CHUNK] = block
        for c in range(0, CHUNK, LANES):
            top = jnp.maximum(top, block[:, c : c + LANES])
    top = jnp.max(top, axis=1, keepdims=True)
    total = jnp.zeros((share, CHUNK), F32)
    target = jnp.zeros((share, CHUNK), F32)
    sublane = lax.broadcasted_iota(I32, (share, 1), 0)
    place = jnp.zeros((share, 1), I32)
    for r in range(share):
        index = j * share + r
        side = index // (n * share // 2)
        index = index - side * (n * share // 2)
        first = core + side - 2 * core * side
        token = 2 * mine_n * (index // mine_n) + first * mine_n + index % mine_n
        place = jnp.where(sublane == r, labels[token], place)
    place = place - section * voc
    lane = lax.broadcasted_iota(I32, (share, CHUNK), 1)
    for k in range(0, voc, CHUNK):
        block = logits[:, k : k + CHUNK]
        expo = jnp.exp(block - top)
        total += expo
        hot = lane + k == place
        target += jnp.where(hot, block, 0.0)
        logits[:, k : k + CHUNK] = jnp.where(hot, 0.0, expo)
    total = jnp.sum(total, axis=1, keepdims=True)
    target = jnp.sum(target, axis=1, keepdims=True)
    inverse = 1.0 / total
    for k in range(0, voc, CHUNK):
        soft = (logits[:, k : k + CHUNK] * inverse).astype(BF16)
        for i in range(n):
            out[i, :, k : k + CHUNK] = soft
    stats = lane_block(share, split3(top + jnp.log(total)) + split3(target)).astype(BF16)
    for i in range(n):
        out[i, :, voc:] = stats


def partial_kernel(got, weight, send, part, stat):
    voc, feat = weight.shape
    half = got.shape[0] // 2
    stats = got[:, voc:].astype(F32).T[:8]
    send[half:, :LANES] = jnp.concatenate([stats[:, :half], stats[:, half:]], axis=0).astype(BF16)
    stat[...] = jnp.concatenate([join3(stats, 0), join3(stats, 3), stats[:6]], axis=0)
    rest = jnp.dot(got[half:, :voc], weight[...], preferred_element_type=F32)
    high = rest.astype(BF16)
    send[:half, :feat] = high
    send[:half, feat:] = (rest - high.astype(F32)).astype(BF16)
    part[...] = jnp.dot(got[:half, :voc], weight[...], preferred_element_type=F32)


def pair_kernel(scalars, part, stat, got, out):
    half, feat = part.shape
    core, j = scalars[2], scalars[3]
    n_z, mine_n, _ = out.shape
    theirs = got[half:, :LANES].astype(F32)
    own_log, own_target = stat[0:1, :], stat[1:2, :]
    other_log = jnp.concatenate([join3(theirs, 8), join3(theirs, 0)], axis=1)
    other_target = jnp.concatenate([join3(theirs, 11), join3(theirs, 3)], axis=1)
    first = jnp.where(core == 0, own_log, other_log)
    second = jnp.where(core == 0, other_log, own_log)
    top = jnp.maximum(first, second)
    pair_log = top + jnp.log(jnp.exp(first - top) + jnp.exp(second - top))
    shares = jnp.concatenate(
        [jnp.exp(own_log - pair_log)[:, :half], jnp.exp(other_log - pair_log)[:, :half]], axis=0
    )
    shares = jnp.concatenate([shares] * (half // 2), axis=0).T
    total = (
        part[...] * shares[:, 0:1]
        + (got[:half, :feat].astype(F32) + got[:half, feat:].astype(F32)) * shares[:, 1:2]
    )
    logs = split3(pair_log)
    logs = [x[:, h * half : (h + 1) * half] for h in range(2) for x in logs]
    targets = jnp.concatenate(split3(own_target + other_target), axis=0)
    targets = jnp.concatenate([targets] * 3, axis=0)[:8]
    mine, other = targets[:, :half], targets[:, half:]
    lane = lax.broadcasted_iota(I32, (1, half), 1)
    base = jnp.zeros((1, half), F32)
    for k in range(3):
        for n, x in enumerate((mine, other)):
            at = SPACE * k + (n + 1) * mine_n
            moved = pltpu.roll(x, (half + at - mine_n * j) % half, 1)[k : k + 1]
            base = jnp.where((lane >= at) & (lane < at + mine_n), moved, base)
    for i in range(n_z):
        row = base
        for k in range(3):
            at = SPACE * k
            moved = pltpu.roll(mine, (half + at - mine_n * i) % half, 1)[k : k + 1]
            row = jnp.where((lane >= at) & (lane < at + mine_n), moved, row)
        out[i, :, :feat] = total[i * mine_n : (i + 1) * mine_n].astype(BF16)
        out[i, :, feat:] = jnp.concatenate(logs + [row, row], axis=0).astype(BF16)


def tail_kernel(
    scalars,
    loss_grad,
    got,
    soft,
    stat,
    whole,
    label,
    grad,
    label_row,
    loss,
    hidden,
    weight,
    staged,
    sems,
):
    n_z, mine_n, width = got.shape
    feat = width - LANES
    tokens = whole.shape[0]
    half = tokens // 2
    section, z, core = scalars[0], scalars[1], scalars[2]
    j, voc = scalars[3], scalars[4]
    pieces = [got[:, k, feat:].astype(F32) for k in range(7)]
    logs = jnp.concatenate(
        [pieces[0] + pieces[1] + pieces[2], pieces[3] + pieces[4] + pieces[5]], axis=1
    )
    top = jnp.max(logs, axis=0, keepdims=True)
    log_total = top + jnp.log(jnp.sum(jnp.exp(logs - top), axis=0, keepdims=True))

    scale = grad[...] * jnp.exp(stat[0:1, :] - log_total)
    label_grad = grad[...] * (jnp.exp(stat[1:2, :] - log_total) - 1.0)
    place = label[...] - section * voc
    line = lax.broadcasted_iota(I32, (CHUNK, tokens), 0)
    copies = []
    for n, k in enumerate(range(0, weight.shape[0], CHUNK)):
        value = soft[k : k + CHUNK, :].astype(F32) * scale
        value = jnp.where(line + k == place, label_grad, value).astype(BF16)
        staged[k : k + CHUNK, :] = jnp.dot(
            value, whole[...], preferred_element_type=F32
        ).astype(BF16)
        at = pl.ds(k, CHUNK)
        copies.append(pltpu.make_async_copy(staged.at[at], weight.at[at], sems.at[n]))
        copies[-1].start()

    target = (
        pieces[6]
        + pltpu.roll(pieces[6], half - SPACE, 1)
        + pltpu.roll(pieces[6], half - 2 * SPACE, 1)
    )
    target = jnp.broadcast_to(jnp.sum(target, axis=0, keepdims=True), (8, half))
    lane = lax.broadcasted_iota(I32, (8, half), 1)
    mine, other = (
        jnp.broadcast_to(x, (8, half)) for x in (log_total[:, :half], log_total[:, half:])
    )
    first = pltpu.roll(mine, (half - mine_n * j) % half, 1) - pltpu.roll(target, half - mine_n, 1)
    second = pltpu.roll(other, (half - mine_n * j) % half, 1) - pltpu.roll(
        target, half - 2 * mine_n, 1
    )
    low = jnp.where(core == 0, first, second)
    high = pltpu.roll(jnp.where(core == 0, second, first), mine_n, 1)
    loss[...] = jnp.where(lane < mine_n, low, high)[:1, : loss.shape[1]]

    back = (half - mine_n * z) % half
    shares = pltpu.roll(jnp.exp(logs[:, :half] - log_total[:, :half]), back, 1)
    label_part = jnp.exp(target - pltpu.roll(mine, back, 1)) - 1.0
    block = [shares] + [label_part] * ((half - n_z) // 8)
    block = jnp.concatenate(block, axis=0).T[:mine_n]
    sublane = lax.broadcasted_iota(I32, (mine_n, 1), 0)
    own_grad = jnp.zeros((mine_n, 1), F32)
    for r in range(mine_n):
        own_grad = jnp.where(sublane == r, loss_grad[section * mine_n + r], own_grad)
    total = label_row[...].astype(F32) * block[:, n_z : n_z + 1]
    for i in range(n_z):
        total += got[i, :, :feat].astype(F32) * block[:, i : i + 1]
    hidden[...] = (own_grad * total).astype(BF16)
    for copy in copies:
        copy.wait()


def local(hidden, head_weight, labels, loss_grad):
    voc, feat = head_weight.shape
    mine_n = hidden.shape[0]
    n_dp = lax.axis_size("dp")
    n_sec = lax.axis_size("section")
    n_z = n_sec // 2
    half = n_z * mine_n
    tokens = 2 * half
    share = tokens // n_dp
    section = lax.axis_index("section")
    z, core = section // 2, section % 2
    j = lax.axis_index("dp")
    scalars = jnp.stack([section, z, core, j, jnp.int32(voc), jnp.int32(mine_n)]).astype(I32)
    along_z = [[2 * k + c for k in range(n_z)] for c in range(2)]
    swap = [(i, i ^ 1) for i in range(n_sec)]
    flops = 2 * tokens * voc * feat

    def exchange_z(x):
        return lax.all_to_all(x, "section", 0, 0, tiled=True, axis_index_groups=along_z)

    def exchange_dp(x):
        return lax.all_to_all(x, "dp", 0, 0, tiled=True)

    def own_core_first(x):
        x = x.reshape(n_z, 2, mine_n)
        first = jnp.where(core == 0, x[:, 0], x[:, 1])
        second = jnp.where(core == 0, x[:, 1], x[:, 0])
        return jnp.concatenate([first.reshape(half), second.reshape(half)])

    label = own_core_first(labels)
    grad = own_core_first(loss_grad)
    columns = section * voc + jnp.arange(voc, dtype=I32)

    mine = exchange_z(jnp.broadcast_to(hidden[None], (n_z, mine_n, feat))).reshape(half, feat)
    hot = labels[:, None] == columns[None, :]
    rows = jnp.dot(hot.astype(BF16), head_weight, preferred_element_type=F32).astype(BF16)
    ready = (mine, rows, head_weight.T, label, grad)
    mine, rows, tall, label, grad = lax.optimization_barrier(ready)
    label_row = lax.psum_scatter(rows, "section", scatter_dimension=0, tiled=True)
    other = lax.ppermute(mine, "section", swap)

    width = voc + LANES
    coded, whole = call(
        logits_kernel,
        [],
        [mine, other, tall],
        [((tokens, width), I16), ((tokens, feat), BF16)],
        scratch=[((tokens, voc), F32)],
        flops=flops,
    )
    coded = exchange_dp(coded.reshape(n_dp, share, width))
    (message,) = call(
        softmax_kernel,
        [scalars, labels],
        [coded],
        [((n_dp, share, width), BF16)],
        scratch=[((share, voc), F32)],
    )
    got = exchange_dp(message).reshape(tokens, width)

    send, part, stat = call(
        partial_kernel,
        [],
        [got, head_weight],
        [((half + 16, 2 * feat), BF16), ((half, feat), F32), ((8, tokens), F32)],
        flops=flops,
    )
    theirs = lax.ppermute(send, "section", swap)
    (message,) = call(
        pair_kernel,
        [scalars],
        [part, stat, theirs],
        [((n_z, mine_n, feat + LANES), BF16)],
    )
    last = exchange_z(message)
    soft = got[:, :voc].T
    loss, grad_hidden, grad_weight = call(
        tail_kernel,
        [scalars, loss_grad],
        [last, soft, stat, whole, label[None], grad[None], label_row],
        [((1, share), F32), ((mine_n, feat), BF16), ((voc, feat), BF16)],
        scratch=[((voc, feat), BF16)],
        copies=voc // CHUNK,
        flops=flops,
    )
    return (loss.reshape(share), grad_hidden, grad_weight)


def solution(mesh):
    return jax.shard_map(
        local,
        mesh=mesh,
        in_specs=(P("section", "dp"), P("section", "dp"), P(), P()),
        out_specs=(P("dp"), P("section", "dp"), P("section", "dp")),
        check_vma=False,
    )
```

time: 123 us -> 222 us (1.80)
  waiting for transfers between devices: 60.6 us -> 133 us
  blocking collectives: 0 us -> 20.5 us
  between operations: 0.84 us -> 14.2 us
  starting transfers between devices: 38.2 us -> 31.4 us
  local copies, waits for them, and re-layouts: 9.54 us -> 13.3 us
    reduce_scatter x0 -> x1, waiting for transfers between devices: none -> 106 us  [local(): lax.psum_scatter(rows, 'section', scatter_dimension=0, tiled=True)]
    all_to_all x0 -> x1, blocking collectives: none -> 20.5 us  [exchange_dp(): return lax.all_to_all(x, 'dp', 0, 0, tiled=True)]
    all_to_all x2, waiting for transfers between devices: 26.9 us -> 7.05 us  [exchange_z(): lax.all_to_all(x, 'section', 0, 0, tiled=True, axis_index_groups=along_z)]
    all_to_all x2 -> x1, waiting for transfers between devices: 30.9 us -> 16.4 us  [exchange_dp(): return lax.all_to_all(x, 'dp', 0, 0, tiled=True)]
    all_to_all x2 -> x1, starting transfers between devices: 13.5 us -> 7.43 us  [exchange_dp(): return lax.all_to_all(x, 'dp', 0, 0, tiled=True)]
    unnamed x16 -> x14, local copies, waits for them, and re-layouts: 5.43 us -> 8.83 us
  transfers between devices with their start and end apart: 6 -> 6, of which waited for: 6 -> 5; matrix products, arithmetic and copies ran while one was open for 8% -> 5% of each run, Pallas kernels for 0% -> 0%
where the time goes in v4:
time: 222 us
  waiting for transfers between devices  133 us (60%)
  starting transfers between devices  31.4 us (14%)
  blocking collectives  20.5 us (9%)
  between operations  14.2 us (6%)
  local copies, waits for them, and re-layouts  13.3 us (6%)
  Pallas kernels  7.17 us (3%)
    reduce_scatter x1, waiting for transfers between devices, local(): lax.psum_scatter(rows, 'section', scatter_dimension=0, tiled=True)  106 us
    all_to_all x1, blocking collectives, exchange_dp(): return lax.all_to_all(x, 'dp', 0, 0, tiled=True)  20.5 us
    all_to_all x2, starting transfers between devices, exchange_z(): lax.all_to_all(x, 'section', 0, 0, tiled=True, axis_index_groups=along_z)  20.1 us
    all_to_all x1, waiting for transfers between devices, exchange_dp(): return lax.all_to_all(x, 'dp', 0, 0, tiled=True)  16.4 us
    unnamed x14, local copies, waits for them, and re-layouts  8.83 us
    all_to_all x1, starting transfers between devices, exchange_dp(): return lax.all_to_all(x, 'dp', 0, 0, tiled=True)  7.43 us
    pallas_call x5, Pallas kernels, call(): pl.pallas_call(kernel, out_shape=[jax.ShapeDtypeStruct(s, d) for s, d in...  7.17 us
    all_to_all x2, waiting for transfers between devices, exchange_z(): lax.all_to_all(x, 'section', 0, 0, tiled=True, axis_index_groups=along_z)  7.05 us
  transfers between devices with their start and end apart: 6, of which 5 were waited for; matrix products, arithmetic and copies ran while one was open for 5% of the time, Pallas kernels for 0%

profile of v4, /device:TPU:6, one launch (start us, length us, event | category | flops | bytes accessed | tf_op | source)
XLA Modules:
  0.0 221.5 jit_solution(14273802762346766003)
XLA Ops:
  7.2 1.4 broadcast_in_dim.6
  8.5 15.2 %all-to-all-start = ((bf16[16,8,512]{2,1,0:T(8,128)(2,1)}), bf16[16,8,512]{2,1,0:T(8,128)(2,1)S(1)}, u32[]{:S(2)}, u32[]{:S(2)}) async-start(bf16[16,8,512]{2,1,0:T(8,128)(2,1)} %broadcast_in_dim.6), calls=%async_computation | async-start | bytes 262144 | tf_op jit(solution)/shard_map/all_to_all | solution.py:285
  23.7 0.8 reshape.52
  24.5 0.1 fusion.9
  24.6 0.1 select_n.57
  24.7 0.1 select_n.59
  24.8 0.8 reshape.51
  25.5 0.1 fusion.7
  25.6 0.1 select_n.53
  25.7 0.1 select_n.55
  25.8 0.0 copy-start
  25.8 0.0 copy-start.3
  25.8 4.1 %copy.10 = bf16[2048,512]{0,1:T(8,128)(2,1)} copy(bf16[2048,512]{1,0:T(8,128)(2,1)} %weight.1) | data formatting | bytes 4194304 | tf_op args[1]
  29.9 0.0 copy-done
  29.9 0.0 copy-done.3
  29.9 1.5 fusion.2
  31.4 7.1 %all-to-all-done = bf16[16,8,512]{2,1,0:T(8,128)(2,1)S(1)} async-done(((bf16[16,8,512]{2,1,0:T(8,128)(2,1)}), bf16[16,8,512]{2,1,0:T(8,128)(2,1)S(1)}, u32[]{:S(2)}, u32[]{:S(2)}) %all-to-all-start) | async-done | bytes 131104 | tf_op jit(solution)/shard_map/all_to_all | solution.py:285
  38.4 1.9 collective-permute-start
  40.3 1.3 collective-permute-done.other
  41.7 0.0 copy-start.1
  41.7 1.6 copy-done.1
  43.2 1.0 shard_map.67
  44.2 0.0 copy-start.2
  44.2 1.0 copy-done.2
  45.2 7.4 %all-to-all-start.1 = ((s16[16,16,2176]{2,1,0:T(8,128)(2,1)}), s16[16,16,2176]{2,1,0:T(8,128)(2,1)S(1)}, u32[]{:S(2)}, u32[]{:S(2)}) async-start(s16[16,16,2176]{2,1,0:T(8,128)(2,1)} %bitcast.16), calls=%async_computation.1 | async-start | bytes 2228224 | tf_op jit(solution)/shard_map/all_to_all | solution.py:288
  52.6 0.1 stack.19.scalars
  52.7 16.4 %all-to-all-done.1.got = s16[16,16,2176]{2,1,0:T(8,128)(2,1)S(1)} async-done(((s16[16,16,2176]{2,1,0:T(8,128)(2,1)}), s16[16,16,2176]{2,1,0:T(8,128)(2,1)S(1)}, u32[]{:S(2)}, u32[]{:S(2)}) %all-to-all-start.1) | async-done | bytes 1114144 | tf_op jit(solution)/shard_map/all_to_all | solution.py:288
  69.1 1.2 shard_map.68
  70.3 20.5 %all_to_all.20 = bf16[16,16,2176]{2,1,0:T(8,128)(2,1)S(1)} all-to-all(bf16[16,16,2176]{2,1,0:T(8,128)(2,1)S(1)} %shard_map.68), channel_id=1, replica_groups=mesh['section'=32,'dp'=16] {'dp'}, dimensions={0} | all-to-all | bytes 2228224 | tf_op jit(solution)/shard_map/all_to_all | solution.py:288
  90.7 0.7 shard_map.69
  91.5 1.9 collective-permute-start.1
  93.4 1.5 collective-permute-done.1.got
  94.9 1.5 shard_map.70
  96.4 5.0 %all-to-all-start.3 = ((bf16[16,8,640]{2,1,0:T(8,128)(2,1)}), bf16[16,8,640]{2,1,0:T(8,128)(2,1)S(1)}, u32[]{:S(2)}, u32[]{:S(2)}) async-start(bf16[16,8,640]{2,1,0:T(8,128)(2,1)} %shard_map.70), calls=%async_computation.3 | async-start | bytes 327680 | tf_op jit(solution)/shard_map/all_to_all | solution.py:285
  101.4 0.0 reduce-scatter.2.cloned.1.call-start
  101.4 0.7 reduce-scatter.2.cloned.1.call-update
  102.1 0.0 copy-start.4
  102.1 1.1 slice.28
  103.2 1.5 copy.12
  104.7 106.4 %reduce-scatter.2.cloned.1.call-done.label_row = bf16[8,512]{1,0:T(8,128)(2,1)} async-done(((bf16[256,512]{1,0:T(8,128)(2,1)}), bf16[8,512]{1,0:T(8,128)(2,1)}) %reduce-scatter.2.cloned.1.call-update) | async-done | bytes 8208 | tf_op jit(solution)/shard_map/reduce_scatter | solution.py:305
  211.1 0.0 all-to-all-done.3.got
  211.1 0.0 copy-done.4
  211.1 0.0 copy-start.5
  211.1 0.7 copy-done.5
  211.8 2.9 %shard_map.71 = (f32[1,16]{1,0:T(1,128)}, bf16[8,512]{1,0:T(8,128)(2,1)}, bf16[2048,512]{1,0:T(8,128)(2,1)}) custom-call(s32[6]{0:T(128)S(1)} %stack.19.scalars, f32[256]{0:T(256)S(1)} %copy-done.4, bf16[16,8,640]{2,1,0:T(8,128)(2,1)S(1)} %all-to-all-done.3.got, bf16[2048,256]{1,0:T(8,128)(2,1)S(1)} %bitcast.17, f32[8,256]{1,0:T(8,128)S(1)} %get-tuple-element.20.stat, ...), custom_call_target="tpu_custom_call" | custom-call | flops 536870912 | bytes 4194304 | tf_op jit(solution)/shard_map/pallas_call | solution.py:31
  (3 shorter events, 0.0 us)
Async XLA Ops:
  8.5 29.9 %all-to-all-start = ((bf16[16,8,512]{2,1,0:T(8,128)(2,1)}), bf16[16,8,512]{2,1,0:T(8,128)(2,1)S(1)}, u32[]{:S(2)}, u32[]{:S(2)}) async-start(bf16[16,8,512]{2,1,0:T(8,128)(2,1)} %broadcast_in_dim.6), calls=%async_computation | async-start | bytes 262144 | tf_op jit(solution)/shard_map/all_to_all | solution.py:285
  25.8 4.1 %copy-start = (bf16[2048,512]{1,0:T(8,128)(2,1)S(1)}, bf16[2048,512]{1,0:T(8,128)(2,1)}, u32[]{:S(2)}) copy-start(bf16[2048,512]{1,0:T(8,128)(2,1)} %weight.1) | copy-start | bytes 6291460
  25.8 4.1 %copy-start.3 = (s32[256]{0:T(256)S(1)}, s32[256]{0:T(256)}, u32[]{:S(2)}) copy-start(s32[256]{0:T(256)} %labels.1) | copy-start | bytes 3076
  38.4 3.2 %collective-permute-start = (bf16[128,512]{1,0:T(8,128)(2,1)S(1)}, bf16[128,512]{1,0:T(8,128)(2,1)S(1)}, u32[]{:S(2)}, u32[]{:S(2)}) collective-permute-start(bf16[128,512]{1,0:T(8,128)(2,1)S(1)} %bitcast.18), channel_id=1, source_target_pairs={{0,16},{16,0},{32,48},{48,32},{64,80},{80,64},{96,112},{112,96},{1... | collective-permute-start | bytes 393224 | tf_op jit(solution)/shard_map/ppermute | solution.py:306
  41.7 1.6 copy-start.1
  44.2 1.0 copy-start.2
  45.2 23.9 %all-to-all-start.1 = ((s16[16,16,2176]{2,1,0:T(8,128)(2,1)}), s16[16,16,2176]{2,1,0:T(8,128)(2,1)S(1)}, u32[]{:S(2)}, u32[]{:S(2)}) async-start(s16[16,16,2176]{2,1,0:T(8,128)(2,1)} %bitcast.16), calls=%async_computation.1 | async-start | bytes 2228224 | tf_op jit(solution)/shard_map/all_to_all | solution.py:288
  91.5 3.5 %collective-permute-start.1 = (bf16[144,1024]{1,0:T(8,128)(2,1)S(1)}, bf16[144,1024]{1,0:T(8,128)(2,1)S(1)}, u32[]{:S(2)}, u32[]{:S(2)}) collective-permute-start(bf16[144,1024]{1,0:T(8,128)(2,1)S(1)} %get-tuple-element.21), channel_id=1, source_target_pairs={{0,16},{16,0},{32,48},{48,32},{64,80},{80,64},{96,112},{112,96},{1... | collective-permute-start | bytes 884744 | tf_op jit(solution)/shard_map/ppermute | solution.py:334
  96.4 114.7 %all-to-all-start.3 = ((bf16[16,8,640]{2,1,0:T(8,128)(2,1)}), bf16[16,8,640]{2,1,0:T(8,128)(2,1)S(1)}, u32[]{:S(2)}, u32[]{:S(2)}) async-start(bf16[16,8,640]{2,1,0:T(8,128)(2,1)} %shard_map.70), calls=%async_computation.3 | async-start | bytes 327680 | tf_op jit(solution)/shard_map/all_to_all | solution.py:285
  101.4 109.8 %reduce-scatter.2.cloned.1.call-start = ((), (), s32[]{:S(2)}) async-start(), calls=%async_computation.5 | async-start | bytes 270336 | tf_op jit(solution)/shard_map/reduce_scatter | solution.py:305
  102.1 109.0 %copy-start.4 = (f32[256]{0:T(256)S(1)}, f32[256]{0:T(256)}, u32[]{:S(2)}) copy-start(f32[256]{0:T(256)} %loss_grad.1) | copy-start | bytes 3076
  211.1 0.7 copy-start.5
Sparse Core Ops, SparseCore 0:
  105.0 106.0 reduce-scatter.1

commit v5 on v4

--- a/solution.py
+++ b/solution.py
@@ -13,6 +13,7 @@
 I32 = jnp.int32
 LANES = 128
 CHUNK = 256
+OWN = 8
 SPACE = 32
 STEPS = 32760.0
 GRAIN = 64.0
@@ -22,21 +23,23 @@
 WHOLE = pl.BlockSpec(memory_space=pltpu.VMEM)
 
 
-def call(kernel, scalars, args, outs, scratch=(), copies=0, flops=0):
+def call(kernel, scalars, args, outs, left=(), scratch=(), copies=0, copies_out=False, flops=0):
+    anywhere = pl.BlockSpec(memory_space=pl.ANY)
     out_specs = [WHOLE] * len(outs)
     scratch_shapes = [pltpu.VMEM(s, d) for s, d in scratch]
+    if copies_out:
+        out_specs[-1] = anywhere
     if copies:
-        out_specs[-1] = pl.BlockSpec(memory_space=pl.ANY)
         scratch_shapes.append(pltpu.SemaphoreType.DMA((copies,)))
     return pl.pallas_call(
         kernel,
         out_shape=[jax.ShapeDtypeStruct(s, d) for s, d in outs],
-        in_specs=[SCALARS] * len(scalars) + [WHOLE] * len(args),
+        in_specs=[SCALARS] * len(scalars) + [WHOLE] * len(args) + [anywhere] * len(left),
         out_specs=out_specs,
         scratch_shapes=scratch_shapes,
         compiler_params=pltpu.CompilerParams(vmem_limit_bytes=16 * MIB),
         cost_estimate=pl.CostEstimate(flops=flops, bytes_accessed=4 * MIB, transcendentals=0),
-    )(*scalars, *args)
+    )(*scalars, *args, *left)
 
 
 def high_part(x):
@@ -130,23 +133,29 @@
         out[i, :, voc:] = stats
 
 
-def partial_kernel(got, weight, send, part, stat):
+def partial_kernel(got, weight, rows, send, part, stat, sems):
     voc, feat = weight.shape
     half = got.shape[0] // 2
+    copy = pltpu.make_async_copy(
+        rows.at[pl.ds(half, half)], send.at[pl.ds(0, half), pl.ds(feat, feat)], sems.at[0]
+    )
+    copy.start()
     stats = got[:, voc:].astype(F32).T[:8]
     send[half:, :LANES] = jnp.concatenate([stats[:, :half], stats[:, half:]], axis=0).astype(BF16)
     stat[...] = jnp.concatenate([join3(stats, 0), join3(stats, 3), stats[:6]], axis=0)
-    rest = jnp.dot(got[half:, :voc], weight[...], preferred_element_type=F32)
-    high = rest.astype(BF16)
-    send[:half, :feat] = high
-    send[:half, feat:] = (rest - high.astype(F32)).astype(BF16)
+    send[:half, :feat] = jnp.dot(
+        got[half:, :voc], weight[...], preferred_element_type=F32
+    ).astype(BF16)
     part[...] = jnp.dot(got[:half, :voc], weight[...], preferred_element_type=F32)
-
-
-def pair_kernel(scalars, part, stat, got, out):
+    copy.wait()
+
+
+def pair_kernel(scalars, part, stat, got, rows, out, own_rows, sems):
     half, feat = part.shape
-    core, j = scalars[2], scalars[3]
-    n_z, mine_n, _ = out.shape
+    core, j, mine_n = scalars[2], scalars[3], OWN
+    n_z = out.shape[0]
+    copy = pltpu.make_async_copy(rows.at[pl.ds(0, half)], own_rows, sems.at[0])
+    copy.start()
     theirs = got[half:, :LANES].astype(F32)
     own_log, own_target = stat[0:1, :], stat[1:2, :]
     other_log = jnp.concatenate([join3(theirs, 8), join3(theirs, 0)], axis=1)
@@ -159,10 +168,7 @@
         [jnp.exp(own_log - pair_log)[:, :half], jnp.exp(other_log - pair_log)[:, :half]], axis=0
     )
     shares = jnp.concatenate([shares] * (half // 2), axis=0).T
-    total = (
-        part[...] * shares[:, 0:1]
-        + (got[:half, :feat].astype(F32) + got[:half, feat:].astype(F32)) * shares[:, 1:2]
-    )
+    total = part[...] * shares[:, 0:1] + got[:half, :feat].astype(F32) * shares[:, 1:2]
     logs = split3(pair_log)
     logs = [x[:, h * half : (h + 1) * half] for h in range(2) for x in logs]
     targets = jnp.concatenate(split3(own_target + other_target), axis=0)
@@ -175,14 +181,21 @@
             at = SPACE * k + (n + 1) * mine_n
             moved = pltpu.roll(x, (half + at - mine_n * j) % half, 1)[k : k + 1]
             base = jnp.where((lane >= at) & (lane < at + mine_n), moved, base)
+    copy.wait()
+    label_rows = own_rows[...].astype(F32) + got[:half, feat:].astype(F32)
     for i in range(n_z):
         row = base
         for k in range(3):
             at = SPACE * k
             moved = pltpu.roll(mine, (half + at - mine_n * i) % half, 1)[k : k + 1]
             row = jnp.where((lane >= at) & (lane < at + mine_n), moved, row)
-        out[i, :, :feat] = total[i * mine_n : (i + 1) * mine_n].astype(BF16)
-        out[i, :, feat:] = jnp.concatenate(logs + [row, row], axis=0).astype(BF16)
+        at = slice(i * mine_n, (i + 1) * mine_n)
+        for n, k in enumerate(range(0, feat, LANES)):
+            here = slice(n * mine_n, (n + 1) * mine_n)
+            out[i, here, :] = total[at, k : k + LANES].astype(BF16)
+            here = slice(here.start + feat // LANES * mine_n, here.stop + feat // LANES * mine_n)
+            out[i, here, :] = label_rows[at, k : k + LANES].astype(BF16)
+        out[i, here.stop :, :] = jnp.concatenate(logs + [row, row], axis=0).astype(BF16)
 
 
 def tail_kernel(
@@ -194,20 +207,19 @@
     whole,
     label,
     grad,
-    label_row,
     loss,
     hidden,
     weight,
     staged,
     sems,
 ):
-    n_z, mine_n, width = got.shape
-    feat = width - LANES
-    tokens = whole.shape[0]
+    n_z, mine_n = got.shape[0], hidden.shape[0]
+    tokens, feat = whole.shape
+    tiles = feat // LANES
     half = tokens // 2
     section, z, core = scalars[0], scalars[1], scalars[2]
     j, voc = scalars[3], scalars[4]
-    pieces = [got[:, k, feat:].astype(F32) for k in range(7)]
+    pieces = [got[:, 2 * tiles * mine_n + k, :].astype(F32) for k in range(7)]
     logs = jnp.concatenate(
         [pieces[0] + pieces[1] + pieces[2], pieces[3] + pieces[4] + pieces[5]], axis=1
     )
@@ -256,10 +268,14 @@
     own_grad = jnp.zeros((mine_n, 1), F32)
     for r in range(mine_n):
         own_grad = jnp.where(sublane == r, loss_grad[section * mine_n + r], own_grad)
-    total = label_row[...].astype(F32) * block[:, n_z : n_z + 1]
-    for i in range(n_z):
-        total += got[i, :, :feat].astype(F32) * block[:, i : i + 1]
-    hidden[...] = (own_grad * total).astype(BF16)
+    for n in range(tiles):
+        part = jnp.zeros((mine_n, LANES), F32)
+        row = jnp.zeros((mine_n, LANES), F32)
+        for i in range(n_z):
+            part += got[i, n * mine_n : (n + 1) * mine_n, :].astype(F32) * block[:, i : i + 1]
+            row += got[i, (tiles + n) * mine_n : (tiles + n + 1) * mine_n, :].astype(F32)
+        part += row * block[:, n_z : n_z + 1]
+        hidden[:, n * LANES : (n + 1) * LANES] = (own_grad * part).astype(BF16)
     for copy in copies:
         copy.wait()
 
@@ -298,11 +314,10 @@
     columns = section * voc + jnp.arange(voc, dtype=I32)
 
     mine = exchange_z(jnp.broadcast_to(hidden[None], (n_z, mine_n, feat))).reshape(half, feat)
-    hot = labels[:, None] == columns[None, :]
+    hot = label[:, None] == columns[None, :]
     rows = jnp.dot(hot.astype(BF16), head_weight, preferred_element_type=F32).astype(BF16)
-    ready = (mine, rows, head_weight.T, label, grad)
-    mine, rows, tall, label, grad = lax.optimization_barrier(ready)
-    label_row = lax.psum_scatter(rows, "section", scatter_dimension=0, tiled=True)
+    ready = (mine, rows, head_weight.T, label[None], grad[None], scalars)
+    mine, rows, tall, label, grad, scalars = lax.optimization_barrier(ready)
     other = lax.ppermute(mine, "section", swap)
 
     width = voc + LANES
@@ -329,6 +344,8 @@
         [],
         [got, head_weight],
         [((half + 16, 2 * feat), BF16), ((half, feat), F32), ((8, tokens), F32)],
+        left=[rows],
+        copies=1,
         flops=flops,
     )
     theirs = lax.ppermute(send, "section", swap)
@@ -336,17 +353,21 @@
         pair_kernel,
         [scalars],
         [part, stat, theirs],
-        [((n_z, mine_n, feat + LANES), BF16)],
+        [((n_z, (2 * feat // LANES + 1) * mine_n, LANES), BF16)],
+        left=[rows],
+        scratch=[((half, feat), BF16)],
+        copies=1,
     )
     last = exchange_z(message)
     soft = got[:, :voc].T
     loss, grad_hidden, grad_weight = call(
         tail_kernel,
         [scalars, loss_grad],
-        [last, soft, stat, whole, label[None], grad[None], label_row],
+        [last, soft, stat, whole, label, grad],
         [((1, share), F32), ((mine_n, feat), BF16), ((voc, feat), BF16)],
         scratch=[((voc, feat), BF16)],
         copies=voc // CHUNK,
+        copies_out=True,
         flops=flops,
     )
     return (loss.reshape(share), grad_hidden, grad_weight)

time: 222 us -> 117 us (0.53)
  waiting for transfers between devices: 133 us -> 29.7 us
  blocking collectives: 20.5 us -> 43.6 us
  between operations: 14.2 us -> 0.84 us
  starting transfers between devices: 31.4 us -> 23.4 us
  local copies, waits for them, and re-layouts: 13.3 us -> 9.68 us
    reduce_scatter x1 -> x0, waiting for transfers between devices: 106 us -> none  [local(): lax.psum_scatter(rows, 'section', scatter_dimension=0, tiled=True)]
    all_to_all x1 -> x2, blocking collectives: 20.5 us -> 43.6 us  [exchange_dp(): return lax.all_to_all(x, 'dp', 0, 0, tiled=True)]
    all_to_all x2, waiting for transfers between devices: 7.05 us -> 26.9 us  [exchange_z(): lax.all_to_all(x, 'section', 0, 0, tiled=True, axis_index_groups=along_z)]
    all_to_all x1 -> x0, waiting for transfers between devices: 16.4 us -> none  [exchange_dp(): return lax.all_to_all(x, 'dp', 0, 0, tiled=True)]
    all_to_all x1 -> x0, starting transfers between devices: 7.43 us -> none  [exchange_dp(): return lax.all_to_all(x, 'dp', 0, 0, tiled=True)]
    unnamed x14 -> x15, local copies, waits for them, and re-layouts: 8.83 us -> 6.22 us
  transfers between devices with their start and end apart: 6 -> 4, of which waited for: 5 -> 4; matrix products, arithmetic and copies ran while one was open for 5% -> 7% of each run, Pallas kernels for 0% -> 0%
where the time goes in v5:
time: 117 us; the launch traced here: 116 us
  blocking collectives  43.6 us (37%)
  waiting for transfers between devices  29.7 us (25%)
  starting transfers between devices  23.4 us (20%)
  local copies, waits for them, and re-layouts  9.68 us (8%)
  Pallas kernels  7.49 us (6%)
    all_to_all x2, blocking collectives, exchange_dp(): return lax.all_to_all(x, 'dp', 0, 0, tiled=True)  43.6 us
    all_to_all x2, waiting for transfers between devices, exchange_z(): lax.all_to_all(x, 'section', 0, 0, tiled=True, axis_index_groups=along_z)  26.9 us
    all_to_all x2, starting transfers between devices, exchange_z(): lax.all_to_all(x, 'section', 0, 0, tiled=True, axis_index_groups=along_z)  19.5 us
    pallas_call x5, Pallas kernels, call(): pl.pallas_call(kernel, out_shape=[jax.ShapeDtypeStruct(s, d) for s, d in...  7.49 us
    unnamed x15, local copies, waits for them, and re-layouts  6.22 us
  transfers between devices with their start and end apart: 4, of which 4 were waited for; matrix products, arithmetic and copies ran while one was open for 7% of the time, Pallas kernels for 0%

profile of v5, /device:TPU:6, one launch (start us, length us, event | category | flops | bytes accessed | tf_op | source)
XLA Modules:
  0.0 115.6 jit_solution(8701971659893542362)
XLA Ops:
  0.6 1.4 %broadcast_in_dim.6 = bf16[16,8,512]{2,1,0:T(8,128)(2,1)} broadcast(bf16[8,512]{1,0:T(8,128)(2,1)} %param.4), dimensions={1,2} | broadcast | bytes 139264 | tf_op jit(solution)/shard_map/broadcast_in_dim | solution.py:316
  2.0 15.2 %all-to-all-start = ((bf16[16,8,512]{2,1,0:T(8,128)(2,1)}), bf16[16,8,512]{2,1,0:T(8,128)(2,1)S(1)}, u32[]{:S(2)}, u32[]{:S(2)}) async-start(bf16[16,8,512]{2,1,0:T(8,128)(2,1)} %broadcast_in_dim.6), calls=%async_computation | async-start | bytes 262144 | tf_op jit(solution)/shard_map/all_to_all | solution.py:301
  17.2 0.8 reshape.51
  18.0 0.1 fusion.8
  18.1 0.1 select_n.54
  18.1 0.1 select_n.52
  18.2 0.8 reshape.52
  19.0 0.1 fusion.9
  19.1 0.1 select_n.56
  19.2 0.1 select_n.58
  19.3 0.0 copy-start
  19.3 4.1 %copy.10 = bf16[2048,512]{0,1:T(8,128)(2,1)} copy(bf16[2048,512]{1,0:T(8,128)(2,1)} %weight.1) | data formatting | bytes 4194304 | tf_op args[1]
  23.4 0.1 stack.19.scalars
  23.5 0.0 copy-done
  23.5 0.7 fusion.2.rows
  24.2 7.6 %all-to-all-done = bf16[16,8,512]{2,1,0:T(8,128)(2,1)S(1)} async-done(((bf16[16,8,512]{2,1,0:T(8,128)(2,1)}), bf16[16,8,512]{2,1,0:T(8,128)(2,1)S(1)}, u32[]{:S(2)}, u32[]{:S(2)}) %all-to-all-start) | async-done | bytes 131104 | tf_op jit(solution)/shard_map/all_to_all | solution.py:301
  31.9 0.0 copy-start.2
  31.9 2.0 %collective-permute-start = (bf16[128,512]{1,0:T(8,128)(2,1)S(1)}, bf16[128,512]{1,0:T(8,128)(2,1)S(1)}, u32[]{:S(2)}, u32[]{:S(2)}) collective-permute-start(bf16[128,512]{1,0:T(8,128)(2,1)S(1)} %bitcast.18), channel_id=1, source_target_pairs={{0,16},{16,0},{32,48},{48,32},{64,80},{80,64},{96,112},{112,96},{1... | collective-permute-start | bytes 393224 | tf_op jit(solution)/shard_map/ppermute | solution.py:321
  33.9 1.3 %collective-permute-done.other = bf16[128,512]{1,0:T(8,128)(2,1)S(1)} collective-permute-done((bf16[128,512]{1,0:T(8,128)(2,1)S(1)}, bf16[128,512]{1,0:T(8,128)(2,1)S(1)}, u32[]{:S(2)}, u32[]{:S(2)}) %collective-permute-start) | collective-permute-done | bytes 131104 | tf_op jit(solution)/shard_map/ppermute | solution.py:321
  35.2 0.0 copy-start.1
  35.2 1.6 %copy-done.1 = bf16[2048,512]{0,1:T(8,128)(2,1)S(1)} copy-done((bf16[2048,512]{0,1:T(8,128)(2,1)S(1)}, bf16[2048,512]{0,1:T(8,128)(2,1)}, u32[]{:S(2)}) %copy-start.1) | copy-done | bytes 2097176
  36.8 1.0 shard_map.67
  37.8 0.0 copy-start.4
  37.8 23.4 %all_to_all.20.got = s16[16,16,2176]{2,1,0:T(8,128)(2,1)S(1)} all-to-all(s16[16,16,2176]{2,1,0:T(8,128)(2,1)S(1)} %bitcast.16), channel_id=1, replica_groups=mesh['section'=32,'dp'=16] {'dp'}, dimensions={0} | all-to-all | bytes 2228224 | tf_op jit(solution)/shard_map/all_to_all | solution.py:304
  61.2 0.0 copy-done.4
  61.2 0.0 copy-done.2
  61.2 1.2 %shard_map.68 = bf16[16,16,2176]{2,1,0:T(8,128)(2,1)S(1)} custom-call(s32[6]{0:T(128)S(1)} %stack.19.scalars, s32[256]{0:T(256)S(1)} %copy-done.2, s16[16,16,2176]{2,1,0:T(8,128)(2,1)S(1)} %all_to_all.20.got), custom_call_target="tpu_custom_call" | custom-call | bytes 4194304 | tf_op jit(solution)/shard_map/pallas_call | solution.py:34
  62.3 20.2 %all_to_all.21 = bf16[16,16,2176]{2,1,0:T(8,128)(2,1)S(1)} all-to-all(bf16[16,16,2176]{2,1,0:T(8,128)(2,1)S(1)} %shard_map.68), channel_id=1, replica_groups=mesh['section'=32,'dp'=16] {'dp'}, dimensions={0} | all-to-all | bytes 2228224 | tf_op jit(solution)/shard_map/all_to_all | solution.py:304
  82.6 0.7 shard_map.69
  83.3 1.9 %collective-permute-start.1 = (bf16[144,1024]{1,0:T(8,128)(2,1)S(1)}, bf16[144,1024]{1,0:T(8,128)(2,1)S(1)}, u32[]{:S(2)}, u32[]{:S(2)}) collective-permute-start(bf16[144,1024]{1,0:T(8,128)(2,1)S(1)} %get-tuple-element.24), channel_id=1, source_target_pairs={{0,16},{16,0},{32,48},{48,32},{64,80},{80,64},{96,112},{112,96},{1... | collective-permute-start | bytes 884744 | tf_op jit(solution)/shard_map/ppermute | solution.py:351
  85.2 1.5 %collective-permute-done.1.got = bf16[144,1024]{1,0:T(8,128)(2,1)S(1)} collective-permute-done((bf16[144,1024]{1,0:T(8,128)(2,1)S(1)}, bf16[144,1024]{1,0:T(8,128)(2,1)S(1)}, u32[]{:S(2)}, u32[]{:S(2)}) %collective-permute-start.1) | collective-permute-done | bytes 294944 | tf_op jit(solution)/shard_map/ppermute | solution.py:351
  86.8 1.8 %shard_map.70 = bf16[16,72,128]{2,1,0:T(8,128)(2,1)} custom-call(s32[6]{0:T(128)S(1)} %stack.19.scalars, f32[128,512]{1,0:T(8,128)S(1)} %get-tuple-element.22.part, f32[8,256]{1,0:T(8,128)S(1)} %get-tuple-element.23.stat, bf16[144,1024]{1,0:T(8,128)(2,1)S(1)} %collective-permute-done.1.got, bf16[256,512]{1,0:T(8,128)(2,1)S(1)} %fusion.2.rows), custom_call_target="tpu_custom_call" | custom-call | bytes 4194304 | tf_op jit(solution)/shard_map/pallas_call | solution.py:34
  88.6 4.3 %all-to-all-start.3 = ((bf16[16,72,128]{2,1,0:T(8,128)(2,1)}), bf16[16,72,128]{2,1,0:T(8,128)(2,1)S(1)}, u32[]{:S(2)}, u32[]{:S(2)}) async-start(bf16[16,72,128]{2,1,0:T(8,128)(2,1)} %shard_map.70), calls=%async_computation.3 | async-start | bytes 589824 | tf_op jit(solution)/shard_map/all_to_all | solution.py:301
  92.8 0.0 copy-start.3
  92.9 0.0 copy-start.5
  92.9 0.1 slice.28
  93.0 0.5 copy.12
  93.5 19.2 %all-to-all-done.3.got = bf16[16,72,128]{2,1,0:T(8,128)(2,1)S(1)} async-done(((bf16[16,72,128]{2,1,0:T(8,128)(2,1)}), bf16[16,72,128]{2,1,0:T(8,128)(2,1)S(1)}, u32[]{:S(2)}, u32[]{:S(2)}) %all-to-all-start.3) | async-done | bytes 294944 | tf_op jit(solution)/shard_map/all_to_all | solution.py:301
  112.7 0.0 copy-done.3
  112.7 0.0 copy-done.5
  112.7 2.9 %shard_map.71 = (f32[1,16]{1,0:T(1,128)}, bf16[8,512]{1,0:T(8,128)(2,1)}, bf16[2048,512]{1,0:T(8,128)(2,1)}) custom-call(s32[6]{0:T(128)S(1)} %stack.19.scalars, f32[256]{0:T(256)S(1)} %copy-done.3, bf16[16,72,128]{2,1,0:T(8,128)(2,1)S(1)} %all-to-all-done.3.got, bf16[2048,256]{1,0:T(8,128)(2,1)S(1)} %bitcast.17, f32[8,256]{1,0:T(8,128)S(1)} %get-tuple-element.23.stat, ...), custom_call_target="tpu_custom_call" | custom-call | flops 536870912 | bytes 4194304 | tf_op jit(solution)/shard_map/pallas_call | solution.py:34
  (5 shorter events, 0.0 us)
Async XLA Ops:
  2.0 29.9 %all-to-all-start = ((bf16[16,8,512]{2,1,0:T(8,128)(2,1)}), bf16[16,8,512]{2,1,0:T(8,128)(2,1)S(1)}, u32[]{:S(2)}, u32[]{:S(2)}) async-start(bf16[16,8,512]{2,1,0:T(8,128)(2,1)} %broadcast_in_dim.6), calls=%async_computation | async-start | bytes 262144 | tf_op jit(solution)/shard_map/all_to_all | solution.py:301
  19.3 4.2 %copy-start = (bf16[2048,512]{1,0:T(8,128)(2,1)S(1)}, bf16[2048,512]{1,0:T(8,128)(2,1)}, u32[]{:S(2)}) copy-start(bf16[2048,512]{1,0:T(8,128)(2,1)} %weight.1) | copy-start | bytes 6291460
  31.9 29.3 %copy-start.2 = (s32[256]{0:T(256)S(1)}, s32[256]{0:T(256)}, u32[]{:S(2)}) copy-start(s32[256]{0:T(256)} %labels.1) | copy-start | bytes 3076
  31.9 3.4 %collective-permute-start = (bf16[128,512]{1,0:T(8,128)(2,1)S(1)}, bf16[128,512]{1,0:T(8,128)(2,1)S(1)}, u32[]{:S(2)}, u32[]{:S(2)}) collective-permute-start(bf16[128,512]{1,0:T(8,128)(2,1)S(1)} %bitcast.18), channel_id=1, source_target_pairs={{0,16},{16,0},{32,48},{48,32},{64,80},{80,64},{96,112},{112,96},{1... | collective-permute-start | bytes 393224 | tf_op jit(solution)/shard_map/ppermute | solution.py:321
  35.2 1.6 %copy-start.1 = (bf16[2048,512]{0,1:T(8,128)(2,1)S(1)}, bf16[2048,512]{0,1:T(8,128)(2,1)}, u32[]{:S(2)}) copy-start(bf16[2048,512]{0,1:T(8,128)(2,1)} %copy.10) | copy-start | bytes 6291460
  37.8 23.4 %copy-start.4 = (bf16[256,512]{1,0:T(8,128)(2,1)}, bf16[256,512]{1,0:T(8,128)(2,1)S(1)}, u32[]{:S(2)}) copy-start(bf16[256,512]{1,0:T(8,128)(2,1)S(1)} %get-tuple-element.25.whole) | copy-start | bytes 786436
  83.3 3.5 %collective-permute-start.1 = (bf16[144,1024]{1,0:T(8,128)(2,1)S(1)}, bf16[144,1024]{1,0:T(8,128)(2,1)S(1)}, u32[]{:S(2)}, u32[]{:S(2)}) collective-permute-start(bf16[144,1024]{1,0:T(8,128)(2,1)S(1)} %get-tuple-element.24), channel_id=1, source_target_pairs={{0,16},{16,0},{32,48},{48,32},{64,80},{80,64},{96,112},{112,96},{1... | collective-permute-start | bytes 884744 | tf_op jit(solution)/shard_map/ppermute | solution.py:351
  88.6 24.2 %all-to-all-start.3 = ((bf16[16,72,128]{2,1,0:T(8,128)(2,1)}), bf16[16,72,128]{2,1,0:T(8,128)(2,1)S(1)}, u32[]{:S(2)}, u32[]{:S(2)}) async-start(bf16[16,72,128]{2,1,0:T(8,128)(2,1)} %shard_map.70), calls=%async_computation.3 | async-start | bytes 589824 | tf_op jit(solution)/shard_map/all_to_all | solution.py:301
  92.8 19.9 %copy-start.3 = (f32[256]{0:T(256)S(1)}, f32[256]{0:T(256)}, u32[]{:S(2)}) copy-start(f32[256]{0:T(256)} %loss_grad.1) | copy-start | bytes 3076
  92.9 19.9 %copy-start.5 = (bf16[256,512]{1,0:T(8,128)(2,1)S(1)}, bf16[256,512]{1,0:T(8,128)(2,1)}, u32[]{:S(2)}) copy-start(bf16[256,512]{1,0:T(8,128)(2,1)} %copy-done.4) | copy-start | bytes 786436

commit v6 on v5

--- a/solution.py
+++ b/solution.py
@@ -64,14 +64,26 @@
     return block[k : k + 1] + block[k + 1 : k + 2] + block[k + 2 : k + 3]
 
 
-def logits_kernel(mine, other, weight, out, whole, part):
+def logits_kernel(mine, other, weight, out, whole, part, staged, sems):
     half = mine.shape[0]
-    voc = weight.shape[1]
+    voc = weight.shape[0]
+    starts = range(0, voc, CHUNK)
+    copies = []
+    for n, k in enumerate(starts):
+        at = pl.ds(k, CHUNK)
+        copies.append(pltpu.make_async_copy(weight.at[at], staged.at[at], sems.at[n]))
+        copies[-1].start()
     whole[:half, :] = mine[...]
     whole[half:, :] = other[...]
     top = jnp.zeros((2 * half, LANES), F32)
-    for k in range(0, voc, CHUNK):
-        block = jnp.dot(whole[...], weight[:, k : k + CHUNK], preferred_element_type=F32)
+    for copy, k in zip(copies, starts):
+        copy.wait()
+        block = lax.dot_general(
+            whole[...],
+            staged[k : k + CHUNK, :],
+            (((1,), (1,)), ((), ())),
+            preferred_element_type=F32,
+        )
         part[:, k : k + CHUNK] = block
         size = jnp.abs(block)
         for c in range(0, CHUNK, LANES):
@@ -79,7 +91,7 @@
     top = jnp.max(top, axis=1, keepdims=True)
     grade = jnp.ceil(jnp.log2(jnp.maximum(top, 1e-30)) * GRAIN)
     per = STEPS * jnp.exp2(grade * (-1.0 / GRAIN))
-    for k in range(0, voc, CHUNK):
+    for k in starts:
         out[:, k : k + CHUNK] = jnp.round(part[:, k : k + CHUNK] * per).astype(I32).astype(I16)
     out[:, voc:] = jnp.broadcast_to(grade, (2 * half, LANES)).astype(I32).astype(I16)
 
@@ -133,7 +145,7 @@
         out[i, :, voc:] = stats
 
 
-def partial_kernel(got, weight, rows, send, part, stat, sems):
+def send_kernel(got, weight, rows, send, stat, sems):
     voc, feat = weight.shape
     half = got.shape[0] // 2
     copy = pltpu.make_async_copy(
@@ -146,8 +158,14 @@
     send[:half, :feat] = jnp.dot(
         got[half:, :voc], weight[...], preferred_element_type=F32
     ).astype(BF16)
-    part[...] = jnp.dot(got[:half, :voc], weight[...], preferred_element_type=F32)
     copy.wait()
+
+
+def keep_kernel(got, weight, part):
+    voc = weight.shape[0]
+    part[...] = jnp.dot(
+        got[: part.shape[0], :voc], weight[...], preferred_element_type=F32
+    )
 
 
 def pair_kernel(scalars, part, stat, got, rows, out, own_rows, sems):
@@ -309,24 +327,23 @@
         second = jnp.where(core == 0, x[:, 1], x[:, 0])
         return jnp.concatenate([first.reshape(half), second.reshape(half)])
 
-    label = own_core_first(labels)
-    grad = own_core_first(loss_grad)
     columns = section * voc + jnp.arange(voc, dtype=I32)
 
     mine = exchange_z(jnp.broadcast_to(hidden[None], (n_z, mine_n, feat))).reshape(half, feat)
-    hot = label[:, None] == columns[None, :]
+    hot = own_core_first(labels)[:, None] == columns[None, :]
     rows = jnp.dot(hot.astype(BF16), head_weight, preferred_element_type=F32).astype(BF16)
-    ready = (mine, rows, head_weight.T, label[None], grad[None], scalars)
-    mine, rows, tall, label, grad, scalars = lax.optimization_barrier(ready)
+    mine, rows, scalars = lax.optimization_barrier((mine, rows, scalars))
     other = lax.ppermute(mine, "section", swap)
 
     width = voc + LANES
     coded, whole = call(
         logits_kernel,
         [],
-        [mine, other, tall],
+        [mine, other],
         [((tokens, width), I16), ((tokens, feat), BF16)],
-        scratch=[((tokens, voc), F32)],
+        left=[head_weight],
+        scratch=[((tokens, voc), F32), ((voc, feat), BF16)],
+        copies=voc // CHUNK,
         flops=flops,
     )
     coded = exchange_dp(coded.reshape(n_dp, share, width))
@@ -339,16 +356,17 @@
     )
     got = exchange_dp(message).reshape(tokens, width)
 
-    send, part, stat = call(
-        partial_kernel,
+    send, stat = call(
+        send_kernel,
         [],
         [got, head_weight],
-        [((half + 16, 2 * feat), BF16), ((half, feat), F32), ((8, tokens), F32)],
+        [((half + 16, 2 * feat), BF16), ((8, tokens), F32)],
         left=[rows],
         copies=1,
-        flops=flops,
+        flops=flops // 2,
     )
     theirs = lax.ppermute(send, "section", swap)
+    (part,) = call(keep_kernel, [], [got, head_weight], [((half, feat), F32)], flops=flops // 2)
     (message,) = call(
         pair_kernel,
         [scalars],
@@ -360,6 +378,8 @@
     )
     last = exchange_z(message)
     soft = got[:, :voc].T
+    late = lax.optimization_barrier((labels, loss_grad, message))
+    label, grad = own_core_first(late[0])[None], own_core_first(late[1])[None]
     loss, grad_hidden, grad_weight = call(
         tail_kernel,
         [scalars, loss_grad],

time: 117 us -> 117 us (level)
  local copies, waits for them, and re-layouts: 9.68 us -> 5.52 us
  Pallas kernels: 7.49 us -> 9.73 us
  matrix products: 0.75 us -> 2.34 us
    unnamed x15 -> x11, local copies, waits for them, and re-layouts: 6.22 us -> 1.5 us
    pallas_call x5 -> x6, Pallas kernels: 7.49 us -> 9.73 us  [call(): pl.pallas_call(kernel, out_shape=[jax.ShapeDtypeStruct(s, d) for s, d in...]
    dot_general x1, matrix products: 0.75 us -> 2.34 us  [local(): jnp.dot(hot.astype(BF16), head_weight, preferred_element_type=F32)]
  transfers between devices with their start and end apart: 4 -> 4, of which waited for: 4 -> 4; matrix products, arithmetic and copies ran while one was open for 7% -> 6% of each run, Pallas kernels for 0% -> 0%
where the time goes in v6:
time: 117 us; the launch traced here: 116 us
  blocking collectives  43.6 us (37%)
  waiting for transfers between devices  30.2 us (26%)
  starting transfers between devices  23.1 us (20%)
  Pallas kernels  9.73 us (8%)
  local copies, waits for them, and re-layouts  5.52 us (5%)
  matrix products  2.34 us (2%)
    all_to_all x2, blocking collectives, exchange_dp(): return lax.all_to_all(x, 'dp', 0, 0, tiled=True)  43.6 us
    all_to_all x2, waiting for transfers between devices, exchange_z(): lax.all_to_all(x, 'section', 0, 0, tiled=True, axis_index_groups=along_z)  27.8 us
    all_to_all x2, starting transfers between devices, exchange_z(): lax.all_to_all(x, 'section', 0, 0, tiled=True, axis_index_groups=along_z)  19.2 us
    pallas_call x6, Pallas kernels, call(): pl.pallas_call(kernel, out_shape=[jax.ShapeDtypeStruct(s, d) for s, d in...  9.73 us
    dot_general x1, matrix products, local(): jnp.dot(hot.astype(BF16), head_weight, preferred_element_type=F32)  2.34 us
  transfers between devices with their start and end apart: 4, of which 4 were waited for; matrix products, arithmetic and copies ran while one was open for 6% of the time, Pallas kernels for 0%

profile of v6, /device:TPU:6, one launch (start us, length us, event | category | flops | bytes accessed | tf_op | source)
XLA Modules:
  0.0 115.5 jit_solution(11996421491157056008)
XLA Ops:
  0.6 1.4 %broadcast_in_dim.6 = bf16[16,8,512]{2,1,0:T(8,128)(2,1)} broadcast(bf16[8,512]{1,0:T(8,128)(2,1)} %param.4), dimensions={1,2} | broadcast | bytes 139264 | tf_op jit(solution)/shard_map/broadcast_in_dim | solution.py:332
  2.0 0.0 copy-start
  2.0 15.3 %all-to-all-start = ((bf16[16,8,512]{2,1,0:T(8,128)(2,1)}), bf16[16,8,512]{2,1,0:T(8,128)(2,1)S(1)}, u32[]{:S(2)}, u32[]{:S(2)}) async-start(bf16[16,8,512]{2,1,0:T(8,128)(2,1)} %broadcast_in_dim.6), calls=%async_computation | async-start | bytes 262144 | tf_op jit(solution)/shard_map/all_to_all | solution.py:319
  17.3 0.8 reshape.64
  18.1 0.1 fusion.7
  18.2 0.1 select_n.68
  18.3 0.1 select_n.70
  18.4 0.1 stack.19.scalars
  18.5 2.3 %fusion.2.rows = bf16[256,512]{1,0:T(8,128)(2,1)S(1)} fusion(bf16[2048,512]{1,0:T(8,128)(2,1)} %weight.5, s32[2048]{0:T(1024)S(1)} %iota_add_fusion, s32[256]{0:T(256)S(1)} %pad_add_fusion), kind=kOutput, calls=%fused_computation.2 | convolution fusion | flops 537526272 | bytes 2368512 | tf_op jit(solution)/shard_map/dot_general | solution.py:334
  20.8 11.2 %all-to-all-done = bf16[16,8,512]{2,1,0:T(8,128)(2,1)S(1)} async-done(((bf16[16,8,512]{2,1,0:T(8,128)(2,1)}), bf16[16,8,512]{2,1,0:T(8,128)(2,1)S(1)}, u32[]{:S(2)}, u32[]{:S(2)}) %all-to-all-start) | async-done | bytes 131104 | tf_op jit(solution)/shard_map/all_to_all | solution.py:319
  32.0 0.0 copy-start.1
  32.0 2.0 %collective-permute-start = (bf16[128,512]{1,0:T(8,128)(2,1)S(1)}, bf16[128,512]{1,0:T(8,128)(2,1)S(1)}, u32[]{:S(2)}, u32[]{:S(2)}) collective-permute-start(bf16[128,512]{1,0:T(8,128)(2,1)S(1)} %bitcast.17), channel_id=1, source_target_pairs={{0,16},{16,0},{32,48},{48,32},{64,80},{80,64},{96,112},{112,96},{1... | collective-permute-start | bytes 393224 | tf_op jit(solution)/shard_map/ppermute | solution.py:336
  34.1 1.3 %collective-permute-done.other = bf16[128,512]{1,0:T(8,128)(2,1)S(1)} collective-permute-done((bf16[128,512]{1,0:T(8,128)(2,1)S(1)}, bf16[128,512]{1,0:T(8,128)(2,1)S(1)}, u32[]{:S(2)}, u32[]{:S(2)}) %collective-permute-start) | collective-permute-done | bytes 131104 | tf_op jit(solution)/shard_map/ppermute | solution.py:336
  35.4 0.0 copy-done
  35.4 3.0 %shard_map.67 = (s16[256,2176]{1,0:T(8,128)(2,1)S(1)}, bf16[256,512]{1,0:T(8,128)(2,1)S(1)}) custom-call(bf16[128,512]{1,0:T(8,128)(2,1)S(1)} %bitcast.18, bf16[128,512]{1,0:T(8,128)(2,1)S(1)} %collective-permute-done.other, bf16[2048,512]{1,0:T(8,128)(2,1)S(1)} %copy-done), custom_call_target="tpu_custom_call" | custom-call | flops 536870912 | bytes 4194304 | tf_op jit(solution)/shard_map/pallas_call | solution.py:34
  38.4 0.0 copy-start.3
  38.4 23.4 %all_to_all.20.got = s16[16,16,2176]{2,1,0:T(8,128)(2,1)S(1)} all-to-all(s16[16,16,2176]{2,1,0:T(8,128)(2,1)S(1)} %bitcast.15), channel_id=1, replica_groups=mesh['section'=32,'dp'=16] {'dp'}, dimensions={0} | all-to-all | bytes 2228224 | tf_op jit(solution)/shard_map/all_to_all | solution.py:322
  61.8 0.0 copy-done.3
  61.8 0.0 copy-done.1
  61.8 1.2 %shard_map.68 = bf16[16,16,2176]{2,1,0:T(8,128)(2,1)S(1)} custom-call(s32[6]{0:T(128)S(1)} %stack.19.scalars, s32[256]{0:T(256)S(1)} %copy-done.1, s16[16,16,2176]{2,1,0:T(8,128)(2,1)S(1)} %all_to_all.20.got), custom_call_target="tpu_custom_call" | custom-call | bytes 4194304 | tf_op jit(solution)/shard_map/pallas_call | solution.py:34
  63.0 20.2 %all_to_all.21 = bf16[16,16,2176]{2,1,0:T(8,128)(2,1)S(1)} all-to-all(bf16[16,16,2176]{2,1,0:T(8,128)(2,1)S(1)} %shard_map.68), channel_id=1, replica_groups=mesh['section'=32,'dp'=16] {'dp'}, dimensions={0} | all-to-all | bytes 2228224 | tf_op jit(solution)/shard_map/all_to_all | solution.py:322
  83.2 0.5 shard_map.70
  83.7 1.9 %collective-permute-start.1 = (bf16[144,1024]{1,0:T(8,128)(2,1)S(1)}, bf16[144,1024]{1,0:T(8,128)(2,1)S(1)}, u32[]{:S(2)}, u32[]{:S(2)}) collective-permute-start(bf16[144,1024]{1,0:T(8,128)(2,1)S(1)} %get-tuple-element.20), channel_id=1, source_target_pairs={{0,16},{16,0},{32,48},{48,32},{64,80},{80,64},{96,112},{112,96},{1... | collective-permute-start | bytes 884744 | tf_op jit(solution)/shard_map/ppermute | solution.py:368
  85.6 0.4 shard_map.69.part
  86.0 1.1 collective-permute-done.1.got
  87.1 1.8 %shard_map.71 = bf16[16,72,128]{2,1,0:T(8,128)(2,1)} custom-call(s32[6]{0:T(128)S(1)} %stack.19.scalars, f32[128,512]{1,0:T(8,128)S(1)} %shard_map.69.part, f32[8,256]{1,0:T(8,128)S(1)} %get-tuple-element.19.stat, bf16[144,1024]{1,0:T(8,128)(2,1)S(1)} %collective-permute-done.1.got, bf16[256,512]{1,0:T(8,128)(2,1)S(1)} %fusion.2.rows), custom_call_target="tpu_custom_call" | custom-call | bytes 4194304 | tf_op jit(solution)/shard_map/pallas_call | solution.py:34
  88.9 3.8 %all-to-all-start.3 = ((bf16[16,72,128]{2,1,0:T(8,128)(2,1)}), bf16[16,72,128]{2,1,0:T(8,128)(2,1)S(1)}, u32[]{:S(2)}, u32[]{:S(2)}) async-start(bf16[16,72,128]{2,1,0:T(8,128)(2,1)} %shard_map.71), calls=%async_computation.3 | async-start | bytes 589824 | tf_op jit(solution)/shard_map/all_to_all | solution.py:319
  92.8 0.0 copy-start.2
  92.8 0.0 copy-start.4
  92.8 1.1 slice.36
  93.9 1.5 %copy.11 = bf16[256,2048]{0,1:T(8,128)(2,1)S(1)} copy(bf16[256,2048]{1,0:T(8,128)(2,1)} %slice.36) | data formatting | bytes 2097152
  95.4 0.1 reshape.67
  95.5 0.1 fusion.9
  95.5 0.1 select_n.73
  95.6 0.1 select_n.75
  95.7 0.0 copy-done.2
  95.7 0.1 reshape.68
  95.8 0.1 fusion.11
  95.9 0.1 select_n.77
  96.0 0.1 select_n.79
  96.1 16.6 %all-to-all-done.3.got = bf16[16,72,128]{2,1,0:T(8,128)(2,1)S(1)} async-done(((bf16[16,72,128]{2,1,0:T(8,128)(2,1)}), bf16[16,72,128]{2,1,0:T(8,128)(2,1)S(1)}, u32[]{:S(2)}, u32[]{:S(2)}) %all-to-all-start.3) | async-done | bytes 294944 | tf_op jit(solution)/shard_map/all_to_all | solution.py:319
  112.7 0.0 copy-done.4
  112.7 2.9 %shard_map.72 = (f32[1,16]{1,0:T(1,128)}, bf16[8,512]{1,0:T(8,128)(2,1)}, bf16[2048,512]{1,0:T(8,128)(2,1)}) custom-call(s32[6]{0:T(128)S(1)} %stack.19.scalars, f32[256]{0:T(256)S(1)} %copy-done.2, bf16[16,72,128]{2,1,0:T(8,128)(2,1)S(1)} %all-to-all-done.3.got, bf16[2048,256]{1,0:T(8,128)(2,1)S(1)} %bitcast.16, f32[8,256]{1,0:T(8,128)S(1)} %get-tuple-element.19.stat, ...), custom_call_target="tpu_custom_call" | custom-call | flops 536870912 | bytes 4194304 | tf_op jit(solution)/shard_map/pallas_call | solution.py:34
  (4 shorter events, 0.0 us)
Async XLA Ops:
  2.0 33.4 %copy-start = (bf16[2048,512]{1,0:T(8,128)(2,1)S(1)}, bf16[2048,512]{1,0:T(8,128)(2,1)}, u32[]{:S(2)}) copy-start(bf16[2048,512]{1,0:T(8,128)(2,1)} %weight.5) | copy-start | bytes 6291460
  2.0 30.0 %all-to-all-start = ((bf16[16,8,512]{2,1,0:T(8,128)(2,1)}), bf16[16,8,512]{2,1,0:T(8,128)(2,1)S(1)}, u32[]{:S(2)}, u32[]{:S(2)}) async-start(bf16[16,8,512]{2,1,0:T(8,128)(2,1)} %broadcast_in_dim.6), calls=%async_computation | async-start | bytes 262144 | tf_op jit(solution)/shard_map/all_to_all | solution.py:319
  32.0 29.8 %copy-start.1 = (s32[256]{0:T(256)S(1)}, s32[256]{0:T(256)}, u32[]{:S(2)}) copy-start(s32[256]{0:T(256)} %labels.1) | copy-start | bytes 3076
  32.0 3.4 %collective-permute-start = (bf16[128,512]{1,0:T(8,128)(2,1)S(1)}, bf16[128,512]{1,0:T(8,128)(2,1)S(1)}, u32[]{:S(2)}, u32[]{:S(2)}) collective-permute-start(bf16[128,512]{1,0:T(8,128)(2,1)S(1)} %bitcast.17), channel_id=1, source_target_pairs={{0,16},{16,0},{32,48},{48,32},{64,80},{80,64},{96,112},{112,96},{1... | collective-permute-start | bytes 393224 | tf_op jit(solution)/shard_map/ppermute | solution.py:336
  38.4 23.4 %copy-start.3 = (bf16[256,512]{1,0:T(8,128)(2,1)}, bf16[256,512]{1,0:T(8,128)(2,1)S(1)}, u32[]{:S(2)}) copy-start(bf16[256,512]{1,0:T(8,128)(2,1)S(1)} %get-tuple-element.21.whole) | copy-start | bytes 786436
  83.7 3.5 %collective-permute-start.1 = (bf16[144,1024]{1,0:T(8,128)(2,1)S(1)}, bf16[144,1024]{1,0:T(8,128)(2,1)S(1)}, u32[]{:S(2)}, u32[]{:S(2)}) collective-permute-start(bf16[144,1024]{1,0:T(8,128)(2,1)S(1)} %get-tuple-element.20), channel_id=1, source_target_pairs={{0,16},{16,0},{32,48},{48,32},{64,80},{80,64},{96,112},{112,96},{1... | collective-permute-start | bytes 884744 | tf_op jit(solution)/shard_map/ppermute | solution.py:368
  88.9 23.7 %all-to-all-start.3 = ((bf16[16,72,128]{2,1,0:T(8,128)(2,1)}), bf16[16,72,128]{2,1,0:T(8,128)(2,1)S(1)}, u32[]{:S(2)}, u32[]{:S(2)}) async-start(bf16[16,72,128]{2,1,0:T(8,128)(2,1)} %shard_map.71), calls=%async_computation.3 | async-start | bytes 589824 | tf_op jit(solution)/shard_map/all_to_all | solution.py:319
  92.8 2.9 %copy-start.2 = (f32[256]{0:T(256)S(1)}, f32[256]{0:T(256)}, u32[]{:S(2)}) copy-start(f32[256]{0:T(256)} %loss_grad.1) | copy-start | bytes 3076
  92.8 19.9 %copy-start.4 = (bf16[256,512]{1,0:T(8,128)(2,1)S(1)}, bf16[256,512]{1,0:T(8,128)(2,1)}, u32[]{:S(2)}) copy-start(bf16[256,512]{1,0:T(8,128)(2,1)} %copy-done.3) | copy-start | bytes 786436

commit v7 on v5

--- a/solution.py
+++ b/solution.py
@@ -62,6 +62,19 @@
 
 def join3(block, k):
     return block[k : k + 1] + block[k + 1 : k + 2] + block[k + 2 : k + 3]
+
+
+def prepare_kernel(weight, label, tall, rows):
+    voc, feat = weight.shape
+    tokens = label.shape[0]
+    lane = lax.broadcasted_iota(I32, (tokens, CHUNK), 1)
+    total = jnp.zeros((tokens, feat), F32)
+    for k in range(0, voc, CHUNK):
+        block = weight[k : k + CHUNK, :]
+        tall[:, k : k + CHUNK] = block.T
+        hot = (lane + k == label[...]).astype(BF16)
+        total += jnp.dot(hot, block, preferred_element_type=F32)
+    rows[...] = total.astype(BF16)
 
 
 def logits_kernel(mine, other, weight, out, whole, part):
@@ -133,7 +146,7 @@
         out[i, :, voc:] = stats
 
 
-def partial_kernel(got, weight, rows, send, part, stat, sems):
+def send_kernel(got, weight, rows, send, stat, sems):
     voc, feat = weight.shape
     half = got.shape[0] // 2
     copy = pltpu.make_async_copy(
@@ -146,8 +159,14 @@
     send[:half, :feat] = jnp.dot(
         got[half:, :voc], weight[...], preferred_element_type=F32
     ).astype(BF16)
-    part[...] = jnp.dot(got[:half, :voc], weight[...], preferred_element_type=F32)
     copy.wait()
+
+
+def keep_kernel(got, weight, part):
+    voc = weight.shape[0]
+    part[...] = jnp.dot(
+        got[: part.shape[0], :voc], weight[...], preferred_element_type=F32
+    )
 
 
 def pair_kernel(scalars, part, stat, got, rows, out, own_rows, sems):
@@ -309,15 +328,15 @@
         second = jnp.where(core == 0, x[:, 1], x[:, 0])
         return jnp.concatenate([first.reshape(half), second.reshape(half)])
 
-    label = own_core_first(labels)
-    grad = own_core_first(loss_grad)
-    columns = section * voc + jnp.arange(voc, dtype=I32)
-
     mine = exchange_z(jnp.broadcast_to(hidden[None], (n_z, mine_n, feat))).reshape(half, feat)
-    hot = label[:, None] == columns[None, :]
-    rows = jnp.dot(hot.astype(BF16), head_weight, preferred_element_type=F32).astype(BF16)
-    ready = (mine, rows, head_weight.T, label[None], grad[None], scalars)
-    mine, rows, tall, label, grad, scalars = lax.optimization_barrier(ready)
+    tall, rows = call(
+        prepare_kernel,
+        [],
+        [head_weight, (own_core_first(labels) - section * voc)[:, None]],
+        [((feat, voc), BF16), ((tokens, feat), BF16)],
+        flops=flops,
+    )
+    mine, tall, rows, scalars = lax.optimization_barrier((mine, tall, rows, scalars))
     other = lax.ppermute(mine, "section", swap)
 
     width = voc + LANES
@@ -339,16 +358,17 @@
     )
     got = exchange_dp(message).reshape(tokens, width)
 
-    send, part, stat = call(
-        partial_kernel,
+    send, stat = call(
+        send_kernel,
         [],
         [got, head_weight],
-        [((half + 16, 2 * feat), BF16), ((half, feat), F32), ((8, tokens), F32)],
+        [((half + 16, 2 * feat), BF16), ((8, tokens), F32)],
         left=[rows],
         copies=1,
-        flops=flops,
+        flops=flops // 2,
     )
     theirs = lax.ppermute(send, "section", swap)
+    (part,) = call(keep_kernel, [], [got, head_weight], [((half, feat), F32)], flops=flops // 2)
     (message,) = call(
         pair_kernel,
         [scalars],
@@ -360,6 +380,8 @@
     )
     last = exchange_z(message)
     soft = got[:, :voc].T
+    late = lax.optimization_barrier((labels, loss_grad, message))
+    label, grad = own_core_first(late[0])[None], own_core_first(late[1])[None]
     loss, grad_hidden, grad_weight = call(
         tail_kernel,
         [scalars, loss_grad],

time: 117 us -> 115 us (0.983)
  local copies, waits for them, and re-layouts: 9.68 us -> 5.3 us
  waiting for transfers between devices: 29.7 us -> 31.7 us
  Pallas kernels: 7.49 us -> 8.73 us
    unnamed x15 -> x9, local copies, waits for them, and re-layouts: 6.22 us -> 2.13 us
    all_to_all x2, waiting for transfers between devices: 26.9 us -> 29.2 us  [exchange_z(): lax.all_to_all(x, 'section', 0, 0, tiled=True, axis_index_groups=along_z)]
    pallas_call x5 -> x7, Pallas kernels: 7.49 us -> 8.73 us  [call(): pl.pallas_call(kernel, out_shape=[jax.ShapeDtypeStruct(s, d) for s, d in...]
  transfers between devices with their start and end apart: 4 -> 4, of which waited for: 4 -> 4; matrix products, arithmetic and copies ran while one was open for 7% -> 2% of each run, Pallas kernels for 0% -> 1%
where the time goes in v7:
time: 115 us; the launch traced here: 113 us
  blocking collectives  43.7 us (38%)
  waiting for transfers between devices  31.7 us (28%)
  starting transfers between devices  22.9 us (20%)
  Pallas kernels  8.73 us (8%)
  local copies, waits for them, and re-layouts  5.3 us (5%)
    all_to_all x2, blocking collectives, exchange_dp(): return lax.all_to_all(x, 'dp', 0, 0, tiled=True)  43.7 us
    all_to_all x2, waiting for transfers between devices, exchange_z(): lax.all_to_all(x, 'section', 0, 0, tiled=True, axis_index_groups=along_z)  29.2 us
    all_to_all x2, starting transfers between devices, exchange_z(): lax.all_to_all(x, 'section', 0, 0, tiled=True, axis_index_groups=along_z)  19 us
    pallas_call x7, Pallas kernels, call(): pl.pallas_call(kernel, out_shape=[jax.ShapeDtypeStruct(s, d) for s, d in...  8.73 us
  transfers between devices with their start and end apart: 4, of which 4 were waited for; matrix products, arithmetic and copies ran while one was open for 2% of the time, Pallas kernels for 1%

profile of v7, /device:TPU:6, one launch (start us, length us, event | category | flops | bytes accessed | tf_op | source)
XLA Modules:
  0.0 113.4 jit_solution(17076906873863124339)
XLA Ops:
  0.6 1.4 %broadcast_in_dim.6 = bf16[16,8,512]{2,1,0:T(8,128)(2,1)} broadcast(bf16[8,512]{1,0:T(8,128)(2,1)} %param.4), dimensions={1,2} | broadcast | bytes 139264 | tf_op jit(solution)/shard_map/broadcast_in_dim | solution.py:331
  2.0 15.2 %all-to-all-start = ((bf16[16,8,512]{2,1,0:T(8,128)(2,1)}), bf16[16,8,512]{2,1,0:T(8,128)(2,1)S(1)}, u32[]{:S(2)}, u32[]{:S(2)}) async-start(bf16[16,8,512]{2,1,0:T(8,128)(2,1)} %broadcast_in_dim.6), calls=%async_computation | async-start | bytes 262144 | tf_op jit(solution)/shard_map/all_to_all | solution.py:320
  17.2 0.8 reshape.102
  18.0 0.1 fusion
  18.1 0.1 concatenate.20
  18.1 0.1 concatenate.21
  18.2 0.1 copy.17
  18.4 0.1 stack.19.scalars
  18.5 0.0 copy-start
  18.5 1.6 %copy-done = bf16[2048,512]{1,0:T(8,128)(2,1)S(1)} copy-done((bf16[2048,512]{1,0:T(8,128)(2,1)S(1)}, bf16[2048,512]{1,0:T(8,128)(2,1)}, u32[]{:S(2)}) %copy-start) | copy-done | bytes 2097176
  20.1 1.1 shard_map.67
  21.2 10.7 %all-to-all-done = bf16[16,8,512]{2,1,0:T(8,128)(2,1)S(1)} async-done(((bf16[16,8,512]{2,1,0:T(8,128)(2,1)}), bf16[16,8,512]{2,1,0:T(8,128)(2,1)S(1)}, u32[]{:S(2)}, u32[]{:S(2)}) %all-to-all-start) | async-done | bytes 131104 | tf_op jit(solution)/shard_map/all_to_all | solution.py:320
  31.9 1.9 %collective-permute-start = (bf16[128,512]{1,0:T(8,128)(2,1)S(1)}, bf16[128,512]{1,0:T(8,128)(2,1)S(1)}, u32[]{:S(2)}, u32[]{:S(2)}) collective-permute-start(bf16[128,512]{1,0:T(8,128)(2,1)S(1)} %bitcast.16), channel_id=1, source_target_pairs={{0,16},{16,0},{32,48},{48,32},{64,80},{80,64},{96,112},{112,96},{1... | collective-permute-start | bytes 393224 | tf_op jit(solution)/shard_map/ppermute | solution.py:340
  33.8 1.3 %collective-permute-done.other = bf16[128,512]{1,0:T(8,128)(2,1)S(1)} collective-permute-done((bf16[128,512]{1,0:T(8,128)(2,1)S(1)}, bf16[128,512]{1,0:T(8,128)(2,1)S(1)}, u32[]{:S(2)}, u32[]{:S(2)}) %collective-permute-start) | collective-permute-done | bytes 131104 | tf_op jit(solution)/shard_map/ppermute | solution.py:340
  35.1 1.0 shard_map.68
  36.1 0.0 copy-start.2
  36.1 23.4 %all_to_all.20.got = s16[16,16,2176]{2,1,0:T(8,128)(2,1)S(1)} all-to-all(s16[16,16,2176]{2,1,0:T(8,128)(2,1)S(1)} %bitcast.14), channel_id=1, replica_groups=mesh['section'=32,'dp'=16] {'dp'}, dimensions={0} | all-to-all | bytes 2228224 | tf_op jit(solution)/shard_map/all_to_all | solution.py:323
  59.5 0.0 copy-done.2
  59.5 1.2 %shard_map.69 = bf16[16,16,2176]{2,1,0:T(8,128)(2,1)S(1)} custom-call(s32[6]{0:T(128)S(1)} %stack.19.scalars, s32[256]{0:T(256)S(1)} %copy-done.2, s16[16,16,2176]{2,1,0:T(8,128)(2,1)S(1)} %all_to_all.20.got), custom_call_target="tpu_custom_call" | custom-call | bytes 4194304 | tf_op jit(solution)/shard_map/pallas_call | solution.py:34
  60.6 0.0 copy-start.1
  60.6 20.4 %all_to_all.21 = bf16[16,16,2176]{2,1,0:T(8,128)(2,1)S(1)} all-to-all(bf16[16,16,2176]{2,1,0:T(8,128)(2,1)S(1)} %shard_map.69), channel_id=1, replica_groups=mesh['section'=32,'dp'=16] {'dp'}, dimensions={0} | all-to-all | bytes 2228224 | tf_op jit(solution)/shard_map/all_to_all | solution.py:323
  81.0 0.0 copy-done.1
  81.0 0.5 shard_map.71
  81.5 1.9 %collective-permute-start.1 = (bf16[144,1024]{1,0:T(8,128)(2,1)S(1)}, bf16[144,1024]{1,0:T(8,128)(2,1)S(1)}, u32[]{:S(2)}, u32[]{:S(2)}) collective-permute-start(bf16[144,1024]{1,0:T(8,128)(2,1)S(1)} %get-tuple-element.26), channel_id=1, source_target_pairs={{0,16},{16,0},{32,48},{48,32},{64,80},{80,64},{96,112},{112,96},{1... | collective-permute-start | bytes 884744 | tf_op jit(solution)/shard_map/ppermute | solution.py:370
  83.4 0.4 shard_map.70.part
  83.9 1.1 collective-permute-done.1.got
  85.0 1.8 %shard_map.72 = bf16[16,72,128]{2,1,0:T(8,128)(2,1)} custom-call(s32[6]{0:T(128)S(1)} %stack.19.scalars, f32[128,512]{1,0:T(8,128)S(1)} %shard_map.70.part, f32[8,256]{1,0:T(8,128)S(1)} %get-tuple-element.25.stat, bf16[144,1024]{1,0:T(8,128)(2,1)S(1)} %collective-permute-done.1.got, bf16[256,512]{1,0:T(8,128)(2,1)S(1)} %get-tuple-element.24.rows), custom_call_target="tpu_custom_call" | custom-call | bytes 4194304 | tf_op jit(solution)/shard_map/pallas_call | solution.py:34
  86.7 3.8 %all-to-all-start.3 = ((bf16[16,72,128]{2,1,0:T(8,128)(2,1)}), bf16[16,72,128]{2,1,0:T(8,128)(2,1)S(1)}, u32[]{:S(2)}, u32[]{:S(2)}) async-start(bf16[16,72,128]{2,1,0:T(8,128)(2,1)} %shard_map.72), calls=%async_computation.3 | async-start | bytes 589824 | tf_op jit(solution)/shard_map/all_to_all | solution.py:320
  90.6 0.1 slice.36
  90.7 0.0 copy-start.3
  90.7 0.5 copy.20
  91.3 0.1 reshape.105
  91.4 0.1 fusion.2
  91.4 0.1 select_n.79
  91.5 0.1 select_n.81
  91.6 0.0 copy-done.3
  91.6 0.1 reshape.106
  91.7 0.1 fusion.4
  91.8 0.1 select_n.83
  91.9 0.1 select_n.85
  92.0 18.5 %all-to-all-done.3.got = bf16[16,72,128]{2,1,0:T(8,128)(2,1)S(1)} async-done(((bf16[16,72,128]{2,1,0:T(8,128)(2,1)}), bf16[16,72,128]{2,1,0:T(8,128)(2,1)S(1)}, u32[]{:S(2)}, u32[]{:S(2)}) %all-to-all-start.3) | async-done | bytes 294944 | tf_op jit(solution)/shard_map/all_to_all | solution.py:320
  110.5 2.9 %shard_map.73 = (f32[1,16]{1,0:T(1,128)}, bf16[8,512]{1,0:T(8,128)(2,1)}, bf16[2048,512]{1,0:T(8,128)(2,1)}) custom-call(s32[6]{0:T(128)S(1)} %stack.19.scalars, f32[256]{0:T(256)S(1)} %copy-done.3, bf16[16,72,128]{2,1,0:T(8,128)(2,1)S(1)} %all-to-all-done.3.got, bf16[2048,256]{1,0:T(8,128)(2,1)S(1)} %bitcast.15, f32[8,256]{1,0:T(8,128)S(1)} %get-tuple-element.25.stat, ...), custom_call_target="tpu_custom_call" | custom-call | flops 536870912 | bytes 4194304 | tf_op jit(solution)/shard_map/pallas_call | solution.py:34
  (4 shorter events, 0.0 us)
Async XLA Ops:
  2.0 29.9 %all-to-all-start = ((bf16[16,8,512]{2,1,0:T(8,128)(2,1)}), bf16[16,8,512]{2,1,0:T(8,128)(2,1)S(1)}, u32[]{:S(2)}, u32[]{:S(2)}) async-start(bf16[16,8,512]{2,1,0:T(8,128)(2,1)} %broadcast_in_dim.6), calls=%async_computation | async-start | bytes 262144 | tf_op jit(solution)/shard_map/all_to_all | solution.py:320
  18.5 1.6 %copy-start = (bf16[2048,512]{1,0:T(8,128)(2,1)S(1)}, bf16[2048,512]{1,0:T(8,128)(2,1)}, u32[]{:S(2)}) copy-start(bf16[2048,512]{1,0:T(8,128)(2,1)} %weight.5) | copy-start | bytes 6291460
  31.9 3.2 %collective-permute-start = (bf16[128,512]{1,0:T(8,128)(2,1)S(1)}, bf16[128,512]{1,0:T(8,128)(2,1)S(1)}, u32[]{:S(2)}, u32[]{:S(2)}) collective-permute-start(bf16[128,512]{1,0:T(8,128)(2,1)S(1)} %bitcast.16), channel_id=1, source_target_pairs={{0,16},{16,0},{32,48},{48,32},{64,80},{80,64},{96,112},{112,96},{1... | collective-permute-start | bytes 393224 | tf_op jit(solution)/shard_map/ppermute | solution.py:340
  36.1 23.4 %copy-start.2 = (s32[256]{0:T(256)S(1)}, s32[256]{0:T(256)}, u32[]{:S(2)}) copy-start(s32[256]{0:T(256)} %labels.1) | copy-start | bytes 3076
  60.6 20.4 %copy-start.1 = (bf16[2048,512]{1,0:T(8,128)(2,1)S(1)}, bf16[2048,512]{1,0:T(8,128)(2,1)}, u32[]{:S(2)}) copy-start(bf16[2048,512]{1,0:T(8,128)(2,1)} %weight.5) | copy-start | bytes 6291460
  81.5 3.5 %collective-permute-start.1 = (bf16[144,1024]{1,0:T(8,128)(2,1)S(1)}, bf16[144,1024]{1,0:T(8,128)(2,1)S(1)}, u32[]{:S(2)}, u32[]{:S(2)}) collective-permute-start(bf16[144,1024]{1,0:T(8,128)(2,1)S(1)} %get-tuple-element.26), channel_id=1, source_target_pairs={{0,16},{16,0},{32,48},{48,32},{64,80},{80,64},{96,112},{112,96},{1... | collective-permute-start | bytes 884744 | tf_op jit(solution)/shard_map/ppermute | solution.py:370
  86.7 23.7 %all-to-all-start.3 = ((bf16[16,72,128]{2,1,0:T(8,128)(2,1)}), bf16[16,72,128]{2,1,0:T(8,128)(2,1)S(1)}, u32[]{:S(2)}, u32[]{:S(2)}) async-start(bf16[16,72,128]{2,1,0:T(8,128)(2,1)} %shard_map.72), calls=%async_computation.3 | async-start | bytes 589824 | tf_op jit(solution)/shard_map/all_to_all | solution.py:320
  90.7 0.9 copy-start.3

commit v8 on v7

--- a/solution.py
+++ b/solution.py
@@ -77,14 +77,13 @@
     rows[...] = total.astype(BF16)
 
 
-def logits_kernel(mine, other, weight, out, whole, part):
-    half = mine.shape[0]
+def code_logits(tokens, weight, out, part, first):
+    count = tokens.shape[0]
+    rows = slice(first, first + count)
     voc = weight.shape[1]
-    whole[:half, :] = mine[...]
-    whole[half:, :] = other[...]
-    top = jnp.zeros((2 * half, LANES), F32)
-    for k in range(0, voc, CHUNK):
-        block = jnp.dot(whole[...], weight[:, k : k + CHUNK], preferred_element_type=F32)
+    top = jnp.zeros((count, LANES), F32)
+    for k in range(0, voc, CHUNK):
+        block = jnp.dot(tokens[...], weight[:, k : k + CHUNK], preferred_element_type=F32)
         part[:, k : k + CHUNK] = block
         size = jnp.abs(block)
         for c in range(0, CHUNK, LANES):
@@ -93,8 +92,22 @@
     grade = jnp.ceil(jnp.log2(jnp.maximum(top, 1e-30)) * GRAIN)
     per = STEPS * jnp.exp2(grade * (-1.0 / GRAIN))
     for k in range(0, voc, CHUNK):
-        out[:, k : k + CHUNK] = jnp.round(part[:, k : k + CHUNK] * per).astype(I32).astype(I16)
-    out[:, voc:] = jnp.broadcast_to(grade, (2 * half, LANES)).astype(I32).astype(I16)
+        out[rows, k : k + CHUNK] = (
+            jnp.round(part[:, k : k + CHUNK] * per).astype(I32).astype(I16)
+        )
+    out[rows, voc:] = jnp.broadcast_to(grade, (count, LANES)).astype(I32).astype(I16)
+
+
+def mine_kernel(mine, weight, out, part):
+    code_logits(mine, weight, out, part, 0)
+
+
+def other_kernel(coded, mine, other, weight, out, whole, part):
+    half = mine.shape[0]
+    out[:half, :] = coded[...]
+    whole[:half, :] = mine[...]
+    whole[half:, :] = other[...]
+    code_logits(other, weight, out, part, half)
 
 
 def softmax_kernel(scalars, labels, got, out, logits):
@@ -146,20 +159,15 @@
         out[i, :, voc:] = stats
 
 
-def send_kernel(got, weight, rows, send, stat, sems):
-    voc, feat = weight.shape
+def send_kernel(got, weight, send, stat):
+    voc = weight.shape[0]
     half = got.shape[0] // 2
-    copy = pltpu.make_async_copy(
-        rows.at[pl.ds(half, half)], send.at[pl.ds(0, half), pl.ds(feat, feat)], sems.at[0]
-    )
-    copy.start()
     stats = got[:, voc:].astype(F32).T[:8]
     send[half:, :LANES] = jnp.concatenate([stats[:, :half], stats[:, half:]], axis=0).astype(BF16)
     stat[...] = jnp.concatenate([join3(stats, 0), join3(stats, 3), stats[:6]], axis=0)
-    send[:half, :feat] = jnp.dot(
+    send[:half, :] = jnp.dot(
         got[half:, :voc], weight[...], preferred_element_type=F32
     ).astype(BF16)
-    copy.wait()
 
 
 def keep_kernel(got, weight, part):
@@ -169,12 +177,10 @@
     )
 
 
-def pair_kernel(scalars, part, stat, got, rows, out, own_rows, sems):
+def pair_kernel(scalars, part, stat, got, label_rows, out):
     half, feat = part.shape
     core, j, mine_n = scalars[2], scalars[3], OWN
     n_z = out.shape[0]
-    copy = pltpu.make_async_copy(rows.at[pl.ds(0, half)], own_rows, sems.at[0])
-    copy.start()
     theirs = got[half:, :LANES].astype(F32)
     own_log, own_target = stat[0:1, :], stat[1:2, :]
     other_log = jnp.concatenate([join3(theirs, 8), join3(theirs, 0)], axis=1)
@@ -187,7 +193,7 @@
         [jnp.exp(own_log - pair_log)[:, :half], jnp.exp(other_log - pair_log)[:, :half]], axis=0
     )
     shares = jnp.concatenate([shares] * (half // 2), axis=0).T
-    total = part[...] * shares[:, 0:1] + got[:half, :feat].astype(F32) * shares[:, 1:2]
+    total = part[...] * shares[:, 0:1] + got[:half, :].astype(F32) * shares[:, 1:2]
     logs = split3(pair_log)
     logs = [x[:, h * half : (h + 1) * half] for h in range(2) for x in logs]
     targets = jnp.concatenate(split3(own_target + other_target), axis=0)
@@ -200,8 +206,6 @@
             at = SPACE * k + (n + 1) * mine_n
             moved = pltpu.roll(x, (half + at - mine_n * j) % half, 1)[k : k + 1]
             base = jnp.where((lane >= at) & (lane < at + mine_n), moved, base)
-    copy.wait()
-    label_rows = own_rows[...].astype(F32) + got[:half, feat:].astype(F32)
     for i in range(n_z):
         row = base
         for k in range(3):
@@ -213,7 +217,7 @@
             here = slice(n * mine_n, (n + 1) * mine_n)
             out[i, here, :] = total[at, k : k + LANES].astype(BF16)
             here = slice(here.start + feat // LANES * mine_n, here.stop + feat // LANES * mine_n)
-            out[i, here, :] = label_rows[at, k : k + LANES].astype(BF16)
+            out[i, here, :] = label_rows[at, k : k + LANES]
         out[i, here.stop :, :] = jnp.concatenate(logs + [row, row], axis=0).astype(BF16)
 
 
@@ -336,17 +340,27 @@
         [((feat, voc), BF16), ((tokens, feat), BF16)],
         flops=flops,
     )
-    mine, tall, rows, scalars = lax.optimization_barrier((mine, tall, rows, scalars))
+    label_rows = rows[:half] + lax.ppermute(rows[half:], "section", swap)
+    ready = lax.optimization_barrier((mine, tall, label_rows, scalars))
+    mine, tall, label_rows, scalars = ready
     other = lax.ppermute(mine, "section", swap)
 
     width = voc + LANES
+    (coded,) = call(
+        mine_kernel,
+        [],
+        [mine, tall],
+        [((half, width), I16)],
+        scratch=[((half, voc), F32)],
+        flops=flops // 2,
+    )
     coded, whole = call(
-        logits_kernel,
+        other_kernel,
         [],
-        [mine, other, tall],
+        [coded, mine, other, tall],
         [((tokens, width), I16), ((tokens, feat), BF16)],
-        scratch=[((tokens, voc), F32)],
-        flops=flops,
+        scratch=[((half, voc), F32)],
+        flops=flops // 2,
     )
     coded = exchange_dp(coded.reshape(n_dp, share, width))
     (message,) = call(
@@ -362,9 +376,7 @@
         send_kernel,
         [],
         [got, head_weight],
-        [((half + 16, 2 * feat), BF16), ((8, tokens), F32)],
-        left=[rows],
-        copies=1,
+        [((half + 16, feat), BF16), ((8, tokens), F32)],
         flops=flops // 2,
     )
     theirs = lax.ppermute(send, "section", swap)
@@ -372,11 +384,8 @@
     (message,) = call(
         pair_kernel,
         [scalars],
-        [part, stat, theirs],
+        [part, stat, theirs, label_rows],
         [((n_z, (2 * feat // LANES + 1) * mine_n, LANES), BF16)],
-        left=[rows],
-        scratch=[((half, feat), BF16)],
-        copies=1,
     )
     last = exchange_z(message)
     soft = got[:, :voc].T

time: 115 us -> 115 us (level)
  waiting for transfers between devices: 31.7 us -> 28.8 us
  starting transfers between devices: 22.9 us -> 25.4 us
    all_to_all x2, waiting for transfers between devices: 29.2 us -> 26 us  [exchange_z(): lax.all_to_all(x, 'section', 0, 0, tiled=True, axis_index_groups=along_z)]
    ppermute x0 -> x1, starting transfers between devices: none -> 1.92 us  [local(): label_rows = rows[:half] + lax.ppermute(rows[half:], 'section', swap)]
    ppermute x0 -> x1, waiting for transfers between devices: none -> 1.21 us  [local(): label_rows = rows[:half] + lax.ppermute(rows[half:], 'section', swap)]
    pallas_call x7 -> x8, Pallas kernels: 8.73 us -> 8.76 us  [call(): pl.pallas_call(kernel, out_shape=[jax.ShapeDtypeStruct(s, d) for s, d in...]
  transfers between devices with their start and end apart: 4 -> 5, of which waited for: 4 -> 5; matrix products, arithmetic and copies ran while one was open for 2% -> 2% of each run, Pallas kernels for 1% -> 2%
where the time goes in v8:
time: 115 us; the launch traced here: 113 us
  blocking collectives  43.7 us (38%)
  waiting for transfers between devices  28.8 us (25%)
  starting transfers between devices  25.4 us (22%)
  Pallas kernels  8.76 us (8%)
  local copies, waits for them, and re-layouts  5.32 us (5%)
    all_to_all x2, blocking collectives, exchange_dp(): return lax.all_to_all(x, 'dp', 0, 0, tiled=True)  43.7 us
    all_to_all x2, waiting for transfers between devices, exchange_z(): lax.all_to_all(x, 'section', 0, 0, tiled=True, axis_index_groups=along_z)  26 us
    all_to_all x2, starting transfers between devices, exchange_z(): lax.all_to_all(x, 'section', 0, 0, tiled=True, axis_index_groups=along_z)  19.7 us
    pallas_call x8, Pallas kernels, call(): pl.pallas_call(kernel, out_shape=[jax.ShapeDtypeStruct(s, d) for s, d in...  8.76 us
  transfers between devices with their start and end apart: 5, of which 5 were waited for; matrix products, arithmetic and copies ran while one was open for 2% of the time, Pallas kernels for 2%

profile of v8, /device:TPU:6, one launch (start us, length us, event | category | flops | bytes accessed | tf_op | source)
XLA Modules:
  0.0 113.1 jit_solution(2382464193383250528)
XLA Ops:
  0.6 1.4 %broadcast_in_dim.6 = bf16[16,8,512]{2,1,0:T(8,128)(2,1)} broadcast(bf16[8,512]{1,0:T(8,128)(2,1)} %param.4), dimensions={1,2} | broadcast | bytes 139264 | tf_op jit(solution)/shard_map/broadcast_in_dim | solution.py:335
  2.0 15.2 %all-to-all-start = ((bf16[16,8,512]{2,1,0:T(8,128)(2,1)}), bf16[16,8,512]{2,1,0:T(8,128)(2,1)S(1)}, u32[]{:S(2)}, u32[]{:S(2)}) async-start(bf16[16,8,512]{2,1,0:T(8,128)(2,1)} %broadcast_in_dim.6), calls=%async_computation | async-start | bytes 262144 | tf_op jit(solution)/shard_map/all_to_all | solution.py:324
  17.2 0.8 reshape.102
  18.0 0.1 fusion
  18.0 0.1 concatenate.20
  18.1 0.1 concatenate.21
  18.2 0.1 copy.17
  18.4 0.0 copy-start
  18.4 1.6 %copy-done = bf16[2048,512]{1,0:T(8,128)(2,1)S(1)} copy-done((bf16[2048,512]{1,0:T(8,128)(2,1)S(1)}, bf16[2048,512]{1,0:T(8,128)(2,1)}, u32[]{:S(2)}) %copy-start) | copy-done | bytes 2097176
  20.0 1.1 shard_map.67
  21.1 1.9 %collective-permute-start = (bf16[128,512]{1,0:T(8,128)(2,1)S(1)}, bf16[128,512]{1,0:T(8,128)(2,1)S(1)}, u32[]{:S(2)}, u32[]{:S(2)}) collective-permute-start(bf16[128,512]{1,0:T(8,128)(2,1)S(1)} %slice.36), channel_id=1, source_target_pairs={{0,16},{16,0},{32,48},{48,32},{64,80},{80,64},{96,112},{112,96},{1... | collective-permute-start | bytes 393224 | tf_op jit(solution)/shard_map/ppermute | solution.py:343
  23.0 0.1 stack.19.scalars
  23.1 1.2 %collective-permute-done = bf16[128,512]{1,0:T(8,128)(2,1)S(1)} collective-permute-done((bf16[128,512]{1,0:T(8,128)(2,1)S(1)}, bf16[128,512]{1,0:T(8,128)(2,1)S(1)}, u32[]{:S(2)}, u32[]{:S(2)}) %collective-permute-start) | collective-permute-done | bytes 131104 | tf_op jit(solution)/shard_map/ppermute | solution.py:343
  24.3 7.6 %all-to-all-done = bf16[16,8,512]{2,1,0:T(8,128)(2,1)S(1)} async-done(((bf16[16,8,512]{2,1,0:T(8,128)(2,1)}), bf16[16,8,512]{2,1,0:T(8,128)(2,1)S(1)}, u32[]{:S(2)}, u32[]{:S(2)}) %all-to-all-start) | async-done | bytes 131104 | tf_op jit(solution)/shard_map/all_to_all | solution.py:324
  31.9 1.9 %collective-permute-start.1 = (bf16[128,512]{1,0:T(8,128)(2,1)S(1)}, bf16[128,512]{1,0:T(8,128)(2,1)S(1)}, u32[]{:S(2)}, u32[]{:S(2)}) collective-permute-start(bf16[128,512]{1,0:T(8,128)(2,1)S(1)} %bitcast.14), channel_id=1, source_target_pairs={{0,16},{16,0},{32,48},{48,32},{64,80},{80,64},{96,112},{112,96},{1... | collective-permute-start | bytes 393224 | tf_op jit(solution)/shard_map/ppermute | solution.py:346
  33.8 0.7 shard_map.68.coded
  34.5 0.7 collective-permute-done.1.other
  35.1 0.6 shard_map.69
  35.8 0.0 copy-start.2
  35.8 23.4 %all_to_all.20.got = s16[16,16,2176]{2,1,0:T(8,128)(2,1)S(1)} all-to-all(s16[16,16,2176]{2,1,0:T(8,128)(2,1)S(1)} %bitcast.17), channel_id=1, replica_groups=mesh['section'=32,'dp'=16] {'dp'}, dimensions={0} | all-to-all | bytes 2228224 | tf_op jit(solution)/shard_map/all_to_all | solution.py:327
  59.1 0.0 copy-done.2
  59.1 1.2 %shard_map.70 = bf16[16,16,2176]{2,1,0:T(8,128)(2,1)S(1)} custom-call(s32[6]{0:T(128)S(1)} %stack.19.scalars, s32[256]{0:T(256)S(1)} %copy-done.2, s16[16,16,2176]{2,1,0:T(8,128)(2,1)S(1)} %all_to_all.20.got), custom_call_target="tpu_custom_call" | custom-call | bytes 4194304 | tf_op jit(solution)/shard_map/pallas_call | solution.py:34
  60.3 0.0 copy-start.1
  60.3 20.4 %all_to_all.21 = bf16[16,16,2176]{2,1,0:T(8,128)(2,1)S(1)} all-to-all(bf16[16,16,2176]{2,1,0:T(8,128)(2,1)S(1)} %shard_map.70), channel_id=1, replica_groups=mesh['section'=32,'dp'=16] {'dp'}, dimensions={0} | all-to-all | bytes 2228224 | tf_op jit(solution)/shard_map/all_to_all | solution.py:327
  80.7 0.0 copy-done.1
  80.7 0.4 shard_map.72
  81.1 1.9 %collective-permute-start.2 = (bf16[144,512]{1,0:T(8,128)(2,1)S(1)}, bf16[144,512]{1,0:T(8,128)(2,1)S(1)}, u32[]{:S(2)}, u32[]{:S(2)}) collective-permute-start(bf16[144,512]{1,0:T(8,128)(2,1)S(1)} %get-tuple-element.25), channel_id=1, source_target_pairs={{0,16},{16,0},{32,48},{48,32},{64,80},{80,64},{96,112},{112,96},{1... | collective-permute-start | bytes 442376 | tf_op jit(solution)/shard_map/ppermute | solution.py:382
  83.1 0.4 shard_map.71.part
  83.5 0.9 collective-permute-done.2.got
  84.4 1.5 %shard_map.73 = bf16[16,72,128]{2,1,0:T(8,128)(2,1)} custom-call(s32[6]{0:T(128)S(1)} %stack.19.scalars, f32[128,512]{1,0:T(8,128)S(1)} %shard_map.71.part, f32[8,256]{1,0:T(8,128)S(1)} %get-tuple-element.24.stat, bf16[144,512]{1,0:T(8,128)(2,1)S(1)} %collective-permute-done.2.got, bf16[128,512]{1,0:T(8,128)(2,1)S(1)} %slice_add_fusion.label_rows), custom_call_target="tpu_custom_call" | custom-call | bytes 4194304 | tf_op jit(solution)/shard_map/pallas_call | solution.py:34
  85.9 4.5 %all-to-all-start.3 = ((bf16[16,72,128]{2,1,0:T(8,128)(2,1)}), bf16[16,72,128]{2,1,0:T(8,128)(2,1)S(1)}, u32[]{:S(2)}, u32[]{:S(2)}) async-start(bf16[16,72,128]{2,1,0:T(8,128)(2,1)} %shard_map.73), calls=%async_computation.3 | async-start | bytes 589824 | tf_op jit(solution)/shard_map/all_to_all | solution.py:324
  90.4 0.1 slice.44
  90.5 0.0 copy-start.3
  90.5 0.5 copy.20
  91.1 0.1 reshape.105
  91.2 0.1 fusion.2
  91.2 0.1 select_n.79
  91.3 0.1 select_n.81
  91.4 0.0 copy-done.3
  91.4 0.1 reshape.106
  91.5 0.1 fusion.4
  91.6 0.1 select_n.83
  91.7 0.1 select_n.85
  91.8 18.5 %all-to-all-done.3.got = bf16[16,72,128]{2,1,0:T(8,128)(2,1)S(1)} async-done(((bf16[16,72,128]{2,1,0:T(8,128)(2,1)}), bf16[16,72,128]{2,1,0:T(8,128)(2,1)S(1)}, u32[]{:S(2)}, u32[]{:S(2)}) %all-to-all-start.3) | async-done | bytes 294944 | tf_op jit(solution)/shard_map/all_to_all | solution.py:324
  110.3 2.9 %shard_map.74 = (f32[1,16]{1,0:T(1,128)}, bf16[8,512]{1,0:T(8,128)(2,1)}, bf16[2048,512]{1,0:T(8,128)(2,1)}) custom-call(s32[6]{0:T(128)S(1)} %stack.19.scalars, f32[256]{0:T(256)S(1)} %copy-done.3, bf16[16,72,128]{2,1,0:T(8,128)(2,1)S(1)} %all-to-all-done.3.got, bf16[2048,256]{1,0:T(8,128)(2,1)S(1)} %bitcast.18, f32[8,256]{1,0:T(8,128)S(1)} %get-tuple-element.24.stat, ...), custom_call_target="tpu_custom_call" | custom-call | flops 536870912 | bytes 4194304 | tf_op jit(solution)/shard_map/pallas_call | solution.py:34
  (6 shorter events, 0.1 us)
Async XLA Ops:
  2.0 29.9 %all-to-all-start = ((bf16[16,8,512]{2,1,0:T(8,128)(2,1)}), bf16[16,8,512]{2,1,0:T(8,128)(2,1)S(1)}, u32[]{:S(2)}, u32[]{:S(2)}) async-start(bf16[16,8,512]{2,1,0:T(8,128)(2,1)} %broadcast_in_dim.6), calls=%async_computation | async-start | bytes 262144 | tf_op jit(solution)/shard_map/all_to_all | solution.py:324
  18.4 1.6 %copy-start = (bf16[2048,512]{1,0:T(8,128)(2,1)S(1)}, bf16[2048,512]{1,0:T(8,128)(2,1)}, u32[]{:S(2)}) copy-start(bf16[2048,512]{1,0:T(8,128)(2,1)} %weight.5) | copy-start | bytes 6291460
  21.1 3.2 %collective-permute-start = (bf16[128,512]{1,0:T(8,128)(2,1)S(1)}, bf16[128,512]{1,0:T(8,128)(2,1)S(1)}, u32[]{:S(2)}, u32[]{:S(2)}) collective-permute-start(bf16[128,512]{1,0:T(8,128)(2,1)S(1)} %slice.36), channel_id=1, source_target_pairs={{0,16},{16,0},{32,48},{48,32},{64,80},{80,64},{96,112},{112,96},{1... | collective-permute-start | bytes 393224 | tf_op jit(solution)/shard_map/ppermute | solution.py:343
  31.9 3.2 %collective-permute-start.1 = (bf16[128,512]{1,0:T(8,128)(2,1)S(1)}, bf16[128,512]{1,0:T(8,128)(2,1)S(1)}, u32[]{:S(2)}, u32[]{:S(2)}) collective-permute-start(bf16[128,512]{1,0:T(8,128)(2,1)S(1)} %bitcast.14), channel_id=1, source_target_pairs={{0,16},{16,0},{32,48},{48,32},{64,80},{80,64},{96,112},{112,96},{1... | collective-permute-start | bytes 393224 | tf_op jit(solution)/shard_map/ppermute | solution.py:346
  35.8 23.4 %copy-start.2 = (s32[256]{0:T(256)S(1)}, s32[256]{0:T(256)}, u32[]{:S(2)}) copy-start(s32[256]{0:T(256)} %labels.1) | copy-start | bytes 3076
  60.3 20.4 %copy-start.1 = (bf16[2048,512]{1,0:T(8,128)(2,1)S(1)}, bf16[2048,512]{1,0:T(8,128)(2,1)}, u32[]{:S(2)}) copy-start(bf16[2048,512]{1,0:T(8,128)(2,1)} %weight.5) | copy-start | bytes 6291460
  81.1 3.3 %collective-permute-start.2 = (bf16[144,512]{1,0:T(8,128)(2,1)S(1)}, bf16[144,512]{1,0:T(8,128)(2,1)S(1)}, u32[]{:S(2)}, u32[]{:S(2)}) collective-permute-start(bf16[144,512]{1,0:T(8,128)(2,1)S(1)} %get-tuple-element.25), channel_id=1, source_target_pairs={{0,16},{16,0},{32,48},{48,32},{64,80},{80,64},{96,112},{112,96},{1... | collective-permute-start | bytes 442376 | tf_op jit(solution)/shard_map/ppermute | solution.py:382
  85.9 24.4 %all-to-all-start.3 = ((bf16[16,72,128]{2,1,0:T(8,128)(2,1)}), bf16[16,72,128]{2,1,0:T(8,128)(2,1)S(1)}, u32[]{:S(2)}, u32[]{:S(2)}) async-start(bf16[16,72,128]{2,1,0:T(8,128)(2,1)} %shard_map.73), calls=%async_computation.3 | async-start | bytes 589824 | tf_op jit(solution)/shard_map/all_to_all | solution.py:324
  90.5 0.9 copy-start.3
